TPU v7x, 128 devices: a whole 4x4x4 slice. The times are simulated.
128 devices in a mesh: fsdp: 16 (over x, z), context: 4 (over y), tensor: 2 (over core).
Axes of the slice: x: 4, y: 4, z: 4, core: 2. Of those that a mesh axis runs over, the one named last changes fastest.
Arguments:
- tokens: bfloat16 [32, 1024, 1024], P('fsdp', 'context'), may hold values from -6 to 6
- segments: int32 [32, 1024], P('fsdp'), may hold values from 0 to 6, as said below
- routes: int32 [32, 1024, 8], P('fsdp', 'context'), may hold values from 0 to 31, all different within a row
- attention_gain: bfloat16 [1024], P('fsdp'), may hold values from 0.5 to 1.5
- w_query: bfloat16 [1024, 1024], P('fsdp', 'tensor'), may hold values from -0.1875 to 0.1875
- w_key: bfloat16 [1024, 512], P('fsdp', 'tensor'), may hold values from -0.1875 to 0.1875
- w_value: bfloat16 [1024, 512], P('fsdp', 'tensor'), may hold values from -0.1875 to 0.1875
- w_out: bfloat16 [1024, 1024], P('fsdp', 'tensor'), may hold values from -0.75 to 0.75
- query_gain: bfloat16 [64], P('fsdp'), may hold values from 0.75 to 1.25
- key_gain: bfloat16 [64], P('fsdp'), may hold values from 0.75 to 1.25
- feedforward_gain: bfloat16 [1024], P('fsdp'), may hold values from 0.5 to 1.5
- router: bfloat16 [1024, 32], P('fsdp'), may hold values from -0.09375 to 0.09375
- w_gate: bfloat16 [32, 1024, 512], P('fsdp', None, 'tensor'), may hold values from -0.1875 to 0.1875
- w_up: bfloat16 [32, 1024, 512], P('fsdp', None, 'tensor'), may hold values from -0.1875 to 0.1875
- w_down: bfloat16 [32, 1024, 512], P('fsdp', None, 'tensor'), may hold values from -1 to 1
- cotangent: bfloat16 [32, 1024, 1024], P('fsdp', 'context'), may hold values from -6 to 6
Outputs:
- block_output: bfloat16 [32, 1024, 1024], P('fsdp', 'context')
- grad_tokens: float32 [32, 1024, 1024], P('fsdp', 'context')
- grad_attention_gain: float32 [1024], P('fsdp')
- grad_query: float32 [1024, 1024], P('fsdp', 'tensor')
- grad_key: float32 [1024, 512], P('fsdp', 'tensor')
- grad_value: float32 [1024, 512], P('fsdp', 'tensor')
- grad_out: float32 [1024, 1024], P('fsdp', 'tensor')
- grad_query_gain: float32 [64], P('fsdp')
- grad_key_gain: float32 [64], P('fsdp')
- grad_feedforward_gain: float32 [1024], P('fsdp')
- grad_router: float32 [1024, 32], P('fsdp')
- grad_gate: float32 [32, 1024, 512], P('fsdp', 'context', 'tensor')
- grad_up: float32 [32, 1024, 512], P('fsdp', 'context', 'tensor')
- grad_down: float32 [32, 1024, 512], P('fsdp', 'context', 'tensor')
Inputs may be any that keep to these rules, and one draw needn't show every extreme that they name: `segments`: within a sequence the numbers never fall and may skip; each sequence starts with 0 and ends with 6. Of the 2 sequences of one index of fsdp, one has a document that covers every position from 127 to 896.
All inputs are finite; a program needn't handle non-finite values.
Results may differ from a plain program's by a relative error of at most 0.02.
Values may be sent and summed in bfloat16 or wider, within the bound.
No kernel may reach another device: no remote copies, remote signals or barrier semaphores. Data moves between devices by JAX's collectives and lax.ppermute only.
A program may use at most 320 MiB of HBM per device.

v0:
```python
import jax
import jax.numpy as jnp
from jax import lax
from jax.sharding import PartitionSpec as P

HD = 64
EXPERTS = 32
TOPK = 8
SEQ = 1024
GROUP = 2


epsilon = 1e-06
negative = -1e30


def rotate_half(values):
    middle = values.shape[-1] // 2
    return jnp.concatenate([-values[..., middle:], values[..., :middle]], axis=-1)


def rotary_tables(offset, length):
    middle = HD // 2
    inverse = 10000.0 ** (-(2.0 * jnp.arange(middle, dtype=jnp.float32) / HD))
    places = offset.astype(jnp.float32) + jnp.arange(length, dtype=jnp.float32)
    angles = places[:, None] * inverse[None, :]
    angles = jnp.concatenate([angles, angles], axis=-1)
    return (jnp.cos(angles)[:, None, :], jnp.sin(angles)[:, None, :])


def inverse_rms(values):
    return lax.rsqrt(jnp.mean(values * values, axis=-1, keepdims=True) + epsilon)


def norm_back(grad_normed, values, factor, gain):
    weighted = grad_normed * gain
    return factor * weighted - values * factor * factor * factor * jnp.mean(
        weighted * values, axis=-1, keepdims=True
    )


def across_context(items):
    return lax.psum(
        (items[0], items[1], items[2], items[3], items[4], items[5], items[6], items[7], items[8]),
        "context",
    )


def across_fsdp(items):
    return (
        lax.psum_scatter(items[0], "fsdp", scatter_dimension=0, tiled=True),
        lax.psum_scatter(items[1], "fsdp", scatter_dimension=0, tiled=True),
        lax.psum_scatter(items[2], "fsdp", scatter_dimension=0, tiled=True),
        lax.psum_scatter(items[3], "fsdp", scatter_dimension=0, tiled=True),
        lax.psum_scatter(items[4], "fsdp", scatter_dimension=0, tiled=True),
        lax.psum_scatter(items[5], "fsdp", scatter_dimension=0, tiled=True),
        lax.psum_scatter(items[6], "fsdp", scatter_dimension=0, tiled=True),
        lax.psum_scatter(items[7], "fsdp", scatter_dimension=0, tiled=True),
        lax.psum_scatter(items[8], "fsdp", scatter_dimension=0, tiled=True),
    )


def over_hidden(partial_sum):
    return lax.psum(partial_sum, "tensor").astype(jnp.bfloat16)


def to_owners(slots):
    return lax.all_to_all(slots, "fsdp", split_axis=0, concat_axis=0, tiled=True)


def to_tokens(slots):
    return lax.all_to_all(slots, "fsdp", split_axis=0, concat_axis=0, tiled=True)


def local(
    tokens,
    segments,
    routes,
    attention_gain,
    w_query,
    w_key,
    w_value,
    w_out,
    query_gain,
    key_gain,
    feedforward_gain,
    router,
    w_gate,
    w_up,
    w_down,
    cotangent,
):
    (
        attention_whole,
        query_whole,
        key_whole,
        value_whole,
        out_whole,
        query_gain_whole,
        key_gain_whole,
        feedforward_whole,
        router_whole,
    ) = (
        lax.all_gather(attention_gain, "fsdp", axis=0, tiled=True),
        lax.all_gather(w_query, "fsdp", axis=0, tiled=True),
        lax.all_gather(w_key, "fsdp", axis=0, tiled=True),
        lax.all_gather(w_value, "fsdp", axis=0, tiled=True),
        lax.all_gather(w_out, "fsdp", axis=0, tiled=True),
        lax.all_gather(query_gain, "fsdp", axis=0, tiled=True),
        lax.all_gather(key_gain, "fsdp", axis=0, tiled=True),
        lax.all_gather(feedforward_gain, "fsdp", axis=0, tiled=True),
        lax.all_gather(router, "fsdp", axis=0, tiled=True),
    )
    seqs_here, local_rows, model_width = tokens.shape
    row_count = seqs_here * local_rows
    first_row = lax.axis_index("context") * local_rows
    cosine, sine = rotary_tables(first_row, local_rows)
    query_segments = lax.dynamic_slice_in_dim(segments, first_row, local_rows, 1)
    same_doc = query_segments[:, :, None] == segments[:, None, :]
    inverse_root = HD ** (-0.5)
    residual = tokens.astype(jnp.float32)
    factor1 = inverse_rms(residual)
    gain1 = attention_whole.astype(jnp.float32)
    normed1 = (residual * factor1 * gain1).astype(jnp.bfloat16)
    heads_here = query_whole.shape[1] // HD
    kv_here = key_whole.shape[1] // HD
    query_proj = jnp.dot(normed1, query_whole, preferred_element_type=jnp.float32).reshape(
        seqs_here, local_rows, heads_here, HD
    )
    key_proj = jnp.dot(normed1, key_whole, preferred_element_type=jnp.float32).reshape(
        seqs_here, local_rows, kv_here, HD
    )
    value_b = jnp.dot(normed1, value_whole, preferred_element_type=jnp.float32).astype(jnp.bfloat16)
    query_factor = inverse_rms(query_proj)
    key_factor = inverse_rms(key_proj)
    query_gain_f = query_gain_whole.astype(jnp.float32)
    key_gain_f = key_gain_whole.astype(jnp.float32)
    query_rot = query_proj * query_factor * query_gain_f
    query_rot = query_rot * cosine + rotate_half(query_rot) * sine
    key_rot = key_proj * key_factor * key_gain_f
    key_rot = key_rot * cosine + rotate_half(key_rot) * sine
    query_b = query_rot.astype(jnp.bfloat16).reshape(seqs_here, local_rows, kv_here, GROUP, HD)
    key_b = key_rot.astype(jnp.bfloat16).reshape(seqs_here, local_rows, kv_here * HD)
    keys_whole, values_whole = (
        lax.all_gather(key_b, "context", axis=1, tiled=True),
        lax.all_gather(value_b, "context", axis=1, tiled=True),
    )
    keys_whole = keys_whole.reshape(seqs_here, SEQ, kv_here, HD)
    values_whole = values_whole.reshape(seqs_here, SEQ, kv_here, HD)

    def score_block():
        raw = jnp.einsum(
            "bqgjd,bkgd->bgjqk", query_b, keys_whole, preferred_element_type=jnp.float32
        )
        return jnp.where(same_doc[:, None, None], raw * inverse_root, negative)

    scores = score_block()
    row_max = jnp.max(scores, axis=-1, keepdims=True)
    row_total = jnp.sum(jnp.exp(scores - row_max), axis=-1, keepdims=True)
    log_total = row_max + jnp.log(row_total)
    probs_b = jnp.exp(scores - log_total).astype(jnp.bfloat16)
    attended = jnp.einsum(
        "bgjqk,bkgd->bqgjd", probs_b, values_whole, preferred_element_type=jnp.float32
    )
    attended = attended.reshape(row_count, heads_here * HD).astype(jnp.bfloat16)
    branch_part = jnp.einsum("rh,dh->rd", attended, out_whole, preferred_element_type=jnp.float32)
    branch = lax.psum(branch_part, "tensor")
    hidden1 = residual.reshape(row_count, model_width) + branch
    factor2 = inverse_rms(hidden1)
    gain2 = feedforward_whole.astype(jnp.float32)
    normed2 = (hidden1 * factor2 * gain2).astype(jnp.bfloat16)
    logits = jnp.dot(normed2, router_whole, preferred_element_type=jnp.float32)
    router_probs = jax.nn.softmax(logits, axis=-1)
    picked = routes.reshape(row_count, TOPK)
    route_match = picked[:, :, None] == jnp.arange(EXPERTS, dtype=jnp.int32)[None, None, :]
    chosen = jnp.sum(jnp.where(route_match, router_probs[:, None, :], 0.0), axis=-1)
    chosen_total = jnp.sum(chosen, axis=-1, keepdims=True)
    gates = chosen / chosen_total
    flat_pick = picked.reshape(-1)
    counts = (flat_pick[:, None] == jnp.arange(EXPERTS, dtype=jnp.int32)[None, :]).astype(jnp.int32)
    place_in = jnp.sum(jnp.cumsum(counts, axis=0) * counts, axis=-1) - 1
    capacity = (5 * row_count * TOPK + 4 * EXPERTS - 1) // (4 * EXPERTS)
    slot_index = jnp.where(place_in < capacity, flat_pick * capacity + place_in, EXPERTS * capacity)
    is_kept = (place_in < capacity).reshape(row_count, TOPK)
    pair_token = jnp.arange(row_count * TOPK, dtype=jnp.int32) // TOPK
    slot_token = (
        jnp.full((EXPERTS * capacity,), row_count, jnp.int32)
        .at[slot_index]
        .set(pair_token, mode="drop")
    )
    padded = jnp.concatenate([normed2, jnp.zeros((1, model_width), jnp.bfloat16)], axis=0)
    fsdp_count = lax.axis_size("fsdp")
    owned_experts = EXPERTS // fsdp_count
    outgoing = padded[slot_token].reshape(fsdp_count, owned_experts, capacity, model_width)
    arrived = to_owners(outgoing)
    gate_pre = jnp.einsum("sxcd,xdf->sxcf", arrived, w_gate, preferred_element_type=jnp.float32)
    up_pre = jnp.einsum("sxcd,xdf->sxcf", arrived, w_up, preferred_element_type=jnp.float32)
    sigmoid_gate = jax.nn.sigmoid(gate_pre)
    swish = gate_pre * sigmoid_gate
    activation = (swish * up_pre).astype(jnp.bfloat16)
    produced_part = jnp.einsum(
        "sxcf,xdf->sxcd", activation, w_down, preferred_element_type=jnp.float32
    )
    produced = over_hidden(produced_part)
    returned = to_tokens(produced)
    share_width = returned.shape[-1]
    returned = returned.reshape(EXPERTS * capacity, share_width)
    returned = jnp.concatenate([returned, jnp.zeros((1, share_width), jnp.bfloat16)], axis=0)
    pair_slot = slot_index.reshape(row_count, TOPK)
    pair_values = returned[pair_slot].astype(jnp.float32)
    pair_weight = jnp.where(is_kept, gates, 0.0)
    mixed_part = jnp.sum(pair_weight[:, :, None] * pair_values, axis=1)
    upstream = cotangent.astype(jnp.float32).reshape(row_count, model_width)
    weight_part = jnp.sum(upstream[:, None, :] * pair_values, axis=-1)
    block_output = (
        (hidden1 + mixed_part).astype(jnp.bfloat16).reshape(seqs_here, local_rows, model_width)
    )
    pair_grads = (pair_weight[:, :, None] * upstream[:, None, :]).reshape(
        row_count * TOPK, model_width
    )
    slot_grads = (
        jnp.zeros((EXPERTS * capacity, model_width), jnp.float32)
        .at[slot_index]
        .set(pair_grads, mode="drop")
    )
    slot_grads = slot_grads.astype(jnp.bfloat16).reshape(
        fsdp_count, owned_experts, capacity, model_width
    )
    grads_arrived = to_owners(slot_grads)
    grad_down_w = jnp.einsum(
        "sxcf,sxcd->xdf", activation, grads_arrived, preferred_element_type=jnp.float32
    )
    grad_act = jnp.einsum(
        "sxcd,xdf->sxcf", grads_arrived, w_down, preferred_element_type=jnp.float32
    )
    grad_gate_b = (
        grad_act * up_pre * sigmoid_gate * (1.0 + gate_pre * (1.0 - sigmoid_gate))
    ).astype(jnp.bfloat16)
    grad_up_b = (grad_act * swish).astype(jnp.bfloat16)
    grad_gate_w = jnp.einsum(
        "sxcd,sxcf->xdf", arrived, grad_gate_b, preferred_element_type=jnp.float32
    )
    grad_up_w = jnp.einsum("sxcd,sxcf->xdf", arrived, grad_up_b, preferred_element_type=jnp.float32)
    back_part = jnp.einsum(
        "sxcf,xdf->sxcd", grad_gate_b, w_gate, preferred_element_type=jnp.float32
    )
    back_part = back_part + jnp.einsum(
        "sxcf,xdf->sxcd", grad_up_b, w_up, preferred_element_type=jnp.float32
    )
    back_slots = over_hidden(back_part)
    back = to_tokens(back_slots)
    back = back.reshape(EXPERTS * capacity, back.shape[-1])
    back = jnp.concatenate([back, jnp.zeros((1, back.shape[-1]), jnp.bfloat16)], axis=0)
    grad_rows = jnp.sum(back[pair_slot].astype(jnp.float32), axis=1)
    grad_normed2 = grad_rows
    grad_gates = jnp.where(is_kept, weight_part, 0.0)
    grad_chosen = grad_gates / chosen_total - jnp.sum(
        grad_gates * chosen, axis=-1, keepdims=True
    ) / (chosen_total * chosen_total)
    grad_router_probs = jnp.sum(jnp.where(route_match, grad_chosen[:, :, None], 0.0), axis=1)
    grad_logits = router_probs * (
        grad_router_probs - jnp.sum(router_probs * grad_router_probs, axis=-1, keepdims=True)
    )
    grad_router_w = jnp.einsum(
        "rd,re->de", normed2.astype(jnp.float32), grad_logits, precision=lax.Precision.HIGHEST
    )
    grad_normed2 = grad_normed2 + jnp.einsum(
        "re,de->rd", grad_logits, router_whole.astype(jnp.float32), precision=lax.Precision.HIGHEST
    )
    grad_gain2 = jnp.sum(grad_normed2 * hidden1 * factor2, axis=0)
    grad_hidden1 = upstream + norm_back(grad_normed2, hidden1, factor2, gain2)
    grad_branch = grad_hidden1.astype(jnp.bfloat16)
    grad_out_w = jnp.einsum("rd,rh->dh", grad_branch, attended, preferred_element_type=jnp.float32)
    grad_attended = jnp.dot(grad_branch, out_whole, preferred_element_type=jnp.float32).astype(
        jnp.bfloat16
    )
    grad_attended = grad_attended.reshape(seqs_here, local_rows, kv_here, GROUP, HD)
    scores = score_block()
    probs = jnp.exp(scores - log_total)
    probs_b = probs.astype(jnp.bfloat16)
    grad_probs = jnp.einsum(
        "bqgjd,bkgd->bgjqk", grad_attended, values_whole, preferred_element_type=jnp.float32
    )
    row_dot = jnp.sum(probs * grad_probs, axis=-1, keepdims=True)
    grad_scores = (probs * (grad_probs - row_dot)).astype(jnp.bfloat16)
    grad_query_rot = (
        jnp.einsum("bgjqk,bkgd->bqgjd", grad_scores, keys_whole, preferred_element_type=jnp.float32)
        * inverse_root
    )
    grad_keys_part = (
        jnp.einsum("bgjqk,bqgjd->bkgd", grad_scores, query_b, preferred_element_type=jnp.float32)
        * inverse_root
    )
    grad_values_part = jnp.einsum(
        "bgjqk,bqgjd->bkgd", probs_b, grad_attended, preferred_element_type=jnp.float32
    )
    grad_keys, grad_values = (
        lax.psum_scatter(
            grad_keys_part.reshape(seqs_here, SEQ, kv_here * HD),
            "context",
            scatter_dimension=1,
            tiled=True,
        ),
        lax.psum_scatter(
            grad_values_part.reshape(seqs_here, SEQ, kv_here * HD),
            "context",
            scatter_dimension=1,
            tiled=True,
        ),
    )
    grad_query_rot = grad_query_rot.reshape(seqs_here, local_rows, heads_here, HD)
    grad_query_unit = grad_query_rot * cosine - rotate_half(grad_query_rot) * sine
    grad_query_gain_part = jnp.sum(grad_query_unit * query_proj * query_factor, axis=(0, 1, 2))
    grad_query_pre = norm_back(grad_query_unit, query_proj, query_factor, query_gain_f)
    grad_query_pre = grad_query_pre.astype(jnp.bfloat16).reshape(row_count, heads_here * HD)
    grad_key_rot = grad_keys.reshape(seqs_here, local_rows, kv_here, HD)
    grad_key_unit = grad_key_rot * cosine - rotate_half(grad_key_rot) * sine
    grad_key_gain_part = jnp.sum(grad_key_unit * key_proj * key_factor, axis=(0, 1, 2))
    grad_key_pre = norm_back(grad_key_unit, key_proj, key_factor, key_gain_f)
    grad_key_pre = grad_key_pre.astype(jnp.bfloat16).reshape(row_count, kv_here * HD)
    grad_value_pre = grad_values.astype(jnp.bfloat16).reshape(row_count, kv_here * HD)
    normed1_flat = normed1.reshape(row_count, model_width)
    grad_query_w = jnp.einsum(
        "rd,rh->dh", normed1_flat, grad_query_pre, preferred_element_type=jnp.float32
    )
    grad_key_w = jnp.einsum(
        "rd,rh->dh", normed1_flat, grad_key_pre, preferred_element_type=jnp.float32
    )
    grad_value_w = jnp.einsum(
        "rd,rh->dh", normed1_flat, grad_value_pre, preferred_element_type=jnp.float32
    )
    input_part = jnp.einsum(
        "rh,dh->rd", grad_query_pre, query_whole, preferred_element_type=jnp.float32
    )
    input_part = input_part + jnp.einsum(
        "rh,dh->rd", grad_key_pre, key_whole, preferred_element_type=jnp.float32
    )
    input_part = input_part + jnp.einsum(
        "rh,dh->rd", grad_value_pre, value_whole, preferred_element_type=jnp.float32
    )
    grad_normed1, grad_query_gain_all, grad_key_gain_all = lax.psum(
        (input_part, grad_query_gain_part, grad_key_gain_part), "tensor"
    )
    residual_flat = residual.reshape(row_count, model_width)
    factor1_flat = factor1.reshape(row_count, 1)
    grad_gain1 = jnp.sum(grad_normed1 * residual_flat * factor1_flat, axis=0)
    grad_tokens = grad_hidden1 + norm_back(grad_normed1, residual_flat, factor1_flat, gain1)
    gathered_grads = (
        grad_gain1,
        grad_query_w,
        grad_key_w,
        grad_value_w,
        grad_out_w,
        grad_query_gain_all,
        grad_key_gain_all,
        grad_gain2,
        grad_router_w,
    )
    reduced = across_fsdp(across_context(gathered_grads))
    grad_gate_out, grad_up_out, grad_down_out = (
        lax.psum_scatter(grad_gate_w, "context", scatter_dimension=1, tiled=True),
        lax.psum_scatter(grad_up_w, "context", scatter_dimension=1, tiled=True),
        lax.psum_scatter(grad_down_w, "context", scatter_dimension=1, tiled=True),
    )
    return (
        block_output,
        grad_tokens.reshape(seqs_here, local_rows, model_width),
        reduced[0],
        reduced[1],
        reduced[2],
        reduced[3],
        reduced[4],
        reduced[5],
        reduced[6],
        reduced[7],
        reduced[8],
        grad_gate_out,
        grad_up_out,
        grad_down_out,
    )


def solution(mesh):
    in_specs = (
        P("fsdp", "context", None),
        P("fsdp", None),
        P("fsdp", "context", None),
        P("fsdp"),
        P("fsdp", "tensor"),
        P("fsdp", "tensor"),
        P("fsdp", "tensor"),
        P("fsdp", "tensor"),
        P("fsdp"),
        P("fsdp"),
        P("fsdp"),
        P("fsdp", None),
        P("fsdp", None, "tensor"),
        P("fsdp", None, "tensor"),
        P("fsdp", None, "tensor"),
        P("fsdp", "context", None),
    )
    out_specs = (
        P("fsdp", "context", None),
        P("fsdp", "context", None),
        P("fsdp"),
        P("fsdp", "tensor"),
        P("fsdp", "tensor"),
        P("fsdp", "tensor"),
        P("fsdp", "tensor"),
        P("fsdp"),
        P("fsdp"),
        P("fsdp"),
        P("fsdp", None),
        P("fsdp", "context", "tensor"),
        P("fsdp", "context", "tensor"),
        P("fsdp", "context", "tensor"),
    )
    return jax.shard_map(local, mesh=mesh, in_specs=in_specs, out_specs=out_specs, check_vma=False)
```

profile of v0, /device:TPU:1, one launch (start us, length us, event | category | flops | bytes accessed | tf_op | source)
XLA Modules:
  0.0 1931.6 jit_solution(4803194563335415289)
XLA Ops:
  14.8 36.4 %all-reduce.16 = (bf16[1024]{0:T(1024)(128)(2,1)S(1)}, bf16[64]{0:T(256)(128)(2,1)S(1)}, bf16[64]{0:T(256)(128)(2,1)}, bf16[1024]{0:T(1024)(128)(2,1)}) all-reduce(bf16[1024]{0:T(1024)(128)(2,1)S(1)} %dynamic-update-slice, bf16[64]{0:T(256)(128)(2,1)S(1)} %dynamic-update-slice.1, ...), channel_id=1, replica_groups=mesh['fsdp'=16,'context'=4,'tensor'=2] {'fsdp'}, use_global_device_ids=true, to_apply=%add.3 | all-reduce | flops 2176 | bytes 8704
  51.8 16.4 all_gather.34
  71.2 18.6 all_gather.36
  114.0 28.2 %all-gather.8.cloned.1.call-done = bf16[2,1024,256]{2,1,0:T(8,128)(2,1)} async-done(((bf16[2,256,256]{2,1,0:T(8,128)(2,1)}), bf16[2,1024,256]{2,1,0:T(8,128)(2,1)}) %all-gather.8.cloned.1.call-update) | async-done | bytes 1048592 | tf_op jit(solution)/shard_map/all_gather | solution.py:145
  144.4 42.5 %all-gather.10.cloned.1.call-done = bf16[1024,512]{1,0:T(8,128)(2,1)} async-done(((bf16[64,512]{1,0:T(8,128)(2,1)}), bf16[1024,512]{1,0:T(8,128)(2,1)}) %all-gather.10.cloned.1.call-update) | async-done | bytes 1048592 | tf_op jit(solution)/shard_map/all_gather | solution.py:105
  218.1 12.9 all-gather.12.cloned.1.call-done
  234.7 16.5 reduce-window.6
  252.8 15.5 scatter_custom_fusion
  273.0 22.5 %gather_fusion = bf16[5120,1024]{1,0:T(8,128)(2,1)} fusion(bf16[513,1024]{1,0:T(8,128)(2,1)S(1)} %concatenate.49, s32[5120]{0:T(1024)S(1)} %fusion.90), kind=kCustom, calls=%fused_computation | custom fusion | bytes 20992000 | tf_op jit(solution)/shard_map/gather | solution.py:194
  300.7 188.5 %all-gather = bf16[16,64,32]{1,2,0:T(8,128)(2,1)S(1)} all-gather(bf16[1,64,32]{1,2,0:T(8,128)(2,1)S(1)} %bitcast.415), channel_id=1, replica_groups=mesh['fsdp'=16,'context'=4,'tensor'=2] {'fsdp'}, dimensions={0}, use_global_device_ids=true | all-gather | bytes 69632 | tf_op jit(solution)/shard_map/all_gather | solution.py:112
  497.3 28.5 %scatter_custom_fusion.1 = f32[5120,1024]{1,0:T(8,128)} fusion(s32[4096]{0:T(1024)} %bitcast.414, f32[]{:T(128)} %constant.26.clone.1, f32[512,1024]{1,0:T(8,128)S(1)} %convert.1, f32[4096]{0:T(1024)S(1)} %broadcast_select_fusion), kind=kCustom, calls=%fused_computation.17 | custom fusion | flops 4194304 | bytes 23085568 | tf_op jit(solution)/shard_map/scatter | solution.py:224
  525.7 12.3 convert_element_type.145
  561.9 104.5 %all-to-all-done.2 = bf16[16,2,160,1024]{3,2,1,0:T(8,128)(2,1)} async-done(((bf16[16,2,160,1024]{3,2,1,0:T(8,128)(2,1)}), bf16[16,2,160,1024]{3,2,1,0:T(8,128)(2,1)}, u32[]{:S(2)}, u32[]{:S(2)}) %all-to-all-start.2) | async-done | bytes 10485792 | tf_op jit(solution)/shard_map/all_to_all | solution.py:68
  666.4 11.1 fusion.20
  686.1 14.3 add_bitcast_fusion
  711.2 118.6 %all-reduce.27 = (bf16[16,2,160,1024]{3,2,0,1:T(8,128)(2,1)}, bf16[16,2,160,1024]{3,2,0,1:T(8,128)(2,1)}) all-reduce(f32[16,2,160,1024]{3,2,0,1:T(8,128)} %convolution_bitcast_fusion, f32[16,2,160,1024]{3,2,0,1:T(8,128)} %add_bitcast_fusion), channel_id=1, replica_groups=mesh['fsdp'=16,'context'=4,'tensor'=2] {'tensor'}, use_global_device_ids=true, to_apply=%region_15.16 | all-reduce | flops 10485760 | bytes 62914560 | tf_op jit(solution)/shard_map/psum | solution.py:64
  857.0 170.0 %all-to-all-done.1 = bf16[16,2,160,1024]{3,2,1,0:T(8,128)(2,1)} async-done(((bf16[16,2,160,1024]{3,2,1,0:T(8,128)(2,1)}), bf16[16,2,160,1024]{3,2,1,0:T(8,128)(2,1)}, u32[]{:S(2)}, u32[]{:S(2)}) %all-to-all-start.1) | async-done | bytes 10485792 | tf_op jit(solution)/shard_map/all_to_all | solution.py:72
  1047.2 26.2 %gather_fusion.1 = bf16[4096,1024]{1,0:T(8,128)(2,1)} fusion(bf16[5121,1024]{1,0:T(8,128)(2,1)} %concatenate.50, s32[4096]{0:T(1024)S(1)} %broadcast_clamp_fusion), kind=kCustom, calls=%fused_computation.1 | custom fusion | bytes 16793600 | tf_op jit(solution)/shard_map/gather | solution.py:210
  1083.7 131.8 %all-to-all-done.3 = bf16[16,2,160,1024]{3,2,1,0:T(8,128)(2,1)} async-done(((bf16[16,2,160,1024]{3,2,1,0:T(8,128)(2,1)}), bf16[16,2,160,1024]{3,2,1,0:T(8,128)(2,1)}, u32[]{:S(2)}, u32[]{:S(2)}) %all-to-all-start.3) | async-done | bytes 10485792 | tf_op jit(solution)/shard_map/all_to_all | solution.py:72
  1225.6 26.3 %gather_fusion.2 = bf16[4096,1024]{1,0:T(8,128)(2,1)} fusion(bf16[5121,1024]{1,0:T(8,128)(2,1)} %concatenate.51, s32[4096]{0:T(1024)S(1)} %broadcast_clamp_fusion), kind=kCustom, calls=%fused_computation.2 | custom fusion | bytes 16793600 | tf_op jit(solution)/shard_map/gather | solution.py:254
  1252.0 12.0 convert_reduce_fusion
  1343.2 22.2 %reduce-scatter.15.cloned.1.call-done = f32[2,256,256]{2,1,0:T(8,128)} async-done(((f32[2,1024,256]{2,1,0:T(8,128)}), f32[2,256,256]{2,1,0:T(8,128)}) %reduce-scatter.15.cloned.1.call-update) | async-done | bytes 524304 | tf_op jit(solution)/shard_map/reduce_scatter | solution.py:304
  1435.6 34.7 %all-reduce.11 = (f32[1024]{0:T(1024)S(1)}, f32[64]{0:T(128)S(1)}, f32[64]{0:T(128)S(1)}, f32[1024]{0:T(1024)S(1)}) all-reduce(f32[1024]{0:T(1024)S(1)} %get-tuple-element.18, f32[64]{0:T(128)S(1)} %reduce_sum.253, f32[64]{0:T(128)S(1)} %reduce_sum.256, ...), channel_id=4, replica_groups=mesh['fsdp'=16,'context'=4,'tensor'=2] {'fsdp'}, use_global_device_ids=true, to_apply=%region_34.35.clone | all-reduce | flops 2176 | bytes 17408
  1481.0 12.0 all-reduce.12
  1493.1 56.8 %reduce-scatter.29.cloned.1.call-done = f32[64,512]{1,0:T(8,128)} async-done(((f32[1024,512]{1,0:T(8,128)}), f32[64,512]{1,0:T(8,128)}) %reduce-scatter.29.cloned.1.call-update) | async-done | bytes 131088 | tf_op jit(solution)/shard_map/reduce_scatter | solution.py:55
  1549.9 77.0 %reduce-scatter.23.cloned.1.call-done = f32[64,512]{1,0:T(8,128)} async-done(((f32[1024,512]{1,0:T(8,128)}), f32[64,512]{1,0:T(8,128)}) %reduce-scatter.23.cloned.1.call-update) | async-done | bytes 131088 | tf_op jit(solution)/shard_map/reduce_scatter | solution.py:52
  1626.9 75.7 %reduce-scatter.27.cloned.1.call-done = f32[64,256]{1,0:T(8,128)} async-done(((f32[1024,256]{1,0:T(8,128)}), f32[64,256]{1,0:T(8,128)}) %reduce-scatter.27.cloned.1.call-update) | async-done | bytes 65552 | tf_op jit(solution)/shard_map/reduce_scatter | solution.py:54
  1702.6 75.5 %reduce-scatter.25.cloned.1.call-done = f32[64,256]{1,0:T(8,128)} async-done(((f32[1024,256]{1,0:T(8,128)}), f32[64,256]{1,0:T(8,128)}) %reduce-scatter.25.cloned.1.call-update) | async-done | bytes 65552 | tf_op jit(solution)/shard_map/reduce_scatter | solution.py:53
  1782.0 29.6 %reduce-scatter.21.cloned.1.call-done = f32[2,256,256]{2,1,0:T(8,128)} async-done(((f32[2,1024,256]{2,1,0:T(8,128)}), f32[2,256,256]{2,1,0:T(8,128)}) %reduce-scatter.21.cloned.1.call-update) | async-done | bytes 524304 | tf_op jit(solution)/shard_map/reduce_scatter | solution.py:363
  1811.7 32.3 %reduce-scatter.17.cloned.1.call-done = f32[2,256,256]{2,1,0:T(8,128)} async-done(((f32[2,1024,256]{2,1,0:T(8,128)}), f32[2,256,256]{2,1,0:T(8,128)}) %reduce-scatter.17.cloned.1.call-update) | async-done | bytes 524304 | tf_op jit(solution)/shard_map/reduce_scatter | solution.py:361
  1843.9 32.4 %reduce-scatter.19.cloned.1.call-done = f32[2,256,256]{2,1,0:T(8,128)} async-done(((f32[2,1024,256]{2,1,0:T(8,128)}), f32[2,256,256]{2,1,0:T(8,128)}) %reduce-scatter.19.cloned.1.call-update) | async-done | bytes 524304 | tf_op jit(solution)/shard_map/reduce_scatter | solution.py:362
  1876.3 42.5 %all-reduce.26.cloned.1.call-done = (f32[64,512]{1,0:T(8,128)}, f32[64,256]{1,0:T(8,128)}, f32[64,256]{1,0:T(8,128)}, f32[64,512]{1,0:T(8,128)}) async-done(((f32[64,512]{1,0:T(8,128)}, f32[64,256]{1,0:T(8,128)}, f32[64,256]{1,0:T(8,128)}, f32[64,512]{1,0:T(8,128)}), (f32[64,512]{1,0:T(8,128)}, f32[64,256]{1,0:T(8,128)}, f32[64,256]{1,0:T(8,128)}, f32[64,512]{1,0:T(8,128)})) %all-reduce.26.cloned.1.call-update) | async-done | bytes 393232 | tf_op jit(solution)/shard_map/psum | solution.py:43
  (449 shorter events, 368.5 us)
Async XLA Ops:
  7.2 659.3 %copy-start = (bf16[2,1024,256]{2,1,0:T(8,128)(2,1)S(1)}, bf16[2,1024,256]{2,1,0:T(8,128)(2,1)}, u32[]{:S(2)}) copy-start(bf16[2,1024,256]{2,1,0:T(8,128)(2,1)} %param.30) | copy-start | bytes 3145732
  7.2 104.4 %all-gather.6.cloned.1.call-start = ((), (), s32[]{:S(2)}) async-start(), calls=%async_computation.14 | async-start | bytes 1310720 | tf_op jit(solution)/shard_map/all_gather | solution.py:146
  70.0 117.0 %copy-start.10 = (bf16[2,256,1024]{2,1,0:T(8,128)(2,1)}, bf16[2,256,1024]{2,1,0:T(8,128)(2,1)S(1)}, u32[]{:S(2)}) copy-start(bf16[2,256,1024]{2,1,0:T(8,128)(2,1)S(1)} %fusion.34) | copy-start | bytes 3145732
  71.1 71.0 %all-gather.8.cloned.1.call-start = ((), (), s32[]{:S(2)}) async-start(), calls=%async_computation.15 | async-start | bytes 1310720 | tf_op jit(solution)/shard_map/all_gather | solution.py:145
  90.1 102.3 %copy-start.29 = (f32[256,64]{0,1:T(8,128)}, f32[256,64]{0,1:T(8,128)S(1)}, u32[]{:S(2)}) copy-start(f32[256,64]{0,1:T(8,128)S(1)} %get-tuple-element.66) | copy-start | bytes 196612
  90.1 102.3 %copy-start.46 = (f32[256,64]{0,1:T(8,128)}, f32[256,64]{0,1:T(8,128)S(1)}, u32[]{:S(2)}) copy-start(f32[256,64]{0,1:T(8,128)S(1)} %get-tuple-element.67) | copy-start | bytes 196612
  103.2 83.7 %all-gather.10.cloned.1.call-start = ((), (), s32[]{:S(2)}) async-start(), calls=%async_computation.16 | async-start | bytes 1114112 | tf_op jit(solution)/shard_map/all_gather | solution.py:105
  104.0 127.1 %all-gather.12.cloned.1.call-start = ((), (), s32[]{:S(2)}) async-start(), calls=%async_computation.17 | async-start | bytes 1114112 | tf_op jit(solution)/shard_map/all_gather | solution.py:108
  104.5 163.9 %all-reduce.22.cloned.1.call-start = ((), (), s32[]{:S(2)}) async-start(), calls=%async_computation.18 | async-start | bytes 4194304 | tf_op jit(solution)/shard_map/psum | solution.py:167
  108.1 162.3 %copy-start.81 = (f32[1024]{0:T(1024)}, f32[1024]{0:T(1024)S(1)}, u32[]{:S(2)}) copy-start(f32[1024]{0:T(1024)S(1)} %convert_element_type.139) | copy-start | bytes 12292
  111.5 98.1 %copy-start.14 = (pred[2,256,1024]{1,2,0:T(8,128)(4,1)}, pred[2,256,1024]{1,2,0:T(8,128)(4,1)S(1)}, u32[]{:S(2)}) copy-start(pred[2,256,1024]{1,2,0:T(8,128)(4,1)S(1)} %broadcast_compare_fusion) | copy-start | bytes 1572868
  295.6 242.5 %all-to-all-start = ((bf16[16,2,160,1024]{3,2,1,0:T(8,128)(2,1)}), bf16[16,2,160,1024]{3,2,1,0:T(8,128)(2,1)}, u32[]{:S(2)}, u32[]{:S(2)}) async-start(bf16[16,2,160,1024]{3,2,1,0:T(8,128)(2,1)} %bitcast.339), calls=%async_computation | async-start | bytes 20971520 | tf_op jit(solution)/shard_map/all_to_all | solution.py:68
  538.1 128.4 %all-to-all-start.2 = ((bf16[16,2,160,1024]{3,2,1,0:T(8,128)(2,1)}), bf16[16,2,160,1024]{3,2,1,0:T(8,128)(2,1)}, u32[]{:S(2)}, u32[]{:S(2)}) async-start(bf16[16,2,160,1024]{3,2,1,0:T(8,128)(2,1)} %bitcast.340), calls=%async_computation.2 | async-start | bytes 20971520 | tf_op jit(solution)/shard_map/all_to_all | solution.py:68
  839.8 187.1 %all-to-all-start.1 = ((bf16[16,2,160,1024]{3,2,1,0:T(8,128)(2,1)}), bf16[16,2,160,1024]{3,2,1,0:T(8,128)(2,1)}, u32[]{:S(2)}, u32[]{:S(2)}) async-start(bf16[16,2,160,1024]{3,2,1,0:T(8,128)(2,1)} %copy.248), calls=%async_computation.1 | async-start | bytes 20971520 | tf_op jit(solution)/shard_map/all_to_all | solution.py:72
  857.0 180.0 %copy-start.78 = (f32[512,8]{0,1:T(8,128)S(1)}, f32[512,8]{0,1:T(8,128)}, u32[]{:S(2)}) copy-start(f32[512,8]{0,1:T(8,128)} %get-tuple-element.47) | copy-start | bytes 49156
  1027.0 188.6 %all-to-all-start.3 = ((bf16[16,2,160,1024]{3,2,1,0:T(8,128)(2,1)}), bf16[16,2,160,1024]{3,2,1,0:T(8,128)(2,1)}, u32[]{:S(2)}, u32[]{:S(2)}) async-start(bf16[16,2,160,1024]{3,2,1,0:T(8,128)(2,1)} %copy.252), calls=%async_computation.3 | async-start | bytes 20971520 | tf_op jit(solution)/shard_map/all_to_all | solution.py:72
  1036.5 297.1 %reduce-scatter.13.cloned.1.call-start = ((), (), s32[]{:S(2)}) async-start(), calls=%async_computation.19 | async-start | bytes 2621440 | tf_op jit(solution)/shard_map/reduce_scatter | solution.py:298
  1083.7 180.4 %copy-start.59 = (f32[512,32]{0,1:T(8,128)}, f32[512,32]{0,1:T(8,128)S(1)}, u32[]{:S(2)}) copy-start(f32[512,32]{0,1:T(8,128)S(1)} %select_reduce_fusion.2) | copy-start | bytes 196612
  1083.7 180.3 %copy-start.90 = (f32[512]{0:T(512)}, f32[512]{0:T(512)S(1)}, u32[]{:S(2)}) copy-start(f32[512]{0:T(512)S(1)} %multiply_reduce_fusion.9) | copy-start | bytes 6148
  1296.8 68.7 %reduce-scatter.15.cloned.1.call-start = ((), (), s32[]{:S(2)}) async-start(), calls=%async_computation.20 | async-start | bytes 2621440 | tf_op jit(solution)/shard_map/reduce_scatter | solution.py:304
  1306.7 126.2 %all-reduce.24.cloned.1.call-start = ((), (), s32[]{:S(2)}) async-start(), calls=%async_computation.21 | async-start | bytes 4194304 | tf_op jit(solution)/shard_map/psum | solution.py:341
  1370.7 102.1 %reduce-scatter.31.cloned.1.call-start = ((), (), s32[]{:S(2)}) async-start(), calls=%async_computation.29 | async-start | bytes 557056
  1373.7 176.2 %reduce-scatter.29.cloned.1.call-start = ((), (), s32[]{:S(2)}) async-start(), calls=%async_computation.28 | async-start | bytes 2228224 | tf_op jit(solution)/shard_map/reduce_scatter | solution.py:55
  1377.6 249.3 %reduce-scatter.23.cloned.1.call-start = ((), (), s32[]{:S(2)}) async-start(), calls=%async_computation.25 | async-start | bytes 2228224 | tf_op jit(solution)/shard_map/reduce_scatter | solution.py:52
  1382.4 320.2 %reduce-scatter.27.cloned.1.call-start = ((), (), s32[]{:S(2)}) async-start(), calls=%async_computation.27 | async-start | bytes 1114112 | tf_op jit(solution)/shard_map/reduce_scatter | solution.py:54
  1384.0 394.1 %reduce-scatter.25.cloned.1.call-start = ((), (), s32[]{:S(2)}) async-start(), calls=%async_computation.26 | async-start | bytes 1114112 | tf_op jit(solution)/shard_map/reduce_scatter | solution.py:53
  1387.2 424.4 %reduce-scatter.21.cloned.1.call-start = ((), (), s32[]{:S(2)}) async-start(), calls=%async_computation.24 | async-start | bytes 2621440 | tf_op jit(solution)/shard_map/reduce_scatter | solution.py:363
  1397.6 446.4 %reduce-scatter.17.cloned.1.call-start = ((), (), s32[]{:S(2)}) async-start(), calls=%async_computation.22 | async-start | bytes 2621440 | tf_op jit(solution)/shard_map/reduce_scatter | solution.py:361
  1407.9 468.4 %reduce-scatter.19.cloned.1.call-start = ((), (), s32[]{:S(2)}) async-start(), calls=%async_computation.23 | async-start | bytes 2621440 | tf_op jit(solution)/shard_map/reduce_scatter | solution.py:362
  1418.4 500.4 %all-reduce.26.cloned.1.call-start = ((), (), s32[]{:S(2)}) async-start(), calls=%async_computation.30 | async-start | bytes 786432 | tf_op jit(solution)/shard_map/psum | solution.py:43
  1426.0 352.1 %copy-start.6 = (f32[512,1024]{1,0:T(8,128)S(1)}, f32[512,1024]{1,0:T(8,128)}, u32[]{:S(2)}) copy-start(f32[512,1024]{1,0:T(8,128)} %copy-done.5) | copy-start | bytes 6291460
  1432.9 492.0 %copy-start.1 = (bf16[2,1024,256]{2,1,0:T(8,128)(2,1)S(1)}, bf16[2,1024,256]{2,1,0:T(8,128)(2,1)}, u32[]{:S(2)}) copy-start(bf16[2,1024,256]{2,1,0:T(8,128)(2,1)} %param.30) | copy-start | bytes 3145732
  (89 other events, 828.9 us)
Sparse Core Ops, SparseCore 0:
  71.3 34.7 all-gather.5
  108.3 33.8 all-gather.7
  144.3 42.5 all-gather.9
  188.9 42.0 all-gather.11
  234.5 27.9 all-reduce.21
  1296.9 36.6 reduce-scatter.12
  1336.0 29.3 reduce-scatter.14
  1370.9 26.8 all-reduce.23
  1400.9 71.8 reduce-scatter.30
  1476.3 73.5 reduce-scatter.28
  1553.2 73.6 reduce-scatter.22
  1630.3 72.2 reduce-scatter.26
  1705.8 72.2 reduce-scatter.24
  1781.0 30.5 reduce-scatter.20
  1814.5 29.3 reduce-scatter.16
  1846.9 29.3 reduce-scatter.18
  1878.7 40.0 all-reduce.25
where the time goes:
time: 1940 us; the launch traced here: 1930 us
  waiting for transfers between devices  945 us (49%)
  blocking collectives  433 us (22%)
  local copies, waits for them, and re-layouts  199 us (10%)
  matrix products  170 us (9%)
  other arithmetic  137 us (7%)
  starting transfers between devices  29 us (1%)
    all_to_all x2, waiting for transfers between devices, to_tokens(): lax.all_to_all(slots, 'fsdp', split_axis=0, concat_axis=0, tiled=True)  302 us
    all_gather x1, blocking collectives, local(): lax.all_gather(router, 'fsdp', axis=0, tiled=True)  188 us
    psum x1, blocking collectives, over_hidden(): return lax.psum(partial_sum, 'tensor').astype(jnp.bfloat16)  119 us
    all_to_all x2, waiting for transfers between devices, to_owners(): lax.all_to_all(slots, 'fsdp', split_axis=0, concat_axis=0, tiled=True)  104 us
    reduce_scatter x1, waiting for transfers between devices, across_fsdp(): lax.psum_scatter(items[1], 'fsdp', scatter_dimension=0, tiled=True)  77 us
    reduce_scatter x1, waiting for transfers between devices, across_fsdp(): lax.psum_scatter(items[3], 'fsdp', scatter_dimension=0, tiled=True)  75.7 us
    reduce_scatter x1, waiting for transfers between devices, across_fsdp(): lax.psum_scatter(items[2], 'fsdp', scatter_dimension=0, tiled=True)  75.5 us
    unnamed x2, blocking collectives  71.2 us
  transfers between devices with their start and end apart: 21, of which 17 were waited for; matrix products, arithmetic and copies ran while one was open for 16% of the time, Pallas kernels for 0%

commit v1 on v0

v1 whole, which is shorter than its diff:
```python
import functools

import jax
import jax.numpy as jnp
import numpy as np
from jax import lax
from jax.experimental import pallas as pl
from jax.experimental.pallas import tpu as pltpu
from jax.sharding import PartitionSpec as P

HD = 64
EXPERTS = 32
TOPK = 8
SEQ = 1024
D = 1024
ROWS = 512
HALF = 256
CAP = 160
MAIN = 96
MORE = 32
PIECES = 2
PAD = 272
N_FSDP = 16
N_CONTEXT = 4
EPS = 1e-06
NEGATIVE = -1e30
VMEM = 62 * 1024 * 1024
BF = jnp.bfloat16
F32 = jnp.float32
NT = (((1,), (1,)), ((), ()))
TN = (((0,), (0,)), ((), ()))


def dot(a, b):
    return jnp.dot(a, b, preferred_element_type=F32)


def dot_nt(a, b):
    return lax.dot_general(a, b, NT, preferred_element_type=F32)


def dot_tn(a, b):
    return lax.dot_general(a, b, TN, preferred_element_type=F32)


def split(v):
    high = v.astype(BF)
    return high, (v - high.astype(F32)).astype(BF)


def params(grid_dims):
    return pltpu.CompilerParams(
        dimension_semantics=("arbitrary",) * grid_dims, vmem_limit_bytes=VMEM
    )


def cost(flops, moved):
    return pl.CostEstimate(flops=flops, bytes_accessed=moved, transcendentals=0)


HBM = pl.BlockSpec(memory_space=pltpu.HBM)


def past(kernel, inputs, others):
    return lambda *refs: kernel(*refs[:inputs], *refs[inputs + others :])


def head_mean(v):
    rows = lax.broadcasted_iota(jnp.int32, (512, 256), 0) % 256 // HD
    cols = lax.broadcasted_iota(jnp.int32, (512, 256), 1) // HD
    block = jnp.where(rows == cols, 1.0, 0.0).astype(BF)
    return dot(jnp.concatenate(split(v), axis=1), block) * (1.0 / HD)


def swap_halves(v):
    lane = lax.broadcasted_iota(jnp.int32, v.shape, 1) % HD
    width = v.shape[1]
    return jnp.where(lane < HD // 2, pltpu.roll(v, width - 32, 1), pltpu.roll(v, 32, 1))


def twice(v):
    return jnp.concatenate([v, v], axis=1)


def rotary_tables():
    middle = HD // 2
    inverse = 10000.0 ** (-(2.0 * np.arange(middle, dtype=np.float64) / HD))
    inverse = inverse.astype(np.float32)
    angles = np.arange(SEQ, dtype=np.float32)[:, None] * inverse[None, :]
    angles = angles.astype(np.float64)
    cosine, sine = np.cos(angles).astype(np.float32), np.sin(angles).astype(np.float32)
    cosine = np.concatenate([cosine] * 4, axis=1)
    sine = np.concatenate([-sine, sine, -sine, sine], axis=1)
    order = lambda v: v.reshape(4, 4, 2, 32, 128).transpose(0, 2, 1, 3, 4).reshape(8, 128, 128)
    return order(cosine), order(sine)


def pack_kernel(where, w_query, w_key, w_value, w_out, router, gain1, gain2, q_gain, k_gain, out):
    out[:, 0:512] = w_query[...]
    out[:, 512:768] = w_key[...]
    out[:, 768:1024] = w_value[...]
    out[:, 1024:1536] = w_out[...]
    diagonal = lax.broadcasted_iota(jnp.int32, (64, 64), 0) == lax.broadcasted_iota(
        jnp.int32, (64, 64), 1
    )
    column = lambda v: jnp.sum(
        jnp.where(diagonal, v[...].astype(F32), 0.0), axis=1, keepdims=True
    )
    row = lax.broadcasted_iota(jnp.int32, (64, 128), 0)
    lane = lax.broadcasted_iota(jnp.int32, (64, 128), 1)
    small = jnp.where(lane == 32, column(gain1), 0.0) + jnp.where(lane == 33, column(gain2), 0.0)
    for i in range(4):
        here = lane == HD + 4 * where[0] + i
        for r, v in enumerate((q_gain, k_gain)):
            small = small + jnp.where(here & (row == r), v[0:1, i : i + 1].astype(F32), 0.0)
    out[:, 1536:1664] = small.astype(BF)
    out[:, 1536:1568] = router[...]


def pack(where, *arrays):
    whole = lambda v: pl.BlockSpec(v.shape, lambda i, r: (0, 0))
    return pl.pallas_call(
        pack_kernel,
        grid_spec=pltpu.PrefetchScalarGridSpec(
            num_scalar_prefetch=1,
            grid=(1,),
            in_specs=[whole(v) for v in arrays],
            out_specs=pl.BlockSpec((64, 1664), lambda i, r: (0, 0)),
        ),
        out_shape=jax.ShapeDtypeStruct((64, 1664), BF),
        compiler_params=params(1),
        cost_estimate=cost(10**6, 10**6),
        name="pack",
    )(where, *arrays)


def stack_pairs(blocks, *others):
    rows, width = blocks[0].shape

    def kernel(a, b, c, d, low, high):
        low[0], low[1] = a[...], b[...]
        high[0], high[1] = c[...], d[...]

    return pl.pallas_call(
        past(kernel, 4, len(others)),
        in_specs=[pl.BlockSpec(memory_space=pltpu.VMEM)] * 4 + [HBM] * len(others),
        out_shape=[jax.ShapeDtypeStruct((2, rows, width), BF)] * 2,
        compiler_params=pltpu.CompilerParams(vmem_limit_bytes=VMEM),
        cost_estimate=cost(10**6, 10**6),
        name="stack_pairs",
    )(*blocks, *others)


def add_blocks(arrays, handed=(), *others):
    blocks, n, k = arrays[0].shape[0], len(arrays), len(handed)

    def kernel(*refs):
        for i, out in enumerate(refs[n + k + len(others) :][:blocks]):
            total = refs[0][i].astype(F32)
            for ref in refs[1:n]:
                total = total + ref[i].astype(F32)
            out[...] = total.astype(BF)

    vmem = pl.BlockSpec(memory_space=pltpu.VMEM)
    out = pl.pallas_call(
        kernel,
        in_specs=[vmem] * n + [HBM] * (k + len(others)),
        out_specs=[vmem] * blocks + [HBM] * k,
        out_shape=[jax.ShapeDtypeStruct(arrays[0].shape[1:], BF)] * blocks
        + [jax.ShapeDtypeStruct(v.shape, v.dtype) for v in handed],
        input_output_aliases={n + i: blocks + i for i in range(k)},
        compiler_params=pltpu.CompilerParams(vmem_limit_bytes=VMEM),
        cost_estimate=cost(10**9, 10**7),
        name="add_blocks",
    )(*arrays, *handed, *others)
    return out[:blocks], *out[blocks:]


def pack_cotangent(where, cotangent, table, *others):
    def kernel(where, rows, table, out):
        out[0:HALF, :] = rows[...].reshape(HALF, D)
        out[HALF:PAD, :] = jnp.concatenate([table[...], jnp.zeros((8, D), BF)], axis=0)

    return pl.pallas_call(
        past(kernel, 3, len(others)),
        grid_spec=pltpu.PrefetchScalarGridSpec(
            num_scalar_prefetch=1,
            grid=(1,),
            in_specs=[
                pl.BlockSpec((2, 4, 1, 32, D), lambda i, r: (0, 0, r[0], 0, 0)),
                pl.BlockSpec((8, D), lambda i, r: (0, 0)),
            ]
            + [HBM] * len(others),
            out_specs=pl.BlockSpec((PAD, D), lambda i, r: (0, 0)),
        ),
        out_shape=jax.ShapeDtypeStruct((PAD, D), BF),
        compiler_params=params(1),
        cost_estimate=cost(10**6, 10**6),
        name="pack_cotangent",
    )(where, cotangent.reshape(2, 4, 2, 32, D), table, *others)


def project_kernel(
    order, near, x0, x1, x2, x3, x4, x5, x6, x7, w0, w1, w2, w3, cos_all, sin_all,
    w, small, heads, cosine, sine, normed, k_proj, k_b, v_b, q_proj, q_b,
):
    @pl.when(pl.program_id(0) == 0)
    def _():
        for i, shards in enumerate((w0, w1, w2, w3)):
            for j in range(4):
                to = pl.ds(pl.multiple_of(order[4 * i + j] * 64, 64), 64)
                w[to, :] = shards[j]
        for i in range(8):
            cosine[i * 128 : i * 128 + 128, :] = cos_all[near[i]]
            sine[i * 128 : i * 128 + 128, :] = sin_all[near[i]]
        last = w[:, 1536:1664].astype(F32)
        small[...] = last.T
        summed = last[0:64]
        for i in range(1, N_FSDP):
            summed = summed + last[i * 64 : i * 64 + 64]
        lane = lax.broadcasted_iota(jnp.int32, (8, 128), 1)
        gains = jnp.where(lane >= HD, summed[0:8], 0.0)
        heads[...] = gains + pltpu.roll(gains, HD, 1)

    gain = small[32:33, :]
    for i, x in enumerate((x0, x1, x2, x3, x4, x5, x6, x7)):
        values = x[0].astype(F32)
        factor = lax.rsqrt(jnp.mean(values * values, axis=1, keepdims=True) + EPS)
        normed[0, i * 128 : i * 128 + 128, :] = (values * factor * gain).astype(BF)
    both = dot(normed[0], w[:, 512:1024])
    keys = both[:, 0:256]
    k_proj[0] = keys
    v_b[0] = both[:, 256:512].astype(BF)
    cos, sin = twice(cosine[...]), twice(sine[...])
    scaled = keys * lax.rsqrt(head_mean(keys * keys) + EPS) * twice(heads[1:2, :])
    k_b[0] = (scaled * cos + swap_halves(scaled) * sin).astype(BF)
    queries = dot(normed[0, 0:256, :], w[:, 0:512])
    q_proj[0] = queries
    for block in range(2):
        at = slice(block * 256, block * 256 + 256)
        head = queries[:, at]
        scaled = head * lax.rsqrt(head_mean(head * head) + EPS) * twice(heads[0:1, :])
        turned = scaled * cos[0:256] + swap_halves(scaled) * sin[0:256]
        q_b[0, :, at] = (turned.astype(BF).astype(F32) * 0.125).astype(BF)


def project(order, near, tokens, shards, cosine, sine, *others):
    row = lambda s, r, n: (0, 0)
    of = lambda s, r, n: (s, 0, 0)
    block = lambda i: pl.BlockSpec((1, 128, D), lambda s, r, n: (n[i], s, 0))
    fixed = ((D, 1664, BF), (128, D, F32), (8, 128, F32), (SEQ, 128, F32), (SEQ, 128, F32))
    shapes = ((SEQ, D, BF), (SEQ, 256, F32), (SEQ, 256, BF), (SEQ, 256, BF), (256, 512, F32), (256, 512, BF))
    return pl.pallas_call(
        past(project_kernel, 16, len(others)),
        grid_spec=pltpu.PrefetchScalarGridSpec(
            num_scalar_prefetch=2,
            grid=(2,),
            in_specs=[block(i) for i in range(8)]
            + [pl.BlockSpec((4, 64, 1664), lambda s, r, n: (0, 0, 0))] * 4
            + [pl.BlockSpec((8, 128, 128), lambda s, r, n: (0, 0, 0))] * 2
            + [HBM] * len(others),
            out_specs=[pl.BlockSpec((r, n), row) for r, n, _ in fixed]
            + [pl.BlockSpec((1, r, n), of) for r, n, _ in shapes],
        ),
        out_shape=[jax.ShapeDtypeStruct((r, n), dt) for r, n, dt in fixed]
        + [jax.ShapeDtypeStruct((2, r, n), dt) for r, n, dt in shapes],
        compiler_params=params(1),
        cost_estimate=cost(10 * 10**9, 20 * 10**6),
        name="project",
    )(order, near, *([tokens] * 8), *shards, cosine, sine, *others)


def as_column(row):
    return jnp.broadcast_to(row, (8, row.shape[1])).T[:, 0:1]


def place_head(v, target, source):
    moved = v if target == source else pltpu.roll(v, HD, 1)
    lane = lax.broadcasted_iota(jnp.int32, v.shape, 1) // HD
    return jnp.where(lane == target, moved, jnp.zeros_like(moved))


def stack_heads(v):
    parts = []
    for block in range(2):
        for j in range(2):
            parts.append(place_head(v[:, block * 128 : block * 128 + 128], block, j))
    return jnp.concatenate(parts, axis=0)


def unstack_heads(v):
    blocks = []
    for block in range(2):
        pair = [v[(2 * block + j) * 256 : (2 * block + j + 1) * 256] for j in range(2)]
        blocks.append(place_head(pair[0], 0, block) + place_head(pair[1], 1, block))
    return jnp.concatenate(blocks, axis=1)


def attend_kernel(q, k, v, seg, w_out, attended, mine, other):
    row = seg[0]
    mask = jnp.where(as_column(row[:, 0:HALF]) == row, 0.0, NEGATIVE)
    queries = stack_heads(q[0].astype(F32)).astype(BF)
    scores = dot_nt(queries, k[0])
    weights = jnp.concatenate(
        [jnp.exp(scores[i * 256 : i * 256 + 256] + mask).astype(BF) for i in range(4)], axis=0
    )
    summed = dot(weights, jnp.concatenate([v[0], jnp.ones((SEQ, 128), BF)], axis=1))
    mixed = unstack_heads(summed[:, :128] / summed[:, 128:]).astype(BF)
    attended[0] = mixed
    part = dot_nt(mixed, w_out[...])

    @pl.when(pl.program_id(1) == 0)
    def _():
        mine[...] = part[0:128]
        other[...] = part[128:256]

    @pl.when(pl.program_id(1) != 0)
    def _():
        mine[...] += part[0:128]
        other[...] += part[128:256]


def attend(q_b, k_b, v_b, seg, w_out, *others):
    half = pl.BlockSpec((128, D), lambda s, p: (s, 0))
    return pl.pallas_call(
        past(attend_kernel, 5, len(others)),
        grid=(2, 2),
        in_specs=[
            pl.BlockSpec((1, HALF, 256), lambda s, p: (s, 0, p)),
            pl.BlockSpec((1, SEQ, 128), lambda s, p: (s, 0, p)),
            pl.BlockSpec((1, SEQ, 128), lambda s, p: (s, 0, p)),
            pl.BlockSpec((1, 1, SEQ), lambda s, p: (s, 0, 0)),
            pl.BlockSpec((D, 256), lambda s, p: (0, 4 + p)),
        ]
        + [HBM] * len(others),
        out_specs=[pl.BlockSpec((1, HALF, 256), lambda s, p: (s, 0, p)), half, half],
        out_shape=[
            jax.ShapeDtypeStruct((2, HALF, 512), BF),
            jax.ShapeDtypeStruct((HALF, D), F32),
            jax.ShapeDtypeStruct((HALF, D), F32),
        ],
        compiler_params=params(2),
        cost_estimate=cost(10 * 10**9, 8 * 10**6),
        name="attend",
    )(q_b, k_b, v_b, seg, w_out, *others)


def experts_to_rows(table):
    return jnp.concatenate([table[8 * k : 8 * k + 8] for k in range(4)], axis=1)


def rows_to_experts(rows):
    return jnp.concatenate([rows[:, 256 * k : 256 * k + 256] for k in range(4)], axis=0)


def route_kernel(tokens, mine, other, small, match, kept, hidden, payload, probs, totals):
    values = tokens[...].astype(F32) + mine[...] + other[...]
    hidden[...] = values
    factor = lax.rsqrt(jnp.mean(values * values, axis=1, keepdims=True) + EPS)
    rows = (values * factor * small[33:34, :]).astype(BF)
    payload[0:HALF, :] = rows
    logits = dot_nt(small[0:32, :].astype(BF), rows)
    raised = jnp.exp(logits - jnp.max(logits, axis=0, keepdims=True))
    prob = raised / jnp.sum(raised, axis=0, keepdims=True)
    probs[...] = prob
    chosen = prob * match[...]
    total = jnp.sum(chosen, axis=0, keepdims=True)
    totals[...] = total
    high, low = split(experts_to_rows(chosen / total * kept[...]))
    payload[HALF:PAD, :] = jnp.concatenate([high, low], axis=0)


def route(*args):
    return pl.pallas_call(
        past(route_kernel, 6, len(args) - 6),
        in_specs=[pl.BlockSpec(memory_space=pltpu.VMEM)] * 6 + [HBM] * (len(args) - 6),
        out_shape=[
            jax.ShapeDtypeStruct((HALF, D), F32),
            jax.ShapeDtypeStruct((PAD, D), BF),
            jax.ShapeDtypeStruct((EXPERTS, HALF), F32),
            jax.ShapeDtypeStruct((1, HALF), F32),
        ],
        compiler_params=pltpu.CompilerParams(vmem_limit_bytes=VMEM),
        cost_estimate=cost(10**8, 5 * 10**6),
        name="route",
    )(*args)


def own_row(table, lane_block, row):
    picked = jnp.zeros((8, 256), F32)
    for k in range(4):
        picked = picked + jnp.where(lane_block == k, table[:, 256 * k : 256 * k + 256], 0.0)
    number = lax.broadcasted_iota(jnp.int32, (8, 256), 0)
    return jnp.sum(jnp.where(number == row, picked, 0.0), axis=0, keepdims=True)


def expert_math(x, g, gate, w):
    pre = dot(x, w[:, 0:1024])
    grad_all = dot(g, w[:, 1024:1536])
    acts, grads, gate_dot = [], [], 0.0
    for part in range(2):
        gate_pre = pre[:, part * 512 : part * 512 + 256]
        up_pre = pre[:, part * 512 + 256 : part * 512 + 512]
        grad = grad_all[:, part * 256 : part * 256 + 256]
        sig = jax.nn.sigmoid(gate_pre)
        swish = gate_pre * sig
        act = (swish * up_pre).astype(BF).astype(F32)
        gate_dot = gate_dot + jnp.sum(act * grad, axis=1, keepdims=True)
        acts.append((act * gate).astype(BF))
        grad = grad * gate
        grads.append((grad * up_pre * sig * (1.0 + gate_pre * (1.0 - sig))).astype(BF))
        grads.append((grad * swish).astype(BF))
    act = jnp.concatenate(acts, axis=1)
    grad = jnp.concatenate(grads, axis=1)
    y = dot_nt(act, w[:, 1024:1536]).astype(BF)
    back = dot_nt(grad, w[:, 0:1024]).astype(BF)
    return y, back, act, grad, gate_dot


def pick_rows(places, first, rows):
    number = lax.broadcasted_iota(jnp.int32, (rows, 256), 0) + first
    return number == places.astype(jnp.int32)


def expert_kernel(order, where_at, x_low, x_high, c_low, c_high, w_m, w_o, *refs):
    refs = refs[len(refs) - 29 :]
    out_y, out_x, kept_x, kept_g, kept_h, more_x, more_g, more_h, pieces = refs[:9]
    x_all, c_all, wv, xs, gs, hs, picks, sums, ys, bs, total, places, gate_rows, dots = refs[9:23]
    mx, mg, mh = refs[23:26]
    in_sem, out_sem, more_sem = refs[26:]
    chunk = where_at[2]
    lane_block, row_at = where_at[0], where_at[1]
    copy = pltpu.make_async_copy
    loads = [
        copy(x_low, x_all.at[0:2], in_sem.at[0]),
        copy(c_low, c_all.at[0:2], in_sem.at[1]),
        copy(x_high, x_all.at[2:4], in_sem.at[2]),
        copy(c_high, c_all.at[2:4], in_sem.at[3]),
    ]

    def load_w(e):
        return [
            copy(w_m.at[e, :, 0:512], wv.at[e, :, 0:512], in_sem.at[4 + e]),
            copy(w_o.at[e, :, 0:512], wv.at[e, :, 512:1024], in_sem.at[6 + e]),
            copy(w_m.at[e, :, 512:768], wv.at[e, :, 1024:1280], in_sem.at[8 + e]),
            copy(w_o.at[e, :, 512:768], wv.at[e, :, 1280:1536], in_sem.at[10 + e]),
        ]

    for load in loads + load_w(0) + load_w(1):
        load.start()
    for load in loads:
        load.wait()

    def gather(h, carry):
        table = c_all[h, HALF : HALF + 8, :].astype(F32)
        gate_table = x_all[h, HALF:PAD, :].astype(F32)
        gate_table = gate_table[0:8] + gate_table[8:16]
        pick = []
        for e in range(2):
            row = own_row(table, lane_block, row_at + e)
            places[pl.ds(4 * e + h, 1), :] = row
            gate_rows[pl.ds(4 * e + h, 1), :] = own_row(gate_table, lane_block, row_at + e)
            pick.append(jnp.where(pick_rows(row, 0, MAIN), 1.0, 0.0))
        pick = jnp.concatenate(pick, axis=0).astype(BF)
        picks[h] = pick
        x = dot(pick, x_all[h, 0:HALF, :]).astype(BF)
        g = dot(pick, c_all[h, 0:HALF, :]).astype(BF)
        to = pl.ds(pl.multiple_of(h * MAIN, MAIN), MAIN)
        for e in range(2):
            xs[e, to, :] = x[e * MAIN : e * MAIN + MAIN]
            gs[e, to, :] = g[e * MAIN : e * MAIN + MAIN]
        return carry

    lax.fori_loop(0, 4, gather, 0)
    rows = pl.ds(pl.multiple_of(chunk * (4 * MAIN), 4 * MAIN), 4 * MAIN)
    sends = [copy(xs.at[e], kept_x.at[e, rows], out_sem.at[e]) for e in range(2)]
    sends += [copy(gs.at[e], kept_g.at[e, rows], out_sem.at[2 + e]) for e in range(2)]
    for send in sends:
        send.start()
    send_h = lambda e: copy(hs.at[e], kept_h.at[e, rows], out_sem.at[4 + e])
    send_x = lambda h: copy(bs.at[h], out_x.at[h], out_sem.at[6 + h])
    send_y = lambda h: copy(ys.at[h], out_y.at[order[h]], out_sem.at[10 + h])

    def gates(e, first, count):
        here = [pick_rows(places[pl.ds(4 * e + h, 1), :], first, count) for h in range(4)]
        columns = [
            jnp.sum(
                jnp.where(here[h], gate_rows[pl.ds(4 * e + h, 1), :], 0.0), axis=1, keepdims=True
            )
            for h in range(4)
        ]
        return here, jnp.concatenate(columns, axis=0)

    def spread(here, gate_dot, count, h):
        part = gate_dot[h * count : h * count + count]
        return jnp.sum(jnp.where(here[h], part, 0.0), axis=0, keepdims=True)

    def math(e, carry):
        here, gate = gates(e, 0, MAIN)
        for load in load_w(e):
            load.wait()
        y, back, act, grad, gate_dot = expert_math(xs[e], gs[e], gate, wv.at[e])
        hs[e, :, 0:512] = act
        hs[e, :, 512:1536] = grad
        send_h(e).start()
        to = pl.ds(pl.multiple_of(e * MAIN, MAIN), MAIN)
        for h in range(4):
            sums[h, to, 0:D] = y[h * MAIN : h * MAIN + MAIN]
            sums[h, to, D : 2 * D] = back[h * MAIN : h * MAIN + MAIN]
            dots[pl.ds(4 * e + h, 1), :] = spread(here, gate_dot, MAIN, h)
        return carry

    lax.fori_loop(0, 2, math, 0)

    counts = []
    for e in range(2):
        most = jnp.max(places[4 * e : 4 * e + 4, :]).astype(jnp.int32) + 1
        counts.append((jnp.maximum(most - MAIN, 0) + MORE - 1) // MORE)
        pieces[e] = jnp.zeros((8, 128), F32) + counts[e].astype(F32)

    @pl.when(counts[0] + counts[1] > 0)
    def _():
        total[...] = jnp.zeros_like(total)

        def piece(n, carry):
            e = jnp.where(n < counts[0], 0, 1)
            i = n - e * counts[0]
            here, gate = gates(e, MAIN + i * MORE, MORE)
            pick = [jnp.where(v, 1.0, 0.0).astype(BF) for v in here]
            for h in range(4):
                to = slice(h * MORE, h * MORE + MORE)
                mx[to, :] = dot(pick[h], x_all[h, 0:HALF, :]).astype(BF)
                mg[to, :] = dot(pick[h], c_all[h, 0:HALF, :]).astype(BF)
            y, back, act, grad, gate_dot = expert_math(mx[...], mg[...], gate, wv.at[e])
            mh[:, 0:512] = act
            mh[:, 512:1536] = grad
            to = pl.ds(pl.multiple_of(i * 4 * MORE, 4 * MORE), 4 * MORE)
            extra = [
                copy(v, far.at[e, to], more_sem.at[k])
                for k, (v, far) in enumerate(((mx, more_x), (mg, more_g), (mh, more_h)))
            ]
            for send in extra:
                send.start()
            both = jnp.concatenate([y, back], axis=1)
            for h in range(4):
                part = both[h * MORE : h * MORE + MORE]
                total[h * HALF : h * HALF + HALF, :] += dot_tn(pick[h], part)
                dots[pl.ds(4 * e + h, 1), :] += spread(here, gate_dot, MORE, h)
            for send in extra:
                send.wait()
            return carry

        lax.fori_loop(0, counts[0] + counts[1], piece, 0)

    def scatter(h, carry):
        out = dot_tn(picks[h], sums[h])
        ys[h] = out[:, 0:D].astype(BF)
        bs[h, 0:HALF, :] = out[:, D : 2 * D].astype(BF)
        row = lax.broadcasted_iota(jnp.int32, (8, 256), 0)
        table = jnp.where(row == row_at, dots[pl.ds(h, 1), :], 0.0)
        table = table + jnp.where(row == row_at + 1, dots[pl.ds(4 + h, 1), :], 0.0)
        table = [jnp.where(lane_block == k, table, 0.0) for k in range(4)]
        high, low = split(jnp.concatenate(table, axis=1))
        bs[h, HALF:PAD, :] = jnp.concatenate([high, low], axis=0)

        @pl.when(counts[0] + counts[1] > 0)
        def _():
            at = pl.ds(pl.multiple_of(h * HALF, HALF), HALF)
            ys[h] = (ys[h].astype(F32) + total[at, 0:D]).astype(BF)
            bs[h, 0:HALF, :] = (bs[h, 0:HALF, :].astype(F32) + total[at, D : 2 * D]).astype(BF)

        send_x(h).start()
        send_y(h).start()
        return carry

    lax.fori_loop(0, 4, scatter, 0)
    for send in sends:
        send.wait()
    for e in range(2):
        send_h(e).wait()
    for h in range(4):
        send_x(h).wait()
        send_y(h).wait()


def expert_chunk(order, where_at, x, cotangents, mine, other, kept, *others):
    rows, more = 4 * MAIN, 4 * MORE * PIECES
    widths = (D, D, 1536)
    shape = lambda *v: jax.ShapeDtypeStruct(v, BF)
    vmem = lambda *v: pltpu.VMEM(v, BF)
    aliases = {8: 0, 9: 2, 10: 3, 11: 4} if kept else {}
    return pl.pallas_call(
        expert_kernel,
        grid_spec=pltpu.PrefetchScalarGridSpec(
            num_scalar_prefetch=2,
            grid=(1,),
            in_specs=[HBM] * (6 + len(kept) + len(others)),
            out_specs=[HBM] * 8 + [pl.BlockSpec((2, 8, 128), lambda i, r, w: (0, 0, 0))],
            scratch_shapes=[
                vmem(4, PAD, D),
                vmem(4, PAD, D),
                vmem(2, D, 1536),
                vmem(2, rows, D),
                vmem(2, rows, D),
                vmem(2, rows, 1536),
                vmem(4, 2 * MAIN, 256),
                vmem(4, 2 * MAIN, 2 * D),
                vmem(4, HALF, D),
                vmem(4, PAD, D),
                pltpu.VMEM((1024, 2 * D), F32),
                pltpu.VMEM((8, 256), F32),
                pltpu.VMEM((8, 256), F32),
                pltpu.VMEM((8, 256), F32),
                vmem(4 * MORE, D),
                vmem(4 * MORE, D),
                vmem(4 * MORE, 1536),
                pltpu.SemaphoreType.DMA((12,)),
                pltpu.SemaphoreType.DMA((14,)),
                pltpu.SemaphoreType.DMA((3,)),
            ],
        ),
        out_shape=[shape(N_FSDP, HALF, D), shape(4, PAD, D)]
        + [shape(2, 4 * rows, n) for n in widths]
        + [shape(2, more, n) for n in widths]
        + [jax.ShapeDtypeStruct((2, 8, 128), F32)],
        input_output_aliases=aliases,
        compiler_params=params(1),
        cost_estimate=cost(14 * 10**9, 30 * 10**6),
        name="experts",
    )(order, where_at, *x, *cotangents, mine, other, *kept, *others)


def expert_weight_kernel(place, x, g, act, grad, *refs):
    more, counts, (down, gate_up), (mx, mg, mh) = refs[:12], refs[12:16], refs[-5:-3], refs[-3:]
    out = refs[-6]
    expert, part = pl.program_id(0), pl.program_id(1)
    down[...] = dot_tn(g[0], act[0])
    gate_up[...] = dot_tn(x[0], grad[0])
    for chunk in range(4):
        count = jnp.max(counts[chunk][0]).astype(jnp.int32)

        @pl.when(count > 0)
        def _(chunk=chunk, count=count):
            def piece(i, carry):
                rows = pl.ds(pl.multiple_of(i * 4 * MORE, 4 * MORE), 4 * MORE)
                for ref, to in zip(more[3 * chunk : 3 * chunk + 3], (mx, mg, mh)):
                    pltpu.sync_copy(ref.at[expert, rows], to)
                for p in range(2):

                    @pl.when(part == p)
                    def _(p=p):
                        at = p * 256
                        down[...] += dot_tn(mg[...], mh[:, at : at + 256])
                        at = 512 + p * 512
                        gate_up[...] += dot_tn(mx[...], mh[:, at : at + 512])

                return carry

            lax.fori_loop(0, count, piece, 0)

    for c in range(4):
        at = slice(c * 256, c * 256 + 256)
        out[c, 0, 0, :, 0:512] = gate_up[at, :].astype(BF)
        out[c, 0, 0, :, 512:768] = down[at, :].astype(BF)


def expert_weights(place, kept, more, counts, *others):
    rows = 16 * MAIN
    by_expert = lambda e, p, r: (e, 0, 0)
    return pl.pallas_call(
        expert_weight_kernel,
        grid_spec=pltpu.PrefetchScalarGridSpec(
            num_scalar_prefetch=1,
            grid=(2, 2),
            in_specs=[
                pl.BlockSpec((1, rows, D), by_expert),
                pl.BlockSpec((1, rows, D), by_expert),
                pl.BlockSpec((1, rows, 256), lambda e, p, r: (e, 0, p)),
                pl.BlockSpec((1, rows, 512), lambda e, p, r: (e, 0, 1 + p)),
            ]
            + [HBM] * 12
            + [pl.BlockSpec((1, 8, 128), by_expert)] * 4
            + [HBM] * len(others),
            out_specs=pl.BlockSpec(
                (4, 1, 1, 256, 768),
                lambda e, p, r: (0, jnp.where(p == 0, r[0], 1 - r[0]), e, 0, 0),
            ),
            scratch_shapes=[
                pltpu.VMEM((D, 256), F32),
                pltpu.VMEM((D, 512), F32),
                pltpu.VMEM((4 * MORE, D), BF),
                pltpu.VMEM((4 * MORE, D), BF),
                pltpu.VMEM((4 * MORE, 1536), BF),
            ],
        ),
        out_shape=jax.ShapeDtypeStruct((4, 2, 2, 256, 768), BF),
        compiler_params=params(2),
        cost_estimate=cost(20 * 10**9, 30 * 10**6),
        name="expert_weights",
    )(place, kept[0], kept[1], kept[2], kept[2], *more, *counts, *others)


def route_back_kernel(
    own, first, second, third, cotangent, hidden, small, normed, probs, totals, match,
    grad_hidden, grad_branch, grad_router, grad_gain,
):
    summed = own[...].astype(F32) + first[...].astype(F32)
    summed = summed + (second[...].astype(F32) + third[...].astype(F32))
    tables = summed[HALF:PAD, :]
    grad_gates = rows_to_experts(tables[0:8] + tables[8:16])
    prob, total = probs[...], totals[...]
    chosen = prob * match[...]
    shared = jnp.sum(grad_gates * chosen, axis=0, keepdims=True) / (total * total)
    grad_prob = (grad_gates / total - shared) * match[...]
    grad_logits = prob * (grad_prob - jnp.sum(prob * grad_prob, axis=0, keepdims=True))
    high, low = split(grad_logits)
    grad_router[...] = dot(high, normed[0:HALF, :]) + dot(low, normed[0:HALF, :])
    router = small[0:32, :].astype(BF)
    grad_normed = summed[0:HALF, :] + dot_tn(high, router) + dot_tn(low, router)
    values = hidden[...]
    factor = lax.rsqrt(jnp.mean(values * values, axis=1, keepdims=True) + EPS)
    grad_gain[...] = jnp.sum(grad_normed * values * factor, axis=0, keepdims=True)
    weighted = grad_normed * small[33:34, :]
    mean = jnp.mean(weighted * values, axis=1, keepdims=True)
    grad = cotangent[0:HALF, :].astype(F32) + factor * weighted - values * (factor * factor * factor * mean)
    grad_hidden[...] = grad
    grad_branch[...] = grad.astype(BF)


def route_back(handed, *args):
    n, others, shapes = len(handed), len(args) - 11, [jax.ShapeDtypeStruct(v.shape, v.dtype) for v in handed]
    vmem = pl.BlockSpec(memory_space=pltpu.VMEM)
    kernel = past(route_back_kernel, 11, others + n)
    return pl.pallas_call(
        lambda *refs: kernel(*refs[n:]),
        in_specs=[HBM] * n + [vmem] * 11 + [HBM] * others,
        out_specs=[HBM] * n + [vmem] * 4,
        input_output_aliases={i: i for i in range(n)},
        out_shape=shapes
        + [
            jax.ShapeDtypeStruct((HALF, D), F32),
            jax.ShapeDtypeStruct((HALF, D), BF),
            jax.ShapeDtypeStruct((EXPERTS, D), F32),
            jax.ShapeDtypeStruct((1, D), F32),
        ],
        compiler_params=pltpu.CompilerParams(vmem_limit_bytes=VMEM),
        cost_estimate=cost(4 * 10**9, 6 * 10**6),
        name="route_back",
    )(*handed, *args)


def norm_back_heads(grad, proj, gain, cosine, sine):
    turned = grad * cosine - swap_halves(grad) * sine
    factor = lax.rsqrt(head_mean(proj * proj) + EPS)
    weighted = turned * gain
    mean = head_mean(weighted * proj)
    back = factor * weighted - proj * (factor * factor * factor * mean)
    return back, jnp.sum(turned * proj * factor, axis=0, keepdims=True)


def attend_back_kernel(
    q, q_proj, k, k_proj, v, seg, branch_m, branch_o, w_out, attended,
    cosine, sine, heads, grad_q, grad_k, grad_v, gains,
):
    row = seg[0]
    mask = jnp.where(as_column(row) == row[:, 0:HALF], 0.0, NEGATIVE)
    keys, values = k[0], v[0]
    grad_branch = jnp.concatenate([branch_m[...], branch_o[...]], axis=0)
    grad_mixed = dot(grad_branch, w_out[...]).astype(BF).astype(F32)
    queries = stack_heads(q[0].astype(F32)).astype(BF)
    grads = stack_heads(grad_mixed).astype(BF)
    high, low = split(stack_heads(attended[0].astype(F32) * grad_mixed))
    ones = jnp.ones((8, 256), BF)
    row_dot = dot_nt(ones, jnp.concatenate([high, low], axis=1))[0:1]
    scores = dot_nt(keys, queries)
    grad_probs = dot_nt(values, grads)
    probs_b, grad_scores = [], []
    for i in range(4):
        at = slice(i * 256, i * 256 + 256)
        raised = jnp.exp(scores[:, at] + mask)
        probs = raised * (1.0 / jnp.sum(raised, axis=0, keepdims=True))
        probs_b.append(probs.astype(BF))
        grad_scores.append((probs * (grad_probs[:, at] - row_dot[:, at])).astype(BF))
    probs_b = jnp.concatenate(probs_b, axis=1)
    grad_scores = jnp.concatenate(grad_scores, axis=1)
    grad_v[0] = dot(probs_b, grads).astype(BF)
    sum_k = dot(grad_scores, queries)
    sum_q = unstack_heads(dot_tn(grad_scores, keys) * 0.125)
    cos, sin = cosine[...], sine[...]
    back, gain_q = norm_back_heads(
        sum_q, q_proj[0], twice(heads[0:1, :]), twice(cos[0:256]), twice(sin[0:256])
    )
    grad_q[0] = back.astype(BF)
    wide = lambda value: jnp.concatenate([value[0:512], value[512:1024]], axis=1)
    back, gain_k = norm_back_heads(
        wide(sum_k), wide(k_proj[0]), twice(heads[1:2, :]), wide(cos), wide(sin)
    )
    grad_k[0, 0:512, :] = back[:, 0:128].astype(BF)
    grad_k[0, 512:1024, :] = back[:, 128:256].astype(BF)
    part = jnp.concatenate([gain_q, gain_k, jnp.zeros((6, 256), F32)], axis=0)

    @pl.when((pl.program_id(0) == 0) & (pl.program_id(1) == 0))
    def _():
        gains[...] = part

    @pl.when((pl.program_id(0) != 0) | (pl.program_id(1) != 0))
    def _():
        gains[...] += part


def attend_back(
    q_b, q_proj, k_b, k_proj, v_b, seg, branch_m, branch_o, w_out, attended,
    cosine, sine, heads,
):
    queries = pl.BlockSpec((1, HALF, 256), lambda s, p: (s, 0, p))
    keys = pl.BlockSpec((1, SEQ, 128), lambda s, p: (s, 0, p))
    table = pl.BlockSpec((SEQ, 128), lambda s, p: (0, 0))
    gain = pl.BlockSpec((8, 128), lambda s, p: (0, 0))
    half = pl.BlockSpec((128, D), lambda s, p: (s, 0))
    return pl.pallas_call(
        attend_back_kernel,
        grid=(2, 2),
        in_specs=[
            queries, queries, keys, keys, keys,
            pl.BlockSpec((1, 1, SEQ), lambda s, p: (s, 0, 0)),
            half, half,
            pl.BlockSpec((D, 256), lambda s, p: (0, 4 + p)),
            queries, table, table, gain,
        ],
        out_specs=[queries, keys, keys, pl.BlockSpec((8, 256), lambda s, p: (0, 0))],
        out_shape=[
            jax.ShapeDtypeStruct((2, HALF, 512), BF),
            jax.ShapeDtypeStruct((2, SEQ, 256), BF),
            jax.ShapeDtypeStruct((2, SEQ, 256), BF),
            jax.ShapeDtypeStruct((8, 256), F32),
        ],
        compiler_params=params(2),
        cost_estimate=cost(18 * 10**9, 16 * 10**6),
        name="attend_back",
    )(
        q_b, q_proj, k_b, k_proj, v_b, seg, branch_m, branch_o, w_out, attended,
        cosine, sine, heads,
    )


def weight_grads_kernel(
    place, normed, gq, gk, gv, branch_m, branch_o, mixed, router, gain, head_gains,
    out_0, out_1, out_2, out_3, out, sem,
):
    step = pl.program_id(0)
    rows = jnp.concatenate([normed[0], normed[1]], axis=0)
    own = jnp.concatenate([normed[0, 0:256, :], normed[1, 0:256, :]], axis=0)
    keys = jnp.concatenate(
        [
            jnp.concatenate([gk[0], gk[1]], axis=0),
            jnp.concatenate([gv[0], gv[1]], axis=0),
        ],
        axis=1,
    )
    queries = jnp.concatenate([gq[0], gq[1]], axis=0)
    branch = jnp.concatenate(
        [branch_m[0:128], branch_o[0:128], branch_m[128:256], branch_o[128:256]], axis=0
    )
    heads = jnp.concatenate([mixed[0], mixed[1]], axis=0)
    at = lax.broadcasted_iota(jnp.int32, (256, 256), 1)
    share = 4 * (at // HD + 4 * step) + at % HD
    spread = (lax.broadcasted_iota(jnp.int32, (256, 256), 0) % HD == share) & (at % HD < 4)
    spread = jnp.where(spread, 1.0, 0.0).astype(BF)
    high, low = split(head_gains[...])
    spread = dot(high, spread) + dot(low, spread)
    row = lax.broadcasted_iota(jnp.int32, (8, 256), 0)
    last = jnp.where(row == 0, gain[...], 0.0)
    last = last + jnp.where(row == 1, spread[0:1], 0.0) + jnp.where(row == 2, spread[1:2], 0.0)
    small = jnp.concatenate([router[...], last, jnp.zeros((88, 256), F32)], axis=0)
    parts = (
        (0, 512, dot_tn(own, queries).astype(BF)),
        (512, 1024, dot_tn(rows, keys).astype(BF)),
        (1024, 1536, dot_tn(branch, heads).astype(BF)),
        (1536, 1664, small.T.astype(BF)),
    )
    for i in range(4):
        to = place[4 * step + i]
        for low, high, value in parts:
            out[to, :, low:high] = value[i * 64 : i * 64 + 64]

    @pl.when(step == 3)
    def _():
        sends = [
            pltpu.make_async_copy(out.at[4 * i : 4 * i + 4], to, sem.at[i])
            for i, to in enumerate((out_0, out_1, out_2, out_3))
        ]
        for send in sends:
            send.start()
        for send in sends:
            send.wait()


def weight_grads(place, *args):
    fixed = lambda i, r: (0, 0, 0)
    column = pl.BlockSpec((HALF, 256), lambda i, r: (0, i))
    return pl.pallas_call(
        past(weight_grads_kernel, 11, len(args) - 10),
        grid_spec=pltpu.PrefetchScalarGridSpec(
            num_scalar_prefetch=1,
            grid=(4,),
            in_specs=[
                pl.BlockSpec((2, SEQ, 256), lambda i, r: (0, 0, i)),
                pl.BlockSpec((2, HALF, 512), fixed),
                pl.BlockSpec((2, SEQ, 256), fixed),
                pl.BlockSpec((2, SEQ, 256), fixed),
                column,
                column,
                pl.BlockSpec((2, HALF, 512), fixed),
                pl.BlockSpec((EXPERTS, 256), lambda i, r: (0, i)),
                pl.BlockSpec((1, 256), lambda i, r: (0, i)),
                pl.BlockSpec((8, 256), lambda i, r: (0, 0)),
            ]
            + [HBM] * (len(args) - 10),
            out_specs=[HBM] * 4,
            scratch_shapes=[pltpu.VMEM((N_FSDP, 64, 1664), BF), pltpu.SemaphoreType.DMA((4,))],
        ),
        out_shape=[jax.ShapeDtypeStruct((4, 64, 1664), BF)] * 4,
        compiler_params=params(1),
        cost_estimate=cost(9 * 10**9, 16 * 10**6),
        name="weight_grads",
    )(place, *args)


def input_grads_kernel(gq, gk, gv, w, mine, other):
    part = dot_nt(jnp.concatenate([gk[0], gv[0]], axis=1), w[:, 512:1024])
    own = dot_nt(gq[0], w[:, 0:512])
    for c in range(4):
        for parity, out in enumerate((mine, other)):
            at = slice(c * 256 + parity * 128, c * 256 + parity * 128 + 128)
            value = part[at] + own[at] if c == 0 else part[at]
            out[c] = value.astype(BF)


def input_grads(gq, gk, gv, weights, *others):
    by = lambda s: (s, 0, 0)
    half = pl.BlockSpec((4, 128, D), lambda s: (0, s, 0))
    return pl.pallas_call(
        past(input_grads_kernel, 4, len(others)),
        grid=(2,),
        in_specs=[
            pl.BlockSpec((1, HALF, 512), by),
            pl.BlockSpec((1, SEQ, 256), by),
            pl.BlockSpec((1, SEQ, 256), by),
            pl.BlockSpec((D, 1024), lambda s: (0, 0)),
        ]
        + [HBM] * len(others),
        out_specs=[half, half],
        out_shape=[jax.ShapeDtypeStruct((4, HALF, D), BF)] * 2,
        compiler_params=params(1),
        cost_estimate=cost(6 * 10**9, 12 * 10**6),
        name="input_grads",
    )(gq, gk, gv, weights, *others)


def finish_kernel(own, first, second, third, tokens, grad_hidden, small, out):
    values = tokens[...].astype(F32)
    factor = lax.rsqrt(jnp.mean(values * values, axis=1, keepdims=True) + EPS)
    summed = own[...].astype(F32) + first[...].astype(F32)
    summed = summed + (second[...].astype(F32) + third[...].astype(F32))
    weighted = summed * small[32:33, :]
    mean = jnp.mean(weighted * values, axis=1, keepdims=True)
    out[...] = grad_hidden[...] + factor * weighted - values * (factor * factor * factor * mean)


def finish(*args):
    return pl.pallas_call(
        past(finish_kernel, 7, len(args) - 7),
        in_specs=[pl.BlockSpec(memory_space=pltpu.VMEM)] * 7 + [HBM] * (len(args) - 7),
        out_shape=jax.ShapeDtypeStruct((HALF, D), F32),
        compiler_params=pltpu.CompilerParams(vmem_limit_bytes=VMEM),
        cost_estimate=cost(10**7, 6 * 10**6),
        name="finish",
    )(*args)


def settle_kernel(
    own, first, second, third, w_query, w_key, w_value, gain, g_query, g_key, g_value, g_out, sums
):
    summed = own[...].astype(F32) + first[...].astype(F32)
    summed = summed + (second[...].astype(F32) + third[...].astype(F32))
    g_query[...] = summed[:, 0:512]
    g_key[...] = summed[:, 512:768]
    g_value[...] = summed[:, 768:1024]
    g_out[...] = summed[:, 1024:1536]
    part = jnp.sum(w_query[...].astype(F32) * summed[:, 0:512], axis=1, keepdims=True)
    part = part + jnp.sum(w_key[...].astype(F32) * summed[:, 512:768], axis=1, keepdims=True)
    part = part + jnp.sum(w_value[...].astype(F32) * summed[:, 768:1024], axis=1, keepdims=True)
    diagonal = lax.broadcasted_iota(jnp.int32, (64, 64), 0) == lax.broadcasted_iota(
        jnp.int32, (64, 64), 1
    )
    column = jnp.sum(jnp.where(diagonal, gain[...].astype(F32), 0.0), axis=1, keepdims=True)
    lane = lax.broadcasted_iota(jnp.int32, (64, 128), 1)
    sums[...] = jnp.where(lane == 35, part / column, summed[:, 1536:1664])


def settle(*args):
    return pl.pallas_call(
        past(settle_kernel, 8, len(args) - 8),
        in_specs=[pl.BlockSpec(memory_space=pltpu.VMEM)] * 8 + [HBM] * (len(args) - 8),
        out_shape=[jax.ShapeDtypeStruct((64, n), F32) for n in (512, 256, 256, 512, 128)],
        compiler_params=pltpu.CompilerParams(vmem_limit_bytes=VMEM),
        cost_estimate=cost(10**6, 2 * 10**6),
        name="settle",
    )(*args)


def join_kernel(where, mine, far, out):
    @pl.when(pl.program_id(0) == 0)
    def _():
        out[...] = mine[...].reshape(2, 4, 1, 32, D)

    @pl.when(pl.program_id(0) == 1)
    def _():
        out[...] = far[...].reshape(2, 4, 1, 32, D)


def join(where, mine, far, *others):
    whole = pl.BlockSpec((HALF, D), lambda i, r: (0, 0))
    return pl.pallas_call(
        past(join_kernel, 3, len(others)),
        grid_spec=pltpu.PrefetchScalarGridSpec(
            num_scalar_prefetch=1,
            grid=(2,),
            in_specs=[whole, whole] + [HBM] * len(others),
            out_specs=pl.BlockSpec(
                (2, 4, 1, 32, D), lambda i, r: (0, 0, jnp.where(i == 0, r[0], 1 - r[0]), 0, 0)
            ),
        ),
        out_shape=jax.ShapeDtypeStruct((2, 4, 2, 32, D), mine.dtype),
        compiler_params=params(1),
        cost_estimate=cost(10**6, 4 * 10**6),
        name="join",
    )(where, mine, far, *others).reshape(2, 256, D)


def ring_pairs(stage, step):
    pairs = []
    for x in range(4):
        for z in range(4):
            for t in range(2):
                if (stage == 0) == (t == 0):
                    far = ((x + step) % 4) * 4 + z
                else:
                    far = x * 4 + (z + step) % 4
                pairs.append(((x * 4 + z) * 2 + t, far * 2 + t))
    return pairs


def ring(value, stage, step):
    return lax.ppermute(value, ("fsdp", "tensor"), ring_pairs(stage, step))


def shift(value, step):
    return lax.ppermute(value, "context", [(i, (i + step) % 4) for i in range(4)])


def swap_cores(value):
    return lax.ppermute(value, "tensor", [(0, 1), (1, 0)])


def gather_row(block, stage=0):
    return block, ring(block, stage, -1), ring(block, stage, 1), ring(block, stage, 2)


def gather_chunks(low, high):
    behind_low, ahead_high = ring(low, 1, 1), ring(high, 1, -1)
    behind_high, ahead_low = ring(high, 1, 1), ring(low, 1, -1)
    far = ring(behind_low, 1, 1), ring(ahead_high, 1, -1)
    return (low, high), (ahead_low, ahead_high), (behind_low, behind_high), far


def scatter_parts(parts, move):
    own, ahead, behind, far = parts
    return own, move(ahead, 1), move(behind, -1), move(far, 2)


def total_of(parts):
    first, second, third, fourth = (p.astype(F32) for p in parts)
    return (first + second) + (third + fourth)


def along(stage):
    return lambda v, n: ring(v, stage, n)


def local(
    tokens, segments, routes, attention_gain, w_query, w_key, w_value, w_out, query_gain,
    key_gain, feedforward_gain, router, w_gate, w_up, w_down, cotangent,
):
    f, c, t = lax.axis_index("fsdp"), lax.axis_index("context"), lax.axis_index("tensor")
    x_at, z_at = f // 4, f % 4
    steps = jnp.array([0, 1, 3, 2], jnp.int32)
    as_row = lambda *v: jnp.stack([jnp.asarray(i, jnp.int32) for i in v])
    all_x, all_z = (x_at + steps) % 4, (z_at + steps) % 4
    order = jnp.where(
        t == 0, all_x[None, :] * 4 + all_z[:, None], all_x[:, None] * 4 + all_z[None, :]
    ).astype(jnp.int32)
    far_x, far_z = steps[(jnp.arange(4) - x_at) % 4], steps[(jnp.arange(4) - z_at) % 4]
    place = jnp.where(
        t == 0, far_x[:, None] + 4 * far_z[None, :], 4 * far_x[:, None] + far_z[None, :]
    )
    place = place.reshape(-1).astype(jnp.int32)
    near = ((c + steps) % 4)[:, None] * 2 + jnp.stack([t, 1 - t])[None, :]
    near = near.reshape(8)

    shard = pack(
        as_row(f), w_query, w_key, w_value, w_out, router, attention_gain[None, :],
        feedforward_gain[None, :], query_gain[None, :], key_gain[None, :],
    )
    shards = jnp.stack(gather_row(shard))
    shards = gather_row(shards, 1)

    parity = lambda v, p: lax.dynamic_index_in_dim(
        v.reshape(2, 4, 2, 32, D), p, 2, keepdims=False
    ).reshape(HALF, D)
    tokens_m = parity(tokens, t)
    tokens_all = lax.all_gather(tokens_m, ("context", "tensor"), axis=0)
    picked = routes.reshape(ROWS, TOPK).T
    experts = jnp.arange(EXPERTS, dtype=jnp.int32)
    match = jnp.any(picked[:, None, :] == experts[None, :, None], axis=0)
    before = lambda n: (jnp.arange(n)[:, None] < jnp.arange(n)[None, :]).astype(BF)
    kept = match & (dot(match.astype(BF), before(ROWS)) < CAP)
    half = lambda v: lax.dynamic_index_in_dim(
        v.astype(F32).reshape(EXPERTS, 2, 4, 2, 32), t, 3, keepdims=False
    ).reshape(EXPERTS, HALF)
    match_half, kept_half = half(match), half(kept)
    local_place = dot(kept_half.astype(BF), before(HALF))
    table = experts_to_rows(jnp.where(kept_half > 0, local_place, -1.0).astype(BF))
    cot_payload = pack_cotangent(as_row(t), cotangent, table, *shards[1:])
    cot_row = gather_row(cot_payload)

    packed = jnp.concatenate([w_gate, w_up, w_down], axis=2)
    packed_o = swap_cores(packed)
    seg = segments.reshape(2, 4, 4, 2, 32).transpose(0, 1, 3, 2, 4).reshape(2, 8, 128)
    seg = jnp.take(seg, near, axis=1).reshape(2, 1, SEQ).astype(F32)

    cosine, sine = (jnp.asarray(v) for v in rotary_tables())
    weights, small, heads, cosine, sine, normed1, k_proj, k_b, v_b, q_proj, q_b = project(
        order.reshape(-1), near.astype(jnp.int32), tokens_all, shards, cosine, sine, packed_o, seg
    )
    cot_chunks = gather_chunks(*stack_pairs(cot_row, small))
    attended, branch_m, branch_o = attend(q_b, k_b, v_b, seg, weights, cot_chunks[0][0])
    hidden1, payload, probs, totals = route(
        tokens_m, branch_m, swap_cores(branch_o), small, match_half, kept_half,
        *cot_chunks[1], *cot_chunks[2],
    )

    chunks = gather_chunks(*stack_pairs(gather_row(payload), *cot_chunks[3]))
    outs_x, more, counts, carried = {}, [], [], ()
    for slot, i in enumerate((0, 1, 3, 2)):
        where_at = as_row(f // 4, 2 * (f % 4), slot)
        result = expert_chunk(
            order[i], where_at, chunks[i], cot_chunks[i], packed, packed_o, carried
        )
        carried = result[0], *result[2:5]
        outs_x[i] = result[1]
        more += result[5:8]
        counts.append(result[8])
    parts = scatter_parts([outs_x[i] for i in range(4)], along(1))
    grads_e = expert_weights(as_row(t), carried[1:], more, counts, parts[1], parts[3])
    back, grads_e = add_blocks(parts, (grads_e,))
    back = scatter_parts(back, along(0))

    grads_e = lax.psum_scatter(
        grads_e.reshape(8, 2, 256, 768), ("context", "tensor"), scatter_dimension=0
    )
    mixed, grad_hidden, grad_branch, grad_router, grad_gain2 = route_back(
        [carried[0]], *back, cot_payload, hidden1, small, payload, probs, totals, match_half
    )
    mixed = lax.psum_scatter(mixed, "fsdp", scatter_dimension=0)
    branch_far = swap_cores(grad_branch)
    gq, gk, gv, gains = attend_back(
        q_b, q_proj, k_b, k_proj, v_b, seg,
        grad_branch, branch_far, weights, attended, cosine, sine, heads,
    )
    grads_w = weight_grads(
        place, normed1, gq, gk, gv, grad_branch, branch_far, attended, grad_router, grad_gain2, gains,
    )
    gin_m, gin_o = input_grads(gq, gk, gv, weights, grads_w[0])
    (sent,) = add_blocks((gin_m, swap_cores(gin_o)))
    gin = scatter_parts(sent, shift)
    grad_tokens = finish(*gin, tokens_m, grad_hidden, small, grads_e)

    grads_w = scatter_parts(grads_w, along(1))
    (grads_w,) = add_blocks(grads_w, (), *sent[1:])
    grads_w = [v[None] for v in scatter_parts(grads_w, along(0))]
    ((grads_w,),) = add_blocks(grads_w, (), *gin[1:])
    g_query, g_key, g_value, g_out, sums = settle(
        *scatter_parts([grads_w] * 4, shift), w_query, w_key, w_value, attention_gain[None, :],
        grad_tokens,
    )
    sums = sums + swap_cores(sums)

    both = lambda v, *others: join(as_row(t), v, swap_cores(v), *others)
    block_half = (hidden1 + mixed.astype(F32)).astype(BF)
    grads_e = grads_e.astype(F32)
    return (
        both(block_half, sums),
        both(grad_tokens),
        sums[:, 35],
        g_query,
        g_key,
        g_value,
        g_out,
        sums[0:4, 33],
        sums[0:4, 34],
        sums[:, 32],
        sums[:, 0:32],
        grads_e[:, :, 0:256],
        grads_e[:, :, 256:512],
        grads_e[:, :, 512:768],
    )


def solution(mesh):
    in_specs = (
        P("fsdp", "context", None),
        P("fsdp", None),
        P("fsdp", "context", None),
        P("fsdp"),
        P("fsdp", "tensor"),
        P("fsdp", "tensor"),
        P("fsdp", "tensor"),
        P("fsdp", "tensor"),
        P("fsdp"),
        P("fsdp"),
        P("fsdp"),
        P("fsdp", None),
        P("fsdp", None, "tensor"),
        P("fsdp", None, "tensor"),
        P("fsdp", None, "tensor"),
        P("fsdp", "context", None),
    )
    out_specs = (
        P("fsdp", "context", None),
        P("fsdp", "context", None),
        P("fsdp"),
        P("fsdp", "tensor"),
        P("fsdp", "tensor"),
        P("fsdp", "tensor"),
        P("fsdp", "tensor"),
        P("fsdp"),
        P("fsdp"),
        P("fsdp"),
        P("fsdp", None),
        P("fsdp", "context", "tensor"),
        P("fsdp", "context", "tensor"),
        P("fsdp", "context", "tensor"),
    )
    return jax.shard_map(local, mesh=mesh, in_specs=in_specs, out_specs=out_specs, check_vma=False)
```

time: 1940 us -> 439 us (0.23)
  waiting for transfers between devices: 945 us -> 130 us
  blocking collectives: 433 us -> 0 us
  Pallas kernels: 0 us -> 188 us
  local copies, waits for them, and re-layouts: 199 us -> 22.1 us
  matrix products: 170 us -> 0.35 us
  other arithmetic: 137 us -> 5.57 us
  starting transfers between devices: 29 us -> 70.5 us
    reduce_scatter x9 -> x1, waiting for transfers between devices: 409 us -> 0.01 us  [local(): lax.psum_scatter(grads_e.reshape(8, 2, 256, 768), ('context', 'tensor'),...]
    all_to_all x4 -> x0, waiting for transfers between devices: 406 us -> none  [the longest x2 302 us: to_tokens(): lax.all_to_all(slots, 'fsdp', split_axis=0, concat_axis=0, tiled=True)]
    all_gather x3 -> x0, blocking collectives: 224 us -> none  [the longest x1 188 us: local(): lax.all_gather(router, 'fsdp', axis=0, tiled=True)]
    pallas_call x0 -> x24, Pallas kernels: none -> 188 us  [the longest x4 63.8 us: expert_chunk(): pl.pallas_call(expert_kernel, grid_spec=pltpu.PrefetchScalarGridSpec(num_...]
    dot_general x29 -> x2, matrix products: 167 us -> 0.35 us  [dot(): return jnp.dot(a, b, preferred_element_type=F32)]
    psum x3 -> x0, blocking collectives: 138 us -> none  [the longest x1 119 us: over_hidden(): return lax.psum(partial_sum, 'tensor').astype(jnp.bfloat16)]
    ppermute x0 -> x49, waiting for transfers between devices: none -> 130 us  [the longest x36 127 us: ring(): return lax.ppermute(value, ('fsdp', 'tensor'), ring_pairs(stage, step))]
    all_gather x4 -> x1, waiting for transfers between devices: 83.6 us -> 0.01 us  [local(): tokens_all = lax.all_gather(tokens_m, ('context', 'tensor'), axis=0)]
  transfers between devices with their start and end apart: 21 -> 52, of which waited for: 17 -> 22; matrix products, arithmetic and copies ran while one was open for 16% -> 5% of each run, Pallas kernels for 0% -> 40%
where the time goes in v1:
time: 439 us; the launch traced here: 431 us
  Pallas kernels  188 us (43%)
  waiting for transfers between devices  130 us (30%)
  starting transfers between devices  70.5 us (16%)
  local copies, waits for them, and re-layouts  22.1 us (5%)
  between operations  14.7 us (3%)
  other arithmetic  5.57 us (1%)
    ppermute x36, waiting for transfers between devices, ring(): return lax.ppermute(value, ('fsdp', 'tensor'), ring_pairs(stage, step))  127 us
    pallas_call x4, Pallas kernels, expert_chunk(): pl.pallas_call(expert_kernel, grid_spec=pltpu.PrefetchScalarGridSpec(num_...  63.8 us
    ppermute x36, starting transfers between devices, ring(): return lax.ppermute(value, ('fsdp', 'tensor'), ring_pairs(stage, step))  46.7 us
    pallas_call x1, Pallas kernels, attend_back(): pl.pallas_call(attend_back_kernel, grid=(2, 2), in_specs=[queries, querie...  23 us
    pallas_call x1, Pallas kernels, expert_weights(): pl.pallas_call(expert_weight_kernel, grid_spec=pltpu.PrefetchScalarGridSp...  18.5 us
    pallas_call x4, Pallas kernels, add_blocks(): pl.pallas_call(kernel, in_specs=[vmem] * n + [HBM] * (k + len(others)), o...  14.3 us
    ppermute x7, starting transfers between devices, swap_cores(): return lax.ppermute(value, 'tensor', [(0, 1), (1, 0)])  13.5 us
    pallas_call x1, Pallas kernels, project(): pl.pallas_call(past(project_kernel, 16, len(others)), grid_spec=pltpu.Pre...  13.4 us
  transfers between devices with their start and end apart: 52, of which 22 were waited for; matrix products, arithmetic and copies ran while one was open for 5% of the time, Pallas kernels for 40%

profile of v1, /device:TPU:1, one launch (start us, length us, event | category | flops | bytes accessed | tf_op | source)
XLA Modules:
  0.0 431.3 jit_solution(16259171642577068365)
XLA Ops:
  17.8 3.7 collective-permute-start.2
  36.8 6.1 %collective-permute-done.5.refs_13_.refs_5_ = bf16[4,64,1664]{2,1,0:T(8,128)(2,1)S(1)} collective-permute-done((bf16[4,64,1664]{2,1,0:T(8,128)(2,1)S(1)}, bf16[4,64,1664]{2,1,0:T(8,128)(2,1)S(1)}, u32[]{:S(2)}, u32[]{:S(2)}) %collective-permute-start.5) | collective-permute-done | bytes 852000 | tf_op jit(solution)/shard_map/ppermute | solution.py:1055
  42.9 9.1 %collective-permute-done.4.refs_12_.refs_4_ = bf16[4,64,1664]{2,1,0:T(8,128)(2,1)S(1)} collective-permute-done((bf16[4,64,1664]{2,1,0:T(8,128)(2,1)S(1)}, bf16[4,64,1664]{2,1,0:T(8,128)(2,1)S(1)}, u32[]{:S(2)}, u32[]{:S(2)}) %collective-permute-start.4) | collective-permute-done | bytes 852000 | tf_op jit(solution)/shard_map/ppermute | solution.py:1055
  59.0 13.4 %project.1 = (bf16[1024,1664]{1,0:T(8,128)(2,1)}, f32[128,1024]{1,0:T(8,128)}, f32[8,128]{1,0:T(8,128)}, f32[1024,128]{1,0:T(8,128)}, f32[1024,128]{1,0:T(8,128)...) custom-call(s32[16]{0:T(128)} %select_n.145.refs_0_, ...), custom_call_target="tpu_custom_call" | custom-call | flops 10000000000 | bytes 20000000 | tf_op jit(solution)/shard_map/project/pallas_call | solution.py:253
  73.3 3.0 stack_pairs.2
  81.8 10.2 %attend.1 = (bf16[2,256,512]{2,1,0:T(8,128)(2,1)}, f32[256,1024]{1,0:T(8,128)}, f32[256,1024]{1,0:T(8,128)}) custom-call(bf16[2,256,512]{2,1,0:T(8,128)(2,1)} %get-tuple-element.105.refs_0_.q, bf16[2,1024,256]{2,1,0:T(8,128)(2,1)} %get-tuple-element.106.refs_1_.k, bf16[2,1024,256]{2,1,0:T(8,128)(2,1)} %get-tuple-element.107.refs_2_.v, ...), custom_call_target="tpu_custom_call" | custom-call | flops 10000000000 | bytes 8000000 | tf_op jit(solution)/shard_map/attend/pallas_call | solution.py:325
  92.1 3.2 collective-permute-start.10
  96.3 8.1 %collective-permute-done.13.refs_8_.c_low = bf16[2,272,1024]{2,1,0:T(8,128)(2,1)} collective-permute-done((bf16[2,272,1024]{2,1,0:T(8,128)(2,1)}, bf16[2,272,1024]{2,1,0:T(8,128)(2,1)}, u32[]{:S(2)}, u32[]{:S(2)}) %collective-permute-start.13) | collective-permute-done | bytes 1114144 | tf_op jit(solution)/shard_map/ppermute | solution.py:1055
  106.0 3.2 route.1
  114.0 11.5 %collective-permute-done.17.refs_3_ = bf16[272,1024]{1,0:T(8,128)(2,1)S(1)} collective-permute-done((bf16[272,1024]{1,0:T(8,128)(2,1)}, bf16[272,1024]{1,0:T(8,128)(2,1)S(1)}, u32[]{:S(2)}, u32[]{:S(2)}) %collective-permute-start.17) | collective-permute-done | bytes 557088 | tf_op jit(solution)/shard_map/ppermute | solution.py:1055
  125.5 7.4 %collective-permute-done.16.refs_2_ = bf16[272,1024]{1,0:T(8,128)(2,1)S(1)} collective-permute-done((bf16[272,1024]{1,0:T(8,128)(2,1)}, bf16[272,1024]{1,0:T(8,128)(2,1)S(1)}, u32[]{:S(2)}, u32[]{:S(2)}) %collective-permute-start.16) | collective-permute-done | bytes 557088 | tf_op jit(solution)/shard_map/ppermute | solution.py:1055
  140.5 14.6 %experts.4 = (bf16[16,256,1024]{2,1,0:T(8,128)(2,1)}, bf16[4,272,1024]{2,1,0:T(8,128)(2,1)}, bf16[2,1536,1024]{2,1,0:T(8,128)(2,1)}, bf16[2,1536,1024]{2,1,0:T(8...) custom-call(s32[4]{0:T(128)} %get-tuple-element.265.order, ...), custom_call_target="tpu_custom_call" | custom-call | flops 14000000000 | bytes 30000000 | tf_op jit(solution)/shard_map/experts/pallas_call | solution.py:592
  155.2 8.4 %collective-permute-done.23.x_high = bf16[2,272,1024]{2,1,0:T(8,128)(2,1)} collective-permute-done((bf16[2,272,1024]{2,1,0:T(8,128)(2,1)}, bf16[2,272,1024]{2,1,0:T(8,128)(2,1)}, u32[]{:S(2)}, u32[]{:S(2)}) %collective-permute-start.23) | collective-permute-done | bytes 1114144 | tf_op jit(solution)/shard_map/ppermute | solution.py:1055
  165.9 14.3 %experts.5 = (bf16[16,256,1024]{2,1,0:T(8,128)(2,1)}, bf16[4,272,1024]{2,1,0:T(8,128)(2,1)}, bf16[2,1536,1024]{2,1,0:T(8,128)(2,1)}, bf16[2,1536,1024]{2,1,0:T(8...) custom-call(s32[4]{0:T(128)} %get-tuple-element.266.order, ...), custom_call_target="tpu_custom_call", output_to_operand_aliasing={{0}: (8, {}), {2}: (9, {}), {3}: (10, {}), {4}: (11, {})} | custom-call | flops 14000000000 | bytes 30000000 | tf_op jit(solution)/shard_map/experts/pallas_call | solution.py:592
  180.4 20.6 %experts.6 = (bf16[16,256,1024]{2,1,0:T(8,128)(2,1)}, bf16[4,272,1024]{2,1,0:T(8,128)(2,1)}, bf16[2,1536,1024]{2,1,0:T(8,128)(2,1)}, bf16[2,1536,1024]{2,1,0:T(8...) custom-call(s32[4]{0:T(128)} %get-tuple-element.267.order, ...), custom_call_target="tpu_custom_call", output_to_operand_aliasing={{0}: (8, {}), {2}: (9, {}), {3}: (10, {}), {4}: (11, {})} | custom-call | flops 14000000000 | bytes 30000000 | tf_op jit(solution)/shard_map/experts/pallas_call | solution.py:592
  202.2 14.3 %experts.7 = (bf16[16,256,1024]{2,1,0:T(8,128)(2,1)}, bf16[4,272,1024]{2,1,0:T(8,128)(2,1)}, bf16[2,1536,1024]{2,1,0:T(8,128)(2,1)}, bf16[2,1536,1024]{2,1,0:T(8...) custom-call(s32[4]{0:T(128)} %get-tuple-element.268.order, ...), custom_call_target="tpu_custom_call", output_to_operand_aliasing={{0}: (8, {}), {2}: (9, {}), {3}: (10, {}), {4}: (11, {})} | custom-call | flops 14000000000 | bytes 30000000 | tf_op jit(solution)/shard_map/experts/pallas_call | solution.py:592
  218.3 14.0 %collective-permute-done.26.refs_16_.refs_1_ = bf16[4,272,1024]{2,1,0:T(8,128)(2,1)} collective-permute-done((bf16[4,272,1024]{2,1,0:T(8,128)(2,1)}, bf16[4,272,1024]{2,1,0:T(8,128)(2,1)}, u32[]{:S(2)}, u32[]{:S(2)}) %collective-permute-start.26) | collective-permute-done | bytes 2228256 | tf_op jit(solution)/shard_map/ppermute | solution.py:1055
  232.3 18.5 %expert_weights.1.refs_4_ = bf16[4,2,2,256,768]{4,3,2,1,0:T(8,128)(2,1)} custom-call(s32[1]{0:T(128)} %bitcast.refs_0_.place, bf16[2,1536,1024]{2,1,0:T(8,128)(2,1)} %get-tuple-element.135.x, bf16[2,1536,1024]{2,1,0:T(8,128)(2,1)} %get-tuple-element.136.g, bf16[2,1536,1536]{2,1,0:T(8,128)(2,1)} %get-tuple-element.137.act.grad, ...), custom_call_target="tpu_custom_call" | custom-call | flops 20000000000 | bytes 30000000 | tf_op jit(solution)/shard_map/expert_weights/pallas_call | solution.py:670
  253.7 5.5 %add_blocks.4 = (bf16[272,1024]{1,0:T(8,128)(2,1)}, bf16[272,1024]{1,0:T(8,128)(2,1)}, bf16[272,1024]{1,0:T(8,128)(2,1)}, bf16[272,1024]{1,0:T(8,128)(2,1)}, bf16[4,2,2,256,768]{4,3,2,1,0:T(8,128)(2,1)}) custom-call(bf16[4,272,1024]{2,1,0:T(8,128)(2,1)} %get-tuple-element.131.refs_0_, ...), custom_call_target="tpu_custom_call", output_to_operand_aliasing={{4}: (4, {})} | custom-call | flops 1000000000 | bytes 10000000 | tf_op jit(solution)/shard_map/add_blocks/pallas_call | solution.py:165
  263.4 6.0 %collective-permute-done.29.refs_2_ = bf16[272,1024]{1,0:T(8,128)(2,1)S(1)} collective-permute-done((bf16[272,1024]{1,0:T(8,128)(2,1)}, bf16[272,1024]{1,0:T(8,128)(2,1)S(1)}, u32[]{:S(2)}, u32[]{:S(2)}) %collective-permute-start.29) | collective-permute-done | bytes 557088 | tf_op jit(solution)/shard_map/ppermute | solution.py:1055
  269.4 5.7 %collective-permute-done.30.refs_3_ = bf16[272,1024]{1,0:T(8,128)(2,1)S(1)} collective-permute-done((bf16[272,1024]{1,0:T(8,128)(2,1)S(1)}, bf16[272,1024]{1,0:T(8,128)(2,1)S(1)}, u32[]{:S(2)}, u32[]{:S(2)}) %collective-permute-start.30) | collective-permute-done | bytes 557088 | tf_op jit(solution)/shard_map/ppermute | solution.py:1055
  277.2 4.8 %route_back.1 = (bf16[16,256,1024]{2,1,0:T(8,128)(2,1)}, f32[256,1024]{1,0:T(8,128)}, bf16[256,1024]{1,0:T(8,128)(2,1)}, f32[32,1024]{1,0:T(8,128)}, f32[1,1024]{1,0:T(1,128)}) custom-call(bf16[16,256,1024]{2,1,0:T(8,128)(2,1)} %get-tuple-element.130.refs_0_, bf16[272,1024]{1,0:T(8,128)(2,1)} %get-tuple-element.154.refs_1_, ...), custom_call_target="tpu_custom_call", output_to_operand_aliasing={{0}: (0, {})} | custom-call | flops 4000000000 | bytes 6000000 | tf_op jit(solution)/shard_map/route_back/pallas_call | solution.py:734
  283.1 4.4 %collective-permute-start.33 = (bf16[256,1024]{1,0:T(8,128)(2,1)S(1)}, bf16[256,1024]{1,0:T(8,128)(2,1)S(1)}, u32[]{:S(2)}, u32[]{:S(2)}) collective-permute-start(bf16[256,1024]{1,0:T(8,128)(2,1)S(1)} %copy-done.30), channel_id=1, source_target_pairs={{0,1},{1,0},{2,3},{3,2},{4,5},{5,4},{6,7},{7,6},{8,9},{9,8},{10,11... | collective-permute-start | bytes 1572872 | tf_op jit(solution)/shard_map/ppermute | solution.py:1063
  289.7 23.0 %attend_back.1 = (bf16[2,256,512]{2,1,0:T(8,128)(2,1)}, bf16[2,1024,256]{2,1,0:T(8,128)(2,1)}, bf16[2,1024,256]{2,1,0:T(8,128)(2,1)}, f32[8,256]{1,0:T(8,128)}) custom-call(bf16[2,256,512]{2,1,0:T(8,128)(2,1)} %get-tuple-element.105.refs_0_.q, f32[2,256,512]{2,1,0:T(8,128)} %get-tuple-element.162.q_proj, bf16[2,1024,256]{2,1,0:T(8,128)(2,1)} %get-tuple-element.106.refs_1_.k, ...), custom_call_target="tpu_custom_call" | custom-call | flops 17999998976 | bytes 16000000 | tf_op jit(solution)/shard_map/attend_back/pallas_call | solution.py:820
  312.7 9.4 %weight_grads.1 = (bf16[4,64,1664]{2,1,0:T(8,128)(2,1)}, bf16[4,64,1664]{2,1,0:T(8,128)(2,1)}, bf16[4,64,1664]{2,1,0:T(8,128)(2,1)}, bf16[4,64,1664]{2,1,0:T(8,128)(2,1)}) custom-call(s32[16]{0:T(128)} %select_n.156.refs_0_, bf16[2,1024,1024]{2,1,0:T(8,128)(2,1)} %get-tuple-element.161.refs_1_, bf16[2,256,512]{2,1,0:T(8,128)(2,1)} %get-tuple-element.169.refs_2_.refs_0_, ...), custom_call_target="tpu_custom_call" | custom-call | flops 8999999488 | bytes 16000000 | tf_op jit(solution)/shard_map/weight_grads/pallas_call | solution.py:901
  322.2 6.8 %input_grads.1 = (bf16[4,256,1024]{2,1,0:T(8,128)(2,1)}, bf16[4,256,1024]{2,1,0:T(8,128)(2,1)}) custom-call(bf16[2,256,512]{2,1,0:T(8,128)(2,1)} %get-tuple-element.169.refs_2_.refs_0_, bf16[2,1024,256]{2,1,0:T(8,128)(2,1)} %get-tuple-element.170.refs_3_.refs_1_, bf16[2,1024,256]{2,1,0:T(8,128)(2,1)} %get-tuple-element.171.refs_4_.refs_2_, ...), custom_call_target="tpu_custom_call" | custom-call | flops 6000000000 | bytes 12000000 | tf_op jit(solution)/shard_map/input_grads/pallas_call | solution.py:942
  333.5 3.7 add_blocks.5
  339.9 19.4 %collective-permute-done.34.refs_1_ = bf16[4,64,1664]{2,1,0:T(8,128)(2,1)S(1)} collective-permute-done((bf16[4,64,1664]{2,1,0:T(8,128)(2,1)}, bf16[4,64,1664]{2,1,0:T(8,128)(2,1)S(1)}, u32[]{:S(2)}, u32[]{:S(2)}) %collective-permute-start.34) | collective-permute-done | bytes 852000 | tf_op jit(solution)/shard_map/ppermute | solution.py:1055
  362.2 13.4 %collective-permute-done.36.refs_3_ = bf16[4,64,1664]{2,1,0:T(8,128)(2,1)} collective-permute-done((bf16[4,64,1664]{2,1,0:T(8,128)(2,1)}, bf16[4,64,1664]{2,1,0:T(8,128)(2,1)}, u32[]{:S(2)}, u32[]{:S(2)}) %collective-permute-start.36) | collective-permute-done | bytes 852000 | tf_op jit(solution)/shard_map/ppermute | solution.py:1055
  381.3 3.7 collective-permute-done.38
  385.4 8.3 %collective-permute-done.40 = bf16[64,1664]{1,0:T(8,128)(2,1)S(1)} collective-permute-done((bf16[64,1664]{1,0:T(8,128)(2,1)}, bf16[64,1664]{1,0:T(8,128)(2,1)S(1)}, u32[]{:S(2)}, u32[]{:S(2)}) %collective-permute-start.40) | collective-permute-done | bytes 213024 | tf_op jit(solution)/shard_map/ppermute | solution.py:1055
  401.1 3.7 finish.1.refs_8_.refs_1_
  (224 shorter events, 115.3 us)
Async XLA Ops:
  7.2 51.8 %all-gather.2.cloned.1.call-start = ((), (), s32[]{:S(2)}) async-start(), calls=%async_computation.2 | async-start | bytes 4718592 | tf_op jit(solution)/shard_map/all_gather | solution.py:1122
  9.3 391.8 %reduce-scatter.5.cloned.1.call-start = ((), (), s32[]{:S(2)}) async-start(), calls=%async_computation.3 | async-start | bytes 7077888 | tf_op jit(solution)/shard_map/reduce_scatter | solution.py:1169
  13.9 45.1 %collective-permute-start.6 = (bf16[2,1024,768]{2,1,0:T(8,128)(2,1)}, bf16[2,1024,768]{2,1,0:T(8,128)(2,1)}, u32[]{:S(2)}, u32[]{:S(2)}) collective-permute-start(bf16[2,1024,768]{2,1,0:T(8,128)(2,1)} %constant_dynamic-update-slice_fusion.w_m), channel_id=1, source_target_pairs={{0,1},{1,0},{2,3},{3,2},{4,5},{5,4},{6,7},{7,6},{8,9},{9,8},{10,11... | collective-permute-start | bytes 9437192 | tf_op jit(solution)/shard_map/ppermute | solution.py:1063
  32.2 19.7 %collective-permute-start.4 = (bf16[4,64,1664]{2,1,0:T(8,128)(2,1)S(1)}, bf16[4,64,1664]{2,1,0:T(8,128)(2,1)S(1)}, u32[]{:S(2)}, u32[]{:S(2)}) collective-permute-start(bf16[4,64,1664]{2,1,0:T(8,128)(2,1)S(1)} %pad_maximum_fusion.refs_10_), channel_id=1, source_target_pairs={{0,8},{1,33},{8,16},{9,41},{16,24},{17,49},{24,0},{25,57},{32,40},... | collective-permute-start | bytes 2555912 | tf_op jit(solution)/shard_map/ppermute | solution.py:1055
  32.6 19.6 %collective-permute-start.3 = (bf16[4,64,1664]{2,1,0:T(8,128)(2,1)S(1)}, bf16[4,64,1664]{2,1,0:T(8,128)(2,1)}, u32[]{:S(2)}, u32[]{:S(2)}) collective-permute-start(bf16[4,64,1664]{2,1,0:T(8,128)(2,1)S(1)} %pad_maximum_fusion.refs_10_), channel_id=1, source_target_pairs={{0,24},{1,97},{8,0},{9,105},{16,8},{17,113},{24,16},{25,121},{32,5... | collective-permute-start | bytes 2555912 | tf_op jit(solution)/shard_map/ppermute | solution.py:1055
  54.8 17.6 %collective-permute-start.9 = (bf16[272,1024]{1,0:T(8,128)(2,1)}, bf16[272,1024]{1,0:T(8,128)(2,1)S(1)}, u32[]{:S(2)}, u32[]{:S(2)}) collective-permute-start(bf16[272,1024]{1,0:T(8,128)(2,1)} %pack_cotangent.1.refs_0_.refs_5_), channel_id=1, source_target_pairs={{0,64},{1,17},{8,72},{9,25},{16,80},{17,1},{24,88},{25,9},{32,96},... | collective-permute-start | bytes 1671176 | tf_op jit(solution)/shard_map/ppermute | solution.py:1055
  56.3 16.1 %collective-permute-start.8 = (bf16[272,1024]{1,0:T(8,128)(2,1)}, bf16[272,1024]{1,0:T(8,128)(2,1)}, u32[]{:S(2)}, u32[]{:S(2)}) collective-permute-start(bf16[272,1024]{1,0:T(8,128)(2,1)} %pack_cotangent.1.refs_0_.refs_5_), channel_id=1, source_target_pairs={{0,32},{1,9},{8,40},{9,17},{16,48},{17,25},{24,56},{25,1},{32,64},... | collective-permute-start | bytes 1671176 | tf_op jit(solution)/shard_map/ppermute | solution.py:1055
  76.3 29.7 %collective-permute-start.14 = (bf16[2,272,1024]{2,1,0:T(8,128)(2,1)}, bf16[2,272,1024]{2,1,0:T(8,128)(2,1)}, u32[]{:S(2)}, u32[]{:S(2)}) collective-permute-start(bf16[2,272,1024]{2,1,0:T(8,128)(2,1)} %get-tuple-element.113.c_high), channel_id=1, source_target_pairs={{0,8},{1,33},{8,16},{9,41},{16,24},{17,49},{24,0},{25,57},{32,40},... | collective-permute-start | bytes 3342344 | tf_op jit(solution)/shard_map/ppermute | solution.py:1055
  78.0 17.2 %collective-permute-start.12 = (bf16[2,272,1024]{2,1,0:T(8,128)(2,1)}, bf16[2,272,1024]{2,1,0:T(8,128)(2,1)}, u32[]{:S(2)}, u32[]{:S(2)}) collective-permute-start(bf16[2,272,1024]{2,1,0:T(8,128)(2,1)} %get-tuple-element.113.c_high), channel_id=1, source_target_pairs={{0,24},{1,97},{8,0},{9,105},{16,8},{17,113},{24,16},{25,121},{32,5... | collective-permute-start | bytes 3342344 | tf_op jit(solution)/shard_map/ppermute | solution.py:1055
  79.0 25.4 %collective-permute-start.13 = (bf16[2,272,1024]{2,1,0:T(8,128)(2,1)}, bf16[2,272,1024]{2,1,0:T(8,128)(2,1)}, u32[]{:S(2)}, u32[]{:S(2)}) collective-permute-start(bf16[2,272,1024]{2,1,0:T(8,128)(2,1)} %get-tuple-element.110.refs_5_.c_low), channel_id=1, source_target_pairs={{0,8},{1,33},{8,16},{9,41},{16,24},{17,49},{24,0},{25,57},{32,40},... | collective-permute-start | bytes 3342344 | tf_op jit(solution)/shard_map/ppermute | solution.py:1055
  79.5 26.6 %collective-permute-start.11 = (bf16[2,272,1024]{2,1,0:T(8,128)(2,1)}, bf16[2,272,1024]{2,1,0:T(8,128)(2,1)}, u32[]{:S(2)}, u32[]{:S(2)}) collective-permute-start(bf16[2,272,1024]{2,1,0:T(8,128)(2,1)} %get-tuple-element.110.refs_5_.c_low), channel_id=1, source_target_pairs={{0,24},{1,97},{8,0},{9,105},{16,8},{17,113},{24,16},{25,121},{32,5... | collective-permute-start | bytes 3342344 | tf_op jit(solution)/shard_map/ppermute | solution.py:1055
  95.2 37.6 %collective-permute-start.19 = (bf16[2,272,1024]{2,1,0:T(8,128)(2,1)}, bf16[2,272,1024]{2,1,0:T(8,128)(2,1)}, u32[]{:S(2)}, u32[]{:S(2)}) collective-permute-start(bf16[2,272,1024]{2,1,0:T(8,128)(2,1)} %collective-permute-done.12.refs_7_.c_high), channel_id=1, source_target_pairs={{0,24},{1,97},{8,0},{9,105},{16,8},{17,113},{24,16},{25,121},{32,5... | collective-permute-start | bytes 3342344 | tf_op jit(solution)/shard_map/ppermute | solution.py:1055
  104.4 28.4 %collective-permute-start.18 = (bf16[2,272,1024]{2,1,0:T(8,128)(2,1)}, bf16[2,272,1024]{2,1,0:T(8,128)(2,1)}, u32[]{:S(2)}, u32[]{:S(2)}) collective-permute-start(bf16[2,272,1024]{2,1,0:T(8,128)(2,1)} %collective-permute-done.13.refs_8_.c_low), channel_id=1, source_target_pairs={{0,8},{1,33},{8,16},{9,41},{16,24},{17,49},{24,0},{25,57},{32,40},... | collective-permute-start | bytes 3342344 | tf_op jit(solution)/shard_map/ppermute | solution.py:1055
  109.2 16.2 %collective-permute-start.17 = (bf16[272,1024]{1,0:T(8,128)(2,1)}, bf16[272,1024]{1,0:T(8,128)(2,1)S(1)}, u32[]{:S(2)}, u32[]{:S(2)}) collective-permute-start(bf16[272,1024]{1,0:T(8,128)(2,1)} %get-tuple-element.115.refs_0_.refs_8_), channel_id=1, source_target_pairs={{0,64},{1,17},{8,72},{9,25},{16,80},{17,1},{24,88},{25,9},{32,96},... | collective-permute-start | bytes 1671176 | tf_op jit(solution)/shard_map/ppermute | solution.py:1055
  109.5 23.3 %collective-permute-start.16 = (bf16[272,1024]{1,0:T(8,128)(2,1)}, bf16[272,1024]{1,0:T(8,128)(2,1)S(1)}, u32[]{:S(2)}, u32[]{:S(2)}) collective-permute-start(bf16[272,1024]{1,0:T(8,128)(2,1)} %get-tuple-element.115.refs_0_.refs_8_), channel_id=1, source_target_pairs={{0,32},{1,9},{8,40},{9,17},{16,48},{17,25},{24,56},{25,1},{32,64},... | collective-permute-start | bytes 1671176 | tf_op jit(solution)/shard_map/ppermute | solution.py:1055
  110.0 22.9 %collective-permute-start.15 = (bf16[272,1024]{1,0:T(8,128)(2,1)}, bf16[272,1024]{1,0:T(8,128)(2,1)}, u32[]{:S(2)}, u32[]{:S(2)}) collective-permute-start(bf16[272,1024]{1,0:T(8,128)(2,1)} %get-tuple-element.115.refs_0_.refs_8_), channel_id=1, source_target_pairs={{0,96},{1,25},{8,104},{9,1},{16,112},{17,9},{24,120},{25,17},{32,0... | collective-permute-start | bytes 1671176 | tf_op jit(solution)/shard_map/ppermute | solution.py:1055
  136.6 29.3 %collective-permute-start.25 = (bf16[2,272,1024]{2,1,0:T(8,128)(2,1)}, bf16[2,272,1024]{2,1,0:T(8,128)(2,1)}, u32[]{:S(2)}, u32[]{:S(2)}) collective-permute-start(bf16[2,272,1024]{2,1,0:T(8,128)(2,1)} %get-tuple-element.116.x_low), channel_id=1, source_target_pairs={{0,24},{1,97},{8,0},{9,105},{16,8},{17,113},{24,16},{25,121},{32,5... | collective-permute-start | bytes 3342344 | tf_op jit(solution)/shard_map/ppermute | solution.py:1055
  137.8 17.2 %collective-permute-start.20 = (bf16[2,272,1024]{2,1,0:T(8,128)(2,1)}, bf16[2,272,1024]{2,1,0:T(8,128)(2,1)}, u32[]{:S(2)}, u32[]{:S(2)}) collective-permute-start(bf16[2,272,1024]{2,1,0:T(8,128)(2,1)} %get-tuple-element.116.x_low), channel_id=1, source_target_pairs={{0,8},{1,33},{8,16},{9,41},{16,24},{17,49},{24,0},{25,57},{32,40},... | collective-permute-start | bytes 3342344 | tf_op jit(solution)/shard_map/ppermute | solution.py:1055
  138.1 25.4 %collective-permute-start.23 = (bf16[2,272,1024]{2,1,0:T(8,128)(2,1)}, bf16[2,272,1024]{2,1,0:T(8,128)(2,1)}, u32[]{:S(2)}, u32[]{:S(2)}) collective-permute-start(bf16[2,272,1024]{2,1,0:T(8,128)(2,1)} %get-tuple-element.117.x_high), channel_id=1, source_target_pairs={{0,24},{1,97},{8,0},{9,105},{16,8},{17,113},{24,16},{25,121},{32,5... | collective-permute-start | bytes 3342344 | tf_op jit(solution)/shard_map/ppermute | solution.py:1055
  140.5 61.7 %collective-permute-start.21 = (bf16[2,272,1024]{2,1,0:T(8,128)(2,1)}, bf16[2,272,1024]{2,1,0:T(8,128)(2,1)}, u32[]{:S(2)}, u32[]{:S(2)}) collective-permute-start(bf16[2,272,1024]{2,1,0:T(8,128)(2,1)} %get-tuple-element.117.x_high), channel_id=1, source_target_pairs={{0,8},{1,33},{8,16},{9,41},{16,24},{17,49},{24,0},{25,57},{32,40},... | collective-permute-start | bytes 3342344 | tf_op jit(solution)/shard_map/ppermute | solution.py:1055
  155.1 25.3 %collective-permute-start.22 = (bf16[2,272,1024]{2,1,0:T(8,128)(2,1)}, bf16[2,272,1024]{2,1,0:T(8,128)(2,1)}, u32[]{:S(2)}, u32[]{:S(2)}) collective-permute-start(bf16[2,272,1024]{2,1,0:T(8,128)(2,1)} %collective-permute-done.20.x_low), channel_id=1, source_target_pairs={{0,8},{1,33},{8,16},{9,41},{16,24},{17,49},{24,0},{25,57},{32,40},... | collective-permute-start | bytes 3342344 | tf_op jit(solution)/shard_map/ppermute | solution.py:1055
  163.5 16.8 %collective-permute-start.24 = (bf16[2,272,1024]{2,1,0:T(8,128)(2,1)}, bf16[2,272,1024]{2,1,0:T(8,128)(2,1)}, u32[]{:S(2)}, u32[]{:S(2)}) collective-permute-start(bf16[2,272,1024]{2,1,0:T(8,128)(2,1)} %collective-permute-done.23.x_high), channel_id=1, source_target_pairs={{0,24},{1,97},{8,0},{9,105},{16,8},{17,113},{24,16},{25,121},{32,5... | collective-permute-start | bytes 3342344 | tf_op jit(solution)/shard_map/ppermute | solution.py:1055
  180.3 52.1 %collective-permute-start.26 = (bf16[4,272,1024]{2,1,0:T(8,128)(2,1)}, bf16[4,272,1024]{2,1,0:T(8,128)(2,1)}, u32[]{:S(2)}, u32[]{:S(2)}) collective-permute-start(bf16[4,272,1024]{2,1,0:T(8,128)(2,1)} %get-tuple-element.132), channel_id=1, source_target_pairs={{0,8},{1,33},{8,16},{9,41},{16,24},{17,49},{24,0},{25,57},{32,40},... | collective-permute-start | bytes 6684680 | tf_op jit(solution)/shard_map/ppermute | solution.py:1055
  201.0 31.3 %collective-permute-start.28 = (bf16[4,272,1024]{2,1,0:T(8,128)(2,1)}, bf16[4,272,1024]{2,1,0:T(8,128)(2,1)}, u32[]{:S(2)}, u32[]{:S(2)}) collective-permute-start(bf16[4,272,1024]{2,1,0:T(8,128)(2,1)} %get-tuple-element.134), channel_id=1, source_target_pairs={{0,16},{1,65},{8,24},{9,73},{16,0},{17,81},{24,8},{25,89},{32,48},... | collective-permute-start | bytes 6684680 | tf_op jit(solution)/shard_map/ppermute | solution.py:1055
  216.6 37.1 %collective-permute-start.27 = (bf16[4,272,1024]{2,1,0:T(8,128)(2,1)}, bf16[4,272,1024]{2,1,0:T(8,128)(2,1)}, u32[]{:S(2)}, u32[]{:S(2)}) collective-permute-start(bf16[4,272,1024]{2,1,0:T(8,128)(2,1)} %get-tuple-element.133), channel_id=1, source_target_pairs={{0,24},{1,97},{8,0},{9,105},{16,8},{17,113},{24,16},{25,121},{32,5... | collective-permute-start | bytes 6684680 | tf_op jit(solution)/shard_map/ppermute | solution.py:1055
  259.2 154.8 %reduce-scatter.7.cloned.1.call-start = ((), (), s32[]{:S(2)}) async-start(), calls=%async_computation.4 | async-start | bytes 8912896
  329.3 29.9 %collective-permute-start.34 = (bf16[4,64,1664]{2,1,0:T(8,128)(2,1)}, bf16[4,64,1664]{2,1,0:T(8,128)(2,1)S(1)}, u32[]{:S(2)}, u32[]{:S(2)}) collective-permute-start(bf16[4,64,1664]{2,1,0:T(8,128)(2,1)} %get-tuple-element.176), channel_id=1, source_target_pairs={{0,8},{1,33},{8,16},{9,41},{16,24},{17,49},{24,0},{25,57},{32,40},... | collective-permute-start | bytes 2555912 | tf_op jit(solution)/shard_map/ppermute | solution.py:1055
  329.3 32.8 %collective-permute-start.35 = (bf16[4,64,1664]{2,1,0:T(8,128)(2,1)}, bf16[4,64,1664]{2,1,0:T(8,128)(2,1)S(1)}, u32[]{:S(2)}, u32[]{:S(2)}) collective-permute-start(bf16[4,64,1664]{2,1,0:T(8,128)(2,1)} %get-tuple-element.177), channel_id=1, source_target_pairs={{0,24},{1,97},{8,0},{9,105},{16,8},{17,113},{24,16},{25,121},{32,5... | collective-permute-start | bytes 2555912 | tf_op jit(solution)/shard_map/ppermute | solution.py:1055
  332.1 43.4 %collective-permute-start.36 = (bf16[4,64,1664]{2,1,0:T(8,128)(2,1)}, bf16[4,64,1664]{2,1,0:T(8,128)(2,1)}, u32[]{:S(2)}, u32[]{:S(2)}) collective-permute-start(bf16[4,64,1664]{2,1,0:T(8,128)(2,1)} %get-tuple-element.178), channel_id=1, source_target_pairs={{0,16},{1,65},{8,24},{9,73},{16,0},{17,81},{24,8},{25,89},{32,48},... | collective-permute-start | bytes 2555912 | tf_op jit(solution)/shard_map/ppermute | solution.py:1055
  337.2 56.6 %collective-permute-start.41 = (bf16[256,1024]{1,0:T(8,128)(2,1)}, bf16[256,1024]{1,0:T(8,128)(2,1)}, u32[]{:S(2)}, u32[]{:S(2)}) collective-permute-start(bf16[256,1024]{1,0:T(8,128)(2,1)} %get-tuple-element.181.refs_4_), channel_id=1, source_target_pairs={{0,2},{2,4},{4,6},{6,0},{1,3},{3,5},{5,7},{7,1},{8,10},{10,12},{12... | collective-permute-start | bytes 1572872 | tf_op jit(solution)/shard_map/ppermute | solution.py:1059
  338.5 55.3 %collective-permute-start.42 = (bf16[256,1024]{1,0:T(8,128)(2,1)}, bf16[256,1024]{1,0:T(8,128)(2,1)}, u32[]{:S(2)}, u32[]{:S(2)}) collective-permute-start(bf16[256,1024]{1,0:T(8,128)(2,1)} %get-tuple-element.182.refs_5_), channel_id=1, source_target_pairs={{0,6},{2,0},{4,2},{6,4},{1,7},{3,1},{5,3},{7,5},{8,14},{10,8},{12,... | collective-permute-start | bytes 1572872 | tf_op jit(solution)/shard_map/ppermute | solution.py:1059
  359.3 34.5 %collective-permute-start.43 = (bf16[256,1024]{1,0:T(8,128)(2,1)}, bf16[256,1024]{1,0:T(8,128)(2,1)}, u32[]{:S(2)}, u32[]{:S(2)}) collective-permute-start(bf16[256,1024]{1,0:T(8,128)(2,1)} %get-tuple-element.183.refs_6_), channel_id=1, source_target_pairs={{0,4},{2,6},{4,0},{6,2},{1,5},{3,7},{5,1},{7,3},{8,12},{10,14},{12... | collective-permute-start | bytes 1572872 | tf_op jit(solution)/shard_map/ppermute | solution.py:1059
  (55 other events, 444.2 us)
Sparse Core Ops, SparseCore 0:
  10.3 35.7 all-gather.1
  259.3 43.9 reduce-scatter.4
  306.7 94.5 reduce-scatter.6

commit v2 on v1

--- a/solution.py
+++ b/solution.py
@@ -17,8 +17,7 @@
 HALF = 256
 CAP = 160
 MAIN = 96
-MORE = 32
-PIECES = 2
+TILES = -(-CAP // MAIN)
 PAD = 272
 N_FSDP = 16
 N_CONTEXT = 4
@@ -422,13 +421,12 @@
     return number == places.astype(jnp.int32)
 
 
-def expert_kernel(order, where_at, x_low, x_high, c_low, c_high, w_m, w_o, *refs):
-    refs = refs[len(refs) - 29 :]
-    out_y, out_x, kept_x, kept_g, kept_h, more_x, more_g, more_h, pieces = refs[:9]
+def expert_kernel(order, where_at, x_low, x_high, c_low, c_high, w_gate, w_up, w_down, *refs):
+    refs = refs[len(refs) - 25 :]
+    out_y, out_x, kept_x, kept_g, kept_h, more_x, more_g, more_h, tiles = refs[:9]
     x_all, c_all, wv, xs, gs, hs, picks, sums, ys, bs, total, places, gate_rows, dots = refs[9:23]
-    mx, mg, mh = refs[23:26]
-    in_sem, out_sem, more_sem = refs[26:]
-    chunk = where_at[2]
+    in_sem, out_sem = refs[23:]
+    slot = where_at[2]
     lane_block, row_at = where_at[0], where_at[1]
     copy = pltpu.make_async_copy
     loads = [
@@ -439,163 +437,167 @@
     ]
 
     def load_w(e):
-        return [
-            copy(w_m.at[e, :, 0:512], wv.at[e, :, 0:512], in_sem.at[4 + e]),
-            copy(w_o.at[e, :, 0:512], wv.at[e, :, 512:1024], in_sem.at[6 + e]),
-            copy(w_m.at[e, :, 512:768], wv.at[e, :, 1024:1280], in_sem.at[8 + e]),
-            copy(w_o.at[e, :, 512:768], wv.at[e, :, 1280:1536], in_sem.at[10 + e]),
-        ]
+        copies = []
+        for part in range(2):
+            for w, at in ((w_gate, 512 * part), (w_up, 512 * part + 256), (w_down, 1024 + 256 * part)):
+                sem = in_sem.at[4 + 2 * len(copies) + e]
+                copies.append(copy(w.at[part, e], wv.at[e, :, at : at + 256], sem))
+        return copies
 
     for load in loads + load_w(0) + load_w(1):
         load.start()
     for load in loads:
         load.wait()
 
-    def gather(h, carry):
+    def read(h, carry):
         table = c_all[h, HALF : HALF + 8, :].astype(F32)
         gate_table = x_all[h, HALF:PAD, :].astype(F32)
         gate_table = gate_table[0:8] + gate_table[8:16]
-        pick = []
         for e in range(2):
-            row = own_row(table, lane_block, row_at + e)
-            places[pl.ds(4 * e + h, 1), :] = row
+            places[pl.ds(4 * e + h, 1), :] = own_row(table, lane_block, row_at + e)
             gate_rows[pl.ds(4 * e + h, 1), :] = own_row(gate_table, lane_block, row_at + e)
-            pick.append(jnp.where(pick_rows(row, 0, MAIN), 1.0, 0.0))
-        pick = jnp.concatenate(pick, axis=0).astype(BF)
-        picks[h] = pick
-        x = dot(pick, x_all[h, 0:HALF, :]).astype(BF)
-        g = dot(pick, c_all[h, 0:HALF, :]).astype(BF)
-        to = pl.ds(pl.multiple_of(h * MAIN, MAIN), MAIN)
+        return carry
+
+    lax.fori_loop(0, 4, read, 0)
+    most = jnp.max(places[...]).astype(jnp.int32)
+    count = jnp.maximum(most, 0) // MAIN + 1
+    tiles[...] = jnp.zeros((8, 128), F32) + count.astype(F32)
+
+    rows = pl.ds(pl.multiple_of(slot * (4 * MAIN), 4 * MAIN), 4 * MAIN)
+
+    def tile(i, carry):
+        first = i * MAIN
+        more = pl.ds(pl.multiple_of(jnp.maximum(i - 1, 0) * (4 * MAIN), 4 * MAIN), 4 * MAIN)
+        sends = lambda e: (
+            (xs, kept_x, more_x, e),
+            (gs, kept_g, more_g, 2 + e),
+            (hs, kept_h, more_h, 4 + e),
+        )
+
+        def start(v, kept, other, e, n):
+            @pl.when(i == 0)
+            def _():
+                copy(v.at[e], kept.at[e, rows], out_sem.at[n]).start()
+
+            @pl.when(i > 0)
+            def _():
+                copy(v.at[e], other.at[e, more], out_sem.at[n]).start()
+
+        def gather(h, carry):
+            pick = [
+                jnp.where(pick_rows(places[pl.ds(4 * e + h, 1), :], first, MAIN), 1.0, 0.0)
+                for e in range(2)
+            ]
+            pick = jnp.concatenate(pick, axis=0).astype(BF)
+            picks[h] = pick
+            x = dot(pick, x_all[h, 0:HALF, :]).astype(BF)
+            g = dot(pick, c_all[h, 0:HALF, :]).astype(BF)
+            to = pl.ds(pl.multiple_of(h * MAIN, MAIN), MAIN)
+            for e in range(2):
+                xs[e, to, :] = x[e * MAIN : e * MAIN + MAIN]
+                gs[e, to, :] = g[e * MAIN : e * MAIN + MAIN]
+            return carry
+
+        lax.fori_loop(0, 4, gather, 0)
         for e in range(2):
-            xs[e, to, :] = x[e * MAIN : e * MAIN + MAIN]
-            gs[e, to, :] = g[e * MAIN : e * MAIN + MAIN]
+            start(xs, kept_x, more_x, e, e)
+            start(gs, kept_g, more_g, e, 2 + e)
+
+        def math(e, carry):
+            here = [pick_rows(places[pl.ds(4 * e + h, 1), :], first, MAIN) for h in range(4)]
+            gate = [
+                jnp.sum(
+                    jnp.where(here[h], gate_rows[pl.ds(4 * e + h, 1), :], 0.0),
+                    axis=1,
+                    keepdims=True,
+                )
+                for h in range(4)
+            ]
+
+            @pl.when(i == 0)
+            def _():
+                for load in load_w(e):
+                    load.wait()
+
+            y, back, act, grad, gate_dot = expert_math(
+                xs[e], gs[e], jnp.concatenate(gate, axis=0), wv.at[e]
+            )
+            hs[e, :, 0:512] = act
+            hs[e, :, 512:1536] = grad
+            start(hs, kept_h, more_h, e, 4 + e)
+            to = pl.ds(pl.multiple_of(e * MAIN, MAIN), MAIN)
+            for h in range(4):
+                at = slice(h * MAIN, h * MAIN + MAIN)
+                sums[h, to, 0:D] = y[at]
+                sums[h, to, D : 2 * D] = back[at]
+                spread = jnp.sum(jnp.where(here[h], gate_dot[at], 0.0), axis=0, keepdims=True)
+                row = pl.ds(4 * e + h, 1)
+                dots[row, :] = jnp.where(i == 0, 0.0, dots[row, :]) + spread
+            return carry
+
+        lax.fori_loop(0, 2, math, 0)
+        last = i == count - 1
+
+        def scatter(h, carry):
+            out = dot_tn(picks[h], sums[h])
+            at = pl.ds(pl.multiple_of(h * HALF, HALF), HALF)
+
+            @pl.when(i > 0)
+            def _():
+                total[at, :] += out
+
+            @pl.when((i == 0) & jnp.logical_not(last))
+            def _():
+                total[at, :] = out
+
+            @pl.when(last)
+            def _():
+                @pl.when(i == 0)
+                def _():
+                    ys[h] = out[:, 0:D].astype(BF)
+                    bs[h, 0:HALF, :] = out[:, D : 2 * D].astype(BF)
+
+                @pl.when(i > 0)
+                def _():
+                    ys[h] = total[at, 0:D].astype(BF)
+                    bs[h, 0:HALF, :] = total[at, D : 2 * D].astype(BF)
+
+                row = lax.broadcasted_iota(jnp.int32, (8, 256), 0)
+                table = jnp.where(row == row_at, dots[pl.ds(h, 1), :], 0.0)
+                table = table + jnp.where(row == row_at + 1, dots[pl.ds(4 + h, 1), :], 0.0)
+                table = [jnp.where(lane_block == k, table, 0.0) for k in range(4)]
+                high, low = split(jnp.concatenate(table, axis=1))
+                bs[h, HALF:PAD, :] = jnp.concatenate([high, low], axis=0)
+                copy(bs.at[h], out_x.at[h], out_sem.at[6 + h]).start()
+                copy(ys.at[h], out_y.at[order[h]], out_sem.at[10 + h]).start()
+
+            return carry
+
+        lax.fori_loop(0, 4, scatter, 0)
+        for e in range(2):
+            for v, kept, _, n in sends(e):
+                copy(v.at[e], kept.at[e, rows], out_sem.at[n]).wait()
         return carry
 
-    lax.fori_loop(0, 4, gather, 0)
-    rows = pl.ds(pl.multiple_of(chunk * (4 * MAIN), 4 * MAIN), 4 * MAIN)
-    sends = [copy(xs.at[e], kept_x.at[e, rows], out_sem.at[e]) for e in range(2)]
-    sends += [copy(gs.at[e], kept_g.at[e, rows], out_sem.at[2 + e]) for e in range(2)]
-    for send in sends:
-        send.start()
-    send_h = lambda e: copy(hs.at[e], kept_h.at[e, rows], out_sem.at[4 + e])
-    send_x = lambda h: copy(bs.at[h], out_x.at[h], out_sem.at[6 + h])
-    send_y = lambda h: copy(ys.at[h], out_y.at[order[h]], out_sem.at[10 + h])
-
-    def gates(e, first, count):
-        here = [pick_rows(places[pl.ds(4 * e + h, 1), :], first, count) for h in range(4)]
-        columns = [
-            jnp.sum(
-                jnp.where(here[h], gate_rows[pl.ds(4 * e + h, 1), :], 0.0), axis=1, keepdims=True
-            )
-            for h in range(4)
-        ]
-        return here, jnp.concatenate(columns, axis=0)
-
-    def spread(here, gate_dot, count, h):
-        part = gate_dot[h * count : h * count + count]
-        return jnp.sum(jnp.where(here[h], part, 0.0), axis=0, keepdims=True)
-
-    def math(e, carry):
-        here, gate = gates(e, 0, MAIN)
-        for load in load_w(e):
-            load.wait()
-        y, back, act, grad, gate_dot = expert_math(xs[e], gs[e], gate, wv.at[e])
-        hs[e, :, 0:512] = act
-        hs[e, :, 512:1536] = grad
-        send_h(e).start()
-        to = pl.ds(pl.multiple_of(e * MAIN, MAIN), MAIN)
-        for h in range(4):
-            sums[h, to, 0:D] = y[h * MAIN : h * MAIN + MAIN]
-            sums[h, to, D : 2 * D] = back[h * MAIN : h * MAIN + MAIN]
-            dots[pl.ds(4 * e + h, 1), :] = spread(here, gate_dot, MAIN, h)
-        return carry
-
-    lax.fori_loop(0, 2, math, 0)
-
-    counts = []
-    for e in range(2):
-        most = jnp.max(places[4 * e : 4 * e + 4, :]).astype(jnp.int32) + 1
-        counts.append((jnp.maximum(most - MAIN, 0) + MORE - 1) // MORE)
-        pieces[e] = jnp.zeros((8, 128), F32) + counts[e].astype(F32)
-
-    @pl.when(counts[0] + counts[1] > 0)
-    def _():
-        total[...] = jnp.zeros_like(total)
-
-        def piece(n, carry):
-            e = jnp.where(n < counts[0], 0, 1)
-            i = n - e * counts[0]
-            here, gate = gates(e, MAIN + i * MORE, MORE)
-            pick = [jnp.where(v, 1.0, 0.0).astype(BF) for v in here]
-            for h in range(4):
-                to = slice(h * MORE, h * MORE + MORE)
-                mx[to, :] = dot(pick[h], x_all[h, 0:HALF, :]).astype(BF)
-                mg[to, :] = dot(pick[h], c_all[h, 0:HALF, :]).astype(BF)
-            y, back, act, grad, gate_dot = expert_math(mx[...], mg[...], gate, wv.at[e])
-            mh[:, 0:512] = act
-            mh[:, 512:1536] = grad
-            to = pl.ds(pl.multiple_of(i * 4 * MORE, 4 * MORE), 4 * MORE)
-            extra = [
-                copy(v, far.at[e, to], more_sem.at[k])
-                for k, (v, far) in enumerate(((mx, more_x), (mg, more_g), (mh, more_h)))
-            ]
-            for send in extra:
-                send.start()
-            both = jnp.concatenate([y, back], axis=1)
-            for h in range(4):
-                part = both[h * MORE : h * MORE + MORE]
-                total[h * HALF : h * HALF + HALF, :] += dot_tn(pick[h], part)
-                dots[pl.ds(4 * e + h, 1), :] += spread(here, gate_dot, MORE, h)
-            for send in extra:
-                send.wait()
-            return carry
-
-        lax.fori_loop(0, counts[0] + counts[1], piece, 0)
-
-    def scatter(h, carry):
-        out = dot_tn(picks[h], sums[h])
-        ys[h] = out[:, 0:D].astype(BF)
-        bs[h, 0:HALF, :] = out[:, D : 2 * D].astype(BF)
-        row = lax.broadcasted_iota(jnp.int32, (8, 256), 0)
-        table = jnp.where(row == row_at, dots[pl.ds(h, 1), :], 0.0)
-        table = table + jnp.where(row == row_at + 1, dots[pl.ds(4 + h, 1), :], 0.0)
-        table = [jnp.where(lane_block == k, table, 0.0) for k in range(4)]
-        high, low = split(jnp.concatenate(table, axis=1))
-        bs[h, HALF:PAD, :] = jnp.concatenate([high, low], axis=0)
-
-        @pl.when(counts[0] + counts[1] > 0)
-        def _():
-            at = pl.ds(pl.multiple_of(h * HALF, HALF), HALF)
-            ys[h] = (ys[h].astype(F32) + total[at, 0:D]).astype(BF)
-            bs[h, 0:HALF, :] = (bs[h, 0:HALF, :].astype(F32) + total[at, D : 2 * D]).astype(BF)
-
-        send_x(h).start()
-        send_y(h).start()
-        return carry
-
-    lax.fori_loop(0, 4, scatter, 0)
-    for send in sends:
-        send.wait()
-    for e in range(2):
-        send_h(e).wait()
+    lax.fori_loop(0, count, tile, 0)
     for h in range(4):
-        send_x(h).wait()
-        send_y(h).wait()
-
-
-def expert_chunk(order, where_at, x, cotangents, mine, other, kept, *others):
-    rows, more = 4 * MAIN, 4 * MORE * PIECES
+        copy(bs.at[h], out_x.at[h], out_sem.at[6 + h]).wait()
+        copy(ys.at[h], out_y.at[order[h]], out_sem.at[10 + h]).wait()
+
+
+def expert_chunk(order, where_at, x, cotangents, weights, kept):
+    rows = 4 * MAIN
     widths = (D, D, 1536)
     shape = lambda *v: jax.ShapeDtypeStruct(v, BF)
     vmem = lambda *v: pltpu.VMEM(v, BF)
-    aliases = {8: 0, 9: 2, 10: 3, 11: 4} if kept else {}
+    aliases = {9: 0, 10: 2, 11: 3, 12: 4} if kept else {}
     return pl.pallas_call(
         expert_kernel,
         grid_spec=pltpu.PrefetchScalarGridSpec(
             num_scalar_prefetch=2,
             grid=(1,),
-            in_specs=[HBM] * (6 + len(kept) + len(others)),
-            out_specs=[HBM] * 8 + [pl.BlockSpec((2, 8, 128), lambda i, r, w: (0, 0, 0))],
+            in_specs=[HBM] * (7 + len(kept)),
+            out_specs=[HBM] * 8 + [pl.BlockSpec((8, 128), lambda i, r, w: (0, 0))],
             scratch_shapes=[
                 vmem(4, PAD, D),
                 vmem(4, PAD, D),
@@ -611,23 +613,19 @@
                 pltpu.VMEM((8, 256), F32),
                 pltpu.VMEM((8, 256), F32),
                 pltpu.VMEM((8, 256), F32),
-                vmem(4 * MORE, D),
-                vmem(4 * MORE, D),
-                vmem(4 * MORE, 1536),
-                pltpu.SemaphoreType.DMA((12,)),
+                pltpu.SemaphoreType.DMA((16,)),
                 pltpu.SemaphoreType.DMA((14,)),
-                pltpu.SemaphoreType.DMA((3,)),
             ],
         ),
         out_shape=[shape(N_FSDP, HALF, D), shape(4, PAD, D)]
         + [shape(2, 4 * rows, n) for n in widths]
-        + [shape(2, more, n) for n in widths]
-        + [jax.ShapeDtypeStruct((2, 8, 128), F32)],
+        + [shape(2, (TILES - 1) * rows, n) for n in widths]
+        + [jax.ShapeDtypeStruct((8, 128), F32)],
         input_output_aliases=aliases,
         compiler_params=params(1),
         cost_estimate=cost(14 * 10**9, 30 * 10**6),
         name="experts",
-    )(order, where_at, *x, *cotangents, mine, other, *kept, *others)
+    )(order, where_at, *x, *cotangents, *weights, *kept)
 
 
 def expert_weight_kernel(place, x, g, act, grad, *refs):
@@ -637,12 +635,12 @@
     down[...] = dot_tn(g[0], act[0])
     gate_up[...] = dot_tn(x[0], grad[0])
     for chunk in range(4):
-        count = jnp.max(counts[chunk][0]).astype(jnp.int32)
+        count = jnp.max(counts[chunk][...]).astype(jnp.int32) - 1
 
         @pl.when(count > 0)
         def _(chunk=chunk, count=count):
             def piece(i, carry):
-                rows = pl.ds(pl.multiple_of(i * 4 * MORE, 4 * MORE), 4 * MORE)
+                rows = pl.ds(pl.multiple_of(i * 4 * MAIN, 4 * MAIN), 4 * MAIN)
                 for ref, to in zip(more[3 * chunk : 3 * chunk + 3], (mx, mg, mh)):
                     pltpu.sync_copy(ref.at[expert, rows], to)
                 for p in range(2):
@@ -679,18 +677,18 @@
                 pl.BlockSpec((1, rows, 512), lambda e, p, r: (e, 0, 1 + p)),
             ]
             + [HBM] * 12
-            + [pl.BlockSpec((1, 8, 128), by_expert)] * 4
+            + [pl.BlockSpec((8, 128), lambda e, p, r: (0, 0))] * 4
             + [HBM] * len(others),
             out_specs=pl.BlockSpec(
                 (4, 1, 1, 256, 768),
-                lambda e, p, r: (0, jnp.where(p == 0, r[0], 1 - r[0]), e, 0, 0),
+                lambda e, p, r: (0, p, e, 0, 0),
             ),
             scratch_shapes=[
                 pltpu.VMEM((D, 256), F32),
                 pltpu.VMEM((D, 512), F32),
-                pltpu.VMEM((4 * MORE, D), BF),
-                pltpu.VMEM((4 * MORE, D), BF),
-                pltpu.VMEM((4 * MORE, 1536), BF),
+                pltpu.VMEM((4 * MAIN, D), BF),
+                pltpu.VMEM((4 * MAIN, D), BF),
+                pltpu.VMEM((4 * MAIN, 1536), BF),
             ],
         ),
         out_shape=jax.ShapeDtypeStruct((4, 2, 2, 256, 768), BF),
@@ -1134,14 +1132,13 @@
     cot_payload = pack_cotangent(as_row(t), cotangent, table, *shards[1:])
     cot_row = gather_row(cot_payload)
 
-    packed = jnp.concatenate([w_gate, w_up, w_down], axis=2)
-    packed_o = swap_cores(packed)
+    experts_w = [lax.all_gather(w, "tensor", axis=0) for w in (w_gate, w_up, w_down)]
     seg = segments.reshape(2, 4, 4, 2, 32).transpose(0, 1, 3, 2, 4).reshape(2, 8, 128)
     seg = jnp.take(seg, near, axis=1).reshape(2, 1, SEQ).astype(F32)
 
     cosine, sine = (jnp.asarray(v) for v in rotary_tables())
     weights, small, heads, cosine, sine, normed1, k_proj, k_b, v_b, q_proj, q_b = project(
-        order.reshape(-1), near.astype(jnp.int32), tokens_all, shards, cosine, sine, packed_o, seg
+        order.reshape(-1), near.astype(jnp.int32), tokens_all, shards, cosine, sine, seg
     )
     cot_chunks = gather_chunks(*stack_pairs(cot_row, small))
     attended, branch_m, branch_o = attend(q_b, k_b, v_b, seg, weights, cot_chunks[0][0])
@@ -1155,7 +1152,7 @@
     for slot, i in enumerate((0, 1, 3, 2)):
         where_at = as_row(f // 4, 2 * (f % 4), slot)
         result = expert_chunk(
-            order[i], where_at, chunks[i], cot_chunks[i], packed, packed_o, carried
+            order[i], where_at, chunks[i], cot_chunks[i], experts_w, carried
         )
         carried = result[0], *result[2:5]
         outs_x[i] = result[1]
@@ -1184,7 +1181,8 @@
     gin_m, gin_o = input_grads(gq, gk, gv, weights, grads_w[0])
     (sent,) = add_blocks((gin_m, swap_cores(gin_o)))
     gin = scatter_parts(sent, shift)
-    grad_tokens = finish(*gin, tokens_m, grad_hidden, small, grads_e)
+    both = lambda v, *others: join(as_row(t), v, swap_cores(v), *others)
+    grad_tokens = both(finish(*gin, tokens_m, grad_hidden, small, grads_e))
 
     grads_w = scatter_parts(grads_w, along(1))
     (grads_w,) = add_blocks(grads_w, (), *sent[1:])
@@ -1196,12 +1194,11 @@
     )
     sums = sums + swap_cores(sums)
 
-    both = lambda v, *others: join(as_row(t), v, swap_cores(v), *others)
     block_half = (hidden1 + mixed.astype(F32)).astype(BF)
     grads_e = grads_e.astype(F32)
     return (
         both(block_half, sums),
-        both(grad_tokens),
+        grad_tokens,
         sums[:, 35],
         g_query,
         g_key,

time: 439 us -> 445 us (1.014); the launches traced: 431 us -> 450 us
  starting transfers between devices: 70.5 us -> 98.7 us
  waiting for transfers between devices: 130 us -> 125 us
    ppermute x36, waiting for transfers between devices: 127 us -> 91.4 us  [ring(): return lax.ppermute(value, ('fsdp', 'tensor'), ring_pairs(stage, step))]
    ppermute x6, waiting for transfers between devices: 2.18 us -> 17.8 us  [shift(): lax.ppermute(value, 'context', [(i, (i + step) % 4) for i in range(4)])]
    unnamed x4 -> x7, waiting for transfers between devices: 0.05 us -> 11.7 us
    ppermute x7 -> x6, starting transfers between devices: 13.5 us -> 23.7 us  [swap_cores(): return lax.ppermute(value, 'tensor', [(0, 1), (1, 0)])]
    ppermute x36, starting transfers between devices: 46.7 us -> 56.5 us  [ring(): return lax.ppermute(value, ('fsdp', 'tensor'), ring_pairs(stage, step))]
    ppermute x6, starting transfers between devices: 10.2 us -> 18.2 us  [shift(): lax.ppermute(value, 'context', [(i, (i + step) % 4) for i in range(4)])]
    unnamed x74 -> x72, local copies, waits for them, and re-layouts: 10.8 us -> 9.77 us
  transfers between devices with their start and end apart: 52 -> 54, of which waited for: 22 -> 20; matrix products, arithmetic and copies ran while one was open for 5% -> 4% of each run, Pallas kernels for 40% -> 39%
where the time goes in v2:
time: 445 us; the launch traced here: 450 us
  Pallas kernels  185 us (42%)
  waiting for transfers between devices  125 us (28%)
  starting transfers between devices  98.7 us (22%)
  local copies, waits for them, and re-layouts  20.3 us (5%)
  between operations  15.1 us (3%)
  other arithmetic  5.77 us (1%)
    ppermute x36, waiting for transfers between devices, ring(): return lax.ppermute(value, ('fsdp', 'tensor'), ring_pairs(stage, step))  91.4 us
    pallas_call x4, Pallas kernels, expert_chunk(): pl.pallas_call(expert_kernel, grid_spec=pltpu.PrefetchScalarGridSpec(num_...  60.1 us
    ppermute x36, starting transfers between devices, ring(): return lax.ppermute(value, ('fsdp', 'tensor'), ring_pairs(stage, step))  56.5 us
    ppermute x6, starting transfers between devices, swap_cores(): return lax.ppermute(value, 'tensor', [(0, 1), (1, 0)])  23.7 us
    pallas_call x1, Pallas kernels, attend_back(): pl.pallas_call(attend_back_kernel, grid=(2, 2), in_specs=[queries, querie...  22.9 us
    pallas_call x1, Pallas kernels, expert_weights(): pl.pallas_call(expert_weight_kernel, grid_spec=pltpu.PrefetchScalarGridSp...  18.5 us
    ppermute x6, starting transfers between devices, shift(): lax.ppermute(value, 'context', [(i, (i + step) % 4) for i in range(4)])  18.2 us
    ppermute x6, waiting for transfers between devices, shift(): lax.ppermute(value, 'context', [(i, (i + step) % 4) for i in range(4)])  17.8 us
  transfers between devices with their start and end apart: 54, of which 20 were waited for; matrix products, arithmetic and copies ran while one was open for 4% of the time, Pallas kernels for 39%

profile of v2, /device:TPU:1, one launch (start us, length us, event | category | flops | bytes accessed | tf_op | source)
XLA Modules:
  0.0 450.5 jit_solution(13119901243204737773)
XLA Ops:
  13.3 4.4 collective-permute-start.2
  31.7 6.4 %collective-permute-done.5.refs_13_.refs_5_ = bf16[4,64,1664]{2,1,0:T(8,128)(2,1)S(1)} collective-permute-done((bf16[4,64,1664]{2,1,0:T(8,128)(2,1)S(1)}, bf16[4,64,1664]{2,1,0:T(8,128)(2,1)S(1)}, u32[]{:S(2)}, u32[]{:S(2)}) %collective-permute-start.5) | collective-permute-done | bytes 852000 | tf_op jit(solution)/shard_map/ppermute | solution.py:1053
  38.1 9.1 %collective-permute-done.4.refs_12_.refs_4_ = bf16[4,64,1664]{2,1,0:T(8,128)(2,1)S(1)} collective-permute-done((bf16[4,64,1664]{2,1,0:T(8,128)(2,1)S(1)}, bf16[4,64,1664]{2,1,0:T(8,128)(2,1)S(1)}, u32[]{:S(2)}, u32[]{:S(2)}) %collective-permute-start.4) | collective-permute-done | bytes 852000 | tf_op jit(solution)/shard_map/ppermute | solution.py:1053
  54.3 14.0 %project.1 = (bf16[1024,1664]{1,0:T(8,128)(2,1)}, f32[128,1024]{1,0:T(8,128)}, f32[8,128]{1,0:T(8,128)}, f32[1024,128]{1,0:T(8,128)}, f32[1024,128]{1,0:T(8,128)...) custom-call(s32[16]{0:T(128)} %select_n.145.refs_0_, ...), custom_call_target="tpu_custom_call" | custom-call | flops 10000000000 | bytes 20000000 | tf_op jit(solution)/shard_map/project/pallas_call | solution.py:252
  77.7 10.3 %attend.1 = (bf16[2,256,512]{2,1,0:T(8,128)(2,1)}, f32[256,1024]{1,0:T(8,128)}, f32[256,1024]{1,0:T(8,128)}) custom-call(bf16[2,256,512]{2,1,0:T(8,128)(2,1)} %get-tuple-element.105.refs_0_.q, bf16[2,1024,256]{2,1,0:T(8,128)(2,1)} %get-tuple-element.106.refs_1_.k, bf16[2,1024,256]{2,1,0:T(8,128)(2,1)} %get-tuple-element.107.refs_2_.v, ...), custom_call_target="tpu_custom_call" | custom-call | flops 10000000000 | bytes 8000000 | tf_op jit(solution)/shard_map/attend/pallas_call | solution.py:324
  88.0 4.2 collective-permute-start.9
  92.7 7.7 %collective-permute-done.12.refs_8_.c_low = bf16[2,272,1024]{2,1,0:T(8,128)(2,1)} collective-permute-done((bf16[2,272,1024]{2,1,0:T(8,128)(2,1)}, bf16[2,272,1024]{2,1,0:T(8,128)(2,1)}, u32[]{:S(2)}, u32[]{:S(2)}) %collective-permute-start.12) | collective-permute-done | bytes 1114144 | tf_op jit(solution)/shard_map/ppermute | solution.py:1053
  109.8 11.6 %collective-permute-done.16.refs_3_ = bf16[272,1024]{1,0:T(8,128)(2,1)S(1)} collective-permute-done((bf16[272,1024]{1,0:T(8,128)(2,1)}, bf16[272,1024]{1,0:T(8,128)(2,1)S(1)}, u32[]{:S(2)}, u32[]{:S(2)}) %collective-permute-start.16) | collective-permute-done | bytes 557088 | tf_op jit(solution)/shard_map/ppermute | solution.py:1053
  121.3 8.3 %collective-permute-done.15.refs_2_ = bf16[272,1024]{1,0:T(8,128)(2,1)S(1)} collective-permute-done((bf16[272,1024]{1,0:T(8,128)(2,1)}, bf16[272,1024]{1,0:T(8,128)(2,1)S(1)}, u32[]{:S(2)}, u32[]{:S(2)}) %collective-permute-start.15) | collective-permute-done | bytes 557088 | tf_op jit(solution)/shard_map/ppermute | solution.py:1053
  136.7 14.9 %experts.4 = (bf16[16,256,1024]{2,1,0:T(8,128)(2,1)}, bf16[4,272,1024]{2,1,0:T(8,128)(2,1)}, bf16[2,1536,1024]{2,1,0:T(8,128)(2,1)}, bf16[2,1536,1024]{2,1,0:T(8...) custom-call(s32[4]{0:T(128)} %get-tuple-element.265.order, ...), custom_call_target="tpu_custom_call" | custom-call | flops 14000000000 | bytes 30000000 | tf_op jit(solution)/shard_map/experts/pallas_call | solution.py:594
  151.7 8.6 %collective-permute-done.22.x_high = bf16[2,272,1024]{2,1,0:T(8,128)(2,1)} collective-permute-done((bf16[2,272,1024]{2,1,0:T(8,128)(2,1)}, bf16[2,272,1024]{2,1,0:T(8,128)(2,1)}, u32[]{:S(2)}, u32[]{:S(2)}) %collective-permute-start.22) | collective-permute-done | bytes 1114144 | tf_op jit(solution)/shard_map/ppermute | solution.py:1053
  162.1 15.3 %experts.5 = (bf16[16,256,1024]{2,1,0:T(8,128)(2,1)}, bf16[4,272,1024]{2,1,0:T(8,128)(2,1)}, bf16[2,1536,1024]{2,1,0:T(8,128)(2,1)}, bf16[2,1536,1024]{2,1,0:T(8...) custom-call(s32[4]{0:T(128)} %get-tuple-element.266.order, ...), custom_call_target="tpu_custom_call", output_to_operand_aliasing={{0}: (9, {}), {2}: (10, {}), {3}: (11, {}), {4}: (12, {})} | custom-call | flops 14000000000 | bytes 30000000 | tf_op jit(solution)/shard_map/experts/pallas_call | solution.py:594
  177.5 14.9 %experts.6 = (bf16[16,256,1024]{2,1,0:T(8,128)(2,1)}, bf16[4,272,1024]{2,1,0:T(8,128)(2,1)}, bf16[2,1536,1024]{2,1,0:T(8,128)(2,1)}, bf16[2,1536,1024]{2,1,0:T(8...) custom-call(s32[4]{0:T(128)} %get-tuple-element.267.order, ...), custom_call_target="tpu_custom_call", output_to_operand_aliasing={{0}: (9, {}), {2}: (10, {}), {3}: (11, {}), {4}: (12, {})} | custom-call | flops 14000000000 | bytes 30000000 | tf_op jit(solution)/shard_map/experts/pallas_call | solution.py:594
  193.7 14.9 %experts.7 = (bf16[16,256,1024]{2,1,0:T(8,128)(2,1)}, bf16[4,272,1024]{2,1,0:T(8,128)(2,1)}, bf16[2,1536,1024]{2,1,0:T(8,128)(2,1)}, bf16[2,1536,1024]{2,1,0:T(8...) custom-call(s32[4]{0:T(128)} %get-tuple-element.268.order, ...), custom_call_target="tpu_custom_call", output_to_operand_aliasing={{0}: (9, {}), {2}: (10, {}), {3}: (11, {}), {4}: (12, {})} | custom-call | flops 14000000000 | bytes 30000000 | tf_op jit(solution)/shard_map/experts/pallas_call | solution.py:594
  210.3 19.1 %collective-permute-done.25.refs_16_.refs_1_ = bf16[4,272,1024]{2,1,0:T(8,128)(2,1)} collective-permute-done((bf16[4,272,1024]{2,1,0:T(8,128)(2,1)}, bf16[4,272,1024]{2,1,0:T(8,128)(2,1)}, u32[]{:S(2)}, u32[]{:S(2)}) %collective-permute-start.25) | collective-permute-done | bytes 2228256 | tf_op jit(solution)/shard_map/ppermute | solution.py:1053
  229.5 18.5 %expert_weights.1.refs_4_ = bf16[4,2,2,256,768]{4,3,2,1,0:T(8,128)(2,1)} custom-call(s32[1]{0:T(128)} %bitcast.refs_0_.place, bf16[2,1536,1024]{2,1,0:T(8,128)(2,1)} %get-tuple-element.135.x, bf16[2,1536,1024]{2,1,0:T(8,128)(2,1)} %get-tuple-element.136.g, bf16[2,1536,1536]{2,1,0:T(8,128)(2,1)} %get-tuple-element.137.act.grad, ...), custom_call_target="tpu_custom_call" | custom-call | flops 20000000000 | bytes 30000000 | tf_op jit(solution)/shard_map/expert_weights/pallas_call | solution.py:668
  248.0 5.5 %add_blocks.4 = (bf16[272,1024]{1,0:T(8,128)(2,1)}, bf16[272,1024]{1,0:T(8,128)(2,1)}, bf16[272,1024]{1,0:T(8,128)(2,1)}, bf16[272,1024]{1,0:T(8,128)(2,1)}, bf16[4,2,2,256,768]{4,3,2,1,0:T(8,128)(2,1)}) custom-call(bf16[4,272,1024]{2,1,0:T(8,128)(2,1)} %get-tuple-element.131.refs_0_, ...), custom_call_target="tpu_custom_call", output_to_operand_aliasing={{4}: (4, {})} | custom-call | flops 1000000000 | bytes 10000000 | tf_op jit(solution)/shard_map/add_blocks/pallas_call | solution.py:164
  257.8 6.0 %collective-permute-done.28.refs_2_ = bf16[272,1024]{1,0:T(8,128)(2,1)S(1)} collective-permute-done((bf16[272,1024]{1,0:T(8,128)(2,1)}, bf16[272,1024]{1,0:T(8,128)(2,1)S(1)}, u32[]{:S(2)}, u32[]{:S(2)}) %collective-permute-start.28) | collective-permute-done | bytes 557088 | tf_op jit(solution)/shard_map/ppermute | solution.py:1053
  263.7 6.1 %collective-permute-done.29.refs_3_ = bf16[272,1024]{1,0:T(8,128)(2,1)S(1)} collective-permute-done((bf16[272,1024]{1,0:T(8,128)(2,1)S(1)}, bf16[272,1024]{1,0:T(8,128)(2,1)S(1)}, u32[]{:S(2)}, u32[]{:S(2)}) %collective-permute-start.29) | collective-permute-done | bytes 557088 | tf_op jit(solution)/shard_map/ppermute | solution.py:1053
  271.7 4.7 %route_back.1 = (bf16[16,256,1024]{2,1,0:T(8,128)(2,1)}, f32[256,1024]{1,0:T(8,128)}, bf16[256,1024]{1,0:T(8,128)(2,1)}, f32[32,1024]{1,0:T(8,128)}, f32[1,1024]{1,0:T(1,128)}) custom-call(bf16[16,256,1024]{2,1,0:T(8,128)(2,1)} %get-tuple-element.130.refs_0_, bf16[272,1024]{1,0:T(8,128)(2,1)} %get-tuple-element.154.refs_1_, ...), custom_call_target="tpu_custom_call", output_to_operand_aliasing={{0}: (0, {})} | custom-call | flops 4000000000 | bytes 6000000 | tf_op jit(solution)/shard_map/route_back/pallas_call | solution.py:732
  277.5 4.4 collective-permute-start.32
  284.2 22.9 %attend_back.1 = (bf16[2,256,512]{2,1,0:T(8,128)(2,1)}, bf16[2,1024,256]{2,1,0:T(8,128)(2,1)}, bf16[2,1024,256]{2,1,0:T(8,128)(2,1)}, f32[8,256]{1,0:T(8,128)}) custom-call(bf16[2,256,512]{2,1,0:T(8,128)(2,1)} %get-tuple-element.105.refs_0_.q, f32[2,256,512]{2,1,0:T(8,128)} %get-tuple-element.162.q_proj, bf16[2,1024,256]{2,1,0:T(8,128)(2,1)} %get-tuple-element.106.refs_1_.k, ...), custom_call_target="tpu_custom_call" | custom-call | flops 17999998976 | bytes 16000000 | tf_op jit(solution)/shard_map/attend_back/pallas_call | solution.py:818
  307.1 9.6 %weight_grads.1 = (bf16[4,64,1664]{2,1,0:T(8,128)(2,1)}, bf16[4,64,1664]{2,1,0:T(8,128)(2,1)}, bf16[4,64,1664]{2,1,0:T(8,128)(2,1)}, bf16[4,64,1664]{2,1,0:T(8,128)(2,1)}) custom-call(s32[16]{0:T(128)} %select_n.156.refs_0_, bf16[2,1024,1024]{2,1,0:T(8,128)(2,1)} %get-tuple-element.161.refs_1_, bf16[2,256,512]{2,1,0:T(8,128)(2,1)} %get-tuple-element.169.refs_2_.refs_0_, ...), custom_call_target="tpu_custom_call" | custom-call | flops 8999999488 | bytes 16000000 | tf_op jit(solution)/shard_map/weight_grads/pallas_call | solution.py:899
  316.7 6.7 %input_grads.1 = (bf16[4,256,1024]{2,1,0:T(8,128)(2,1)}, bf16[4,256,1024]{2,1,0:T(8,128)(2,1)}) custom-call(bf16[2,256,512]{2,1,0:T(8,128)(2,1)} %get-tuple-element.169.refs_2_.refs_0_, bf16[2,1024,256]{2,1,0:T(8,128)(2,1)} %get-tuple-element.170.refs_3_.refs_1_, bf16[2,1024,256]{2,1,0:T(8,128)(2,1)} %get-tuple-element.171.refs_4_.refs_2_, ...), custom_call_target="tpu_custom_call" | custom-call | flops 6000000000 | bytes 12000000 | tf_op jit(solution)/shard_map/input_grads/pallas_call | solution.py:940
  323.9 4.1 collective-permute-done.36.refs_1_
  337.0 8.3 %collective-permute-start.41 = (bf16[256,1024]{1,0:T(8,128)(2,1)}, bf16[256,1024]{1,0:T(8,128)(2,1)}, u32[]{:S(2)}, u32[]{:S(2)}) collective-permute-start(bf16[256,1024]{1,0:T(8,128)(2,1)} %get-tuple-element.182.refs_5_), channel_id=1, source_target_pairs={{0,6},{2,0},{4,2},{6,4},{1,7},{3,1},{5,3},{7,5},{8,14},{10,8},{12,... | collective-permute-start | bytes 1572872 | tf_op jit(solution)/shard_map/ppermute | solution.py:1057
  345.3 7.8 %collective-permute-done.40.refs_4_.refs_1_ = bf16[256,1024]{1,0:T(8,128)(2,1)} collective-permute-done((bf16[256,1024]{1,0:T(8,128)(2,1)}, bf16[256,1024]{1,0:T(8,128)(2,1)}, u32[]{:S(2)}, u32[]{:S(2)}) %collective-permute-start.40) | collective-permute-done | bytes 524320 | tf_op jit(solution)/shard_map/ppermute | solution.py:1057
  353.4 10.0 %collective-permute-done.42.refs_6_.refs_3_ = bf16[256,1024]{1,0:T(8,128)(2,1)} collective-permute-done((bf16[256,1024]{1,0:T(8,128)(2,1)}, bf16[256,1024]{1,0:T(8,128)(2,1)}, u32[]{:S(2)}, u32[]{:S(2)}) %collective-permute-start.42) | collective-permute-done | bytes 524320 | tf_op jit(solution)/shard_map/ppermute | solution.py:1057
  367.2 12.6 %collective-permute-start.46 = (f32[256,1024]{1,0:T(8,128)}, f32[256,1024]{1,0:T(8,128)}, u32[]{:S(2)}, u32[]{:S(2)}) collective-permute-start(f32[256,1024]{1,0:T(8,128)} %finish.1.refs_1_), channel_id=1, source_target_pairs={{0,1},{1,0},{2,3},{3,2},{4,5},{5,4},{6,7},{7,6},{8,9},{9,8},{10,11... | collective-permute-start | bytes 3145736 | tf_op jit(solution)/shard_map/ppermute | solution.py:1061
  386.9 11.8 %collective-permute-start.39 = (bf16[64,1664]{1,0:T(8,128)(2,1)}, bf16[64,1664]{1,0:T(8,128)(2,1)S(1)}, u32[]{:S(2)}, u32[]{:S(2)}) collective-permute-start(bf16[64,1664]{1,0:T(8,128)(2,1)} %get-tuple-element.187), channel_id=1, source_target_pairs={{0,64},{1,17},{8,72},{9,25},{16,80},{17,1},{24,88},{25,9},{32,96},... | collective-permute-start | bytes 638984 | tf_op jit(solution)/shard_map/ppermute | solution.py:1053
  406.9 6.9 %collective-permute-start.45 = (bf16[64,1664]{1,0:T(8,128)(2,1)}, bf16[64,1664]{1,0:T(8,128)(2,1)S(1)}, u32[]{:S(2)}, u32[]{:S(2)}) collective-permute-start(bf16[64,1664]{1,0:T(8,128)(2,1)} %add_blocks.7.refs_0_), channel_id=1, source_target_pairs={{0,4},{2,6},{4,0},{6,2},{1,5},{3,7},{5,1},{7,3},{8,12},{10,14},{12... | collective-permute-start | bytes 638984 | tf_op jit(solution)/shard_map/ppermute | solution.py:1057
  415.3 10.2 %reduce-scatter.7.cloned.1.call-done = bf16[1,256,1024]{2,1,0:T(8,128)(2,1)} async-done(((bf16[16,256,1024]{2,1,0:T(8,128)(2,1)}), bf16[1,256,1024]{2,1,0:T(8,128)(2,1)}) %reduce-scatter.7.cloned.1.call-update) | async-done | bytes 524304
  (228 shorter events, 115.4 us)
Async XLA Ops:
  7.2 47.0 %all-gather.8.cloned.1.call-start = ((), (), s32[]{:S(2)}) async-start(), calls=%async_computation.2 | async-start | bytes 4718592 | tf_op jit(solution)/shard_map/all_gather | solution.py:1120
  9.3 127.4 %all-gather.10.cloned.1.call-start = ((), (), s32[]{:S(2)}) async-start(), calls=%async_computation.4 | async-start | bytes 3145728 | tf_op jit(solution)/shard_map/all_gather | solution.py:1135
  10.0 126.6 %all-gather.12.cloned.1.call-start = ((), (), s32[]{:S(2)}) async-start(), calls=%async_computation.5 | async-start | bytes 3145728 | tf_op jit(solution)/shard_map/all_gather | solution.py:1135
  10.8 125.9 %all-gather.14.cloned.1.call-start = ((), (), s32[]{:S(2)}) async-start(), calls=%async_computation.6 | async-start | bytes 3145728 | tf_op jit(solution)/shard_map/all_gather | solution.py:1135
  20.4 343.1 %reduce-scatter.5.cloned.1.call-start = ((), (), s32[]{:S(2)}) async-start(), calls=%async_computation.3 | async-start | bytes 7077888 | tf_op jit(solution)/shard_map/reduce_scatter | solution.py:1166
  27.1 20.0 %collective-permute-start.4 = (bf16[4,64,1664]{2,1,0:T(8,128)(2,1)S(1)}, bf16[4,64,1664]{2,1,0:T(8,128)(2,1)S(1)}, u32[]{:S(2)}, u32[]{:S(2)}) collective-permute-start(bf16[4,64,1664]{2,1,0:T(8,128)(2,1)S(1)} %pad_maximum_fusion.refs_10_), channel_id=1, source_target_pairs={{0,8},{1,33},{8,16},{9,41},{16,24},{17,49},{24,0},{25,57},{32,40},... | collective-permute-start | bytes 2555912 | tf_op jit(solution)/shard_map/ppermute | solution.py:1053
  27.7 19.6 %collective-permute-start.3 = (bf16[4,64,1664]{2,1,0:T(8,128)(2,1)S(1)}, bf16[4,64,1664]{2,1,0:T(8,128)(2,1)}, u32[]{:S(2)}, u32[]{:S(2)}) collective-permute-start(bf16[4,64,1664]{2,1,0:T(8,128)(2,1)S(1)} %pad_maximum_fusion.refs_10_), channel_id=1, source_target_pairs={{0,24},{1,97},{8,0},{9,105},{16,8},{17,113},{24,16},{25,121},{32,5... | collective-permute-start | bytes 2555912 | tf_op jit(solution)/shard_map/ppermute | solution.py:1053
  50.0 18.3 %collective-permute-start.8 = (bf16[272,1024]{1,0:T(8,128)(2,1)}, bf16[272,1024]{1,0:T(8,128)(2,1)S(1)}, u32[]{:S(2)}, u32[]{:S(2)}) collective-permute-start(bf16[272,1024]{1,0:T(8,128)(2,1)} %pack_cotangent.1.refs_0_.refs_5_), channel_id=1, source_target_pairs={{0,64},{1,17},{8,72},{9,25},{16,80},{17,1},{24,88},{25,9},{32,96},... | collective-permute-start | bytes 1671176 | tf_op jit(solution)/shard_map/ppermute | solution.py:1053
  72.3 29.7 %collective-permute-start.13 = (bf16[2,272,1024]{2,1,0:T(8,128)(2,1)}, bf16[2,272,1024]{2,1,0:T(8,128)(2,1)}, u32[]{:S(2)}, u32[]{:S(2)}) collective-permute-start(bf16[2,272,1024]{2,1,0:T(8,128)(2,1)} %get-tuple-element.113.c_high), channel_id=1, source_target_pairs={{0,8},{1,33},{8,16},{9,41},{16,24},{17,49},{24,0},{25,57},{32,40},... | collective-permute-start | bytes 3342344 | tf_op jit(solution)/shard_map/ppermute | solution.py:1053
  74.0 18.2 %collective-permute-start.11 = (bf16[2,272,1024]{2,1,0:T(8,128)(2,1)}, bf16[2,272,1024]{2,1,0:T(8,128)(2,1)}, u32[]{:S(2)}, u32[]{:S(2)}) collective-permute-start(bf16[2,272,1024]{2,1,0:T(8,128)(2,1)} %get-tuple-element.113.c_high), channel_id=1, source_target_pairs={{0,24},{1,97},{8,0},{9,105},{16,8},{17,113},{24,16},{25,121},{32,5... | collective-permute-start | bytes 3342344 | tf_op jit(solution)/shard_map/ppermute | solution.py:1053
  75.0 25.4 %collective-permute-start.12 = (bf16[2,272,1024]{2,1,0:T(8,128)(2,1)}, bf16[2,272,1024]{2,1,0:T(8,128)(2,1)}, u32[]{:S(2)}, u32[]{:S(2)}) collective-permute-start(bf16[2,272,1024]{2,1,0:T(8,128)(2,1)} %get-tuple-element.110.refs_5_.c_low), channel_id=1, source_target_pairs={{0,8},{1,33},{8,16},{9,41},{16,24},{17,49},{24,0},{25,57},{32,40},... | collective-permute-start | bytes 3342344 | tf_op jit(solution)/shard_map/ppermute | solution.py:1053
  75.5 26.6 %collective-permute-start.10 = (bf16[2,272,1024]{2,1,0:T(8,128)(2,1)}, bf16[2,272,1024]{2,1,0:T(8,128)(2,1)}, u32[]{:S(2)}, u32[]{:S(2)}) collective-permute-start(bf16[2,272,1024]{2,1,0:T(8,128)(2,1)} %get-tuple-element.110.refs_5_.c_low), channel_id=1, source_target_pairs={{0,24},{1,97},{8,0},{9,105},{16,8},{17,113},{24,16},{25,121},{32,5... | collective-permute-start | bytes 3342344 | tf_op jit(solution)/shard_map/ppermute | solution.py:1053
  92.2 37.4 %collective-permute-start.18 = (bf16[2,272,1024]{2,1,0:T(8,128)(2,1)}, bf16[2,272,1024]{2,1,0:T(8,128)(2,1)}, u32[]{:S(2)}, u32[]{:S(2)}) collective-permute-start(bf16[2,272,1024]{2,1,0:T(8,128)(2,1)} %collective-permute-done.11.refs_7_.c_high), channel_id=1, source_target_pairs={{0,24},{1,97},{8,0},{9,105},{16,8},{17,113},{24,16},{25,121},{32,5... | collective-permute-start | bytes 3342344 | tf_op jit(solution)/shard_map/ppermute | solution.py:1053
  100.4 29.2 %collective-permute-start.17 = (bf16[2,272,1024]{2,1,0:T(8,128)(2,1)}, bf16[2,272,1024]{2,1,0:T(8,128)(2,1)}, u32[]{:S(2)}, u32[]{:S(2)}) collective-permute-start(bf16[2,272,1024]{2,1,0:T(8,128)(2,1)} %collective-permute-done.12.refs_8_.c_low), channel_id=1, source_target_pairs={{0,8},{1,33},{8,16},{9,41},{16,24},{17,49},{24,0},{25,57},{32,40},... | collective-permute-start | bytes 3342344 | tf_op jit(solution)/shard_map/ppermute | solution.py:1053
  105.2 24.4 %collective-permute-start.15 = (bf16[272,1024]{1,0:T(8,128)(2,1)}, bf16[272,1024]{1,0:T(8,128)(2,1)S(1)}, u32[]{:S(2)}, u32[]{:S(2)}) collective-permute-start(bf16[272,1024]{1,0:T(8,128)(2,1)} %get-tuple-element.115.refs_0_.refs_8_), channel_id=1, source_target_pairs={{0,32},{1,9},{8,40},{9,17},{16,48},{17,25},{24,56},{25,1},{32,64},... | collective-permute-start | bytes 1671176 | tf_op jit(solution)/shard_map/ppermute | solution.py:1053
  105.3 24.3 %collective-permute-start.14 = (bf16[272,1024]{1,0:T(8,128)(2,1)}, bf16[272,1024]{1,0:T(8,128)(2,1)}, u32[]{:S(2)}, u32[]{:S(2)}) collective-permute-start(bf16[272,1024]{1,0:T(8,128)(2,1)} %get-tuple-element.115.refs_0_.refs_8_), channel_id=1, source_target_pairs={{0,96},{1,25},{8,104},{9,1},{16,112},{17,9},{24,120},{25,17},{32,0... | collective-permute-start | bytes 1671176 | tf_op jit(solution)/shard_map/ppermute | solution.py:1053
  133.4 28.6 %collective-permute-start.24 = (bf16[2,272,1024]{2,1,0:T(8,128)(2,1)}, bf16[2,272,1024]{2,1,0:T(8,128)(2,1)}, u32[]{:S(2)}, u32[]{:S(2)}) collective-permute-start(bf16[2,272,1024]{2,1,0:T(8,128)(2,1)} %get-tuple-element.116.x_low), channel_id=1, source_target_pairs={{0,24},{1,97},{8,0},{9,105},{16,8},{17,113},{24,16},{25,121},{32,5... | collective-permute-start | bytes 3342344 | tf_op jit(solution)/shard_map/ppermute | solution.py:1053
  134.9 25.4 %collective-permute-start.22 = (bf16[2,272,1024]{2,1,0:T(8,128)(2,1)}, bf16[2,272,1024]{2,1,0:T(8,128)(2,1)}, u32[]{:S(2)}, u32[]{:S(2)}) collective-permute-start(bf16[2,272,1024]{2,1,0:T(8,128)(2,1)} %get-tuple-element.117.x_high), channel_id=1, source_target_pairs={{0,24},{1,97},{8,0},{9,105},{16,8},{17,113},{24,16},{25,121},{32,5... | collective-permute-start | bytes 3342344 | tf_op jit(solution)/shard_map/ppermute | solution.py:1053
  136.6 57.0 %collective-permute-start.20 = (bf16[2,272,1024]{2,1,0:T(8,128)(2,1)}, bf16[2,272,1024]{2,1,0:T(8,128)(2,1)}, u32[]{:S(2)}, u32[]{:S(2)}) collective-permute-start(bf16[2,272,1024]{2,1,0:T(8,128)(2,1)} %get-tuple-element.117.x_high), channel_id=1, source_target_pairs={{0,8},{1,33},{8,16},{9,41},{16,24},{17,49},{24,0},{25,57},{32,40},... | collective-permute-start | bytes 3342344 | tf_op jit(solution)/shard_map/ppermute | solution.py:1053
  151.6 25.9 %collective-permute-start.21 = (bf16[2,272,1024]{2,1,0:T(8,128)(2,1)}, bf16[2,272,1024]{2,1,0:T(8,128)(2,1)}, u32[]{:S(2)}, u32[]{:S(2)}) collective-permute-start(bf16[2,272,1024]{2,1,0:T(8,128)(2,1)} %collective-permute-done.19.x_low), channel_id=1, source_target_pairs={{0,8},{1,33},{8,16},{9,41},{16,24},{17,49},{24,0},{25,57},{32,40},... | collective-permute-start | bytes 3342344 | tf_op jit(solution)/shard_map/ppermute | solution.py:1053
  177.4 52.1 %collective-permute-start.25 = (bf16[4,272,1024]{2,1,0:T(8,128)(2,1)}, bf16[4,272,1024]{2,1,0:T(8,128)(2,1)}, u32[]{:S(2)}, u32[]{:S(2)}) collective-permute-start(bf16[4,272,1024]{2,1,0:T(8,128)(2,1)} %get-tuple-element.132), channel_id=1, source_target_pairs={{0,8},{1,33},{8,16},{9,41},{16,24},{17,49},{24,0},{25,57},{32,40},... | collective-permute-start | bytes 6684680 | tf_op jit(solution)/shard_map/ppermute | solution.py:1053
  192.5 37.0 %collective-permute-start.27 = (bf16[4,272,1024]{2,1,0:T(8,128)(2,1)}, bf16[4,272,1024]{2,1,0:T(8,128)(2,1)}, u32[]{:S(2)}, u32[]{:S(2)}) collective-permute-start(bf16[4,272,1024]{2,1,0:T(8,128)(2,1)} %get-tuple-element.134), channel_id=1, source_target_pairs={{0,16},{1,65},{8,24},{9,73},{16,0},{17,81},{24,8},{25,89},{32,48},... | collective-permute-start | bytes 6684680 | tf_op jit(solution)/shard_map/ppermute | solution.py:1053
  208.6 39.4 %collective-permute-start.26 = (bf16[4,272,1024]{2,1,0:T(8,128)(2,1)}, bf16[4,272,1024]{2,1,0:T(8,128)(2,1)}, u32[]{:S(2)}, u32[]{:S(2)}) collective-permute-start(bf16[4,272,1024]{2,1,0:T(8,128)(2,1)} %get-tuple-element.133), channel_id=1, source_target_pairs={{0,24},{1,97},{8,0},{9,105},{16,8},{17,113},{24,16},{25,121},{32,5... | collective-permute-start | bytes 6684680 | tf_op jit(solution)/shard_map/ppermute | solution.py:1053
  253.5 172.0 %reduce-scatter.7.cloned.1.call-start = ((), (), s32[]{:S(2)}) async-start(), calls=%async_computation.7 | async-start | bytes 8912896
  331.6 21.4 %collective-permute-start.40 = (bf16[256,1024]{1,0:T(8,128)(2,1)}, bf16[256,1024]{1,0:T(8,128)(2,1)}, u32[]{:S(2)}, u32[]{:S(2)}) collective-permute-start(bf16[256,1024]{1,0:T(8,128)(2,1)} %get-tuple-element.181.refs_4_), channel_id=1, source_target_pairs={{0,2},{2,4},{4,6},{6,0},{1,3},{3,5},{5,7},{7,1},{8,10},{10,12},{12... | collective-permute-start | bytes 1572872 | tf_op jit(solution)/shard_map/ppermute | solution.py:1057
  332.9 46.9 %collective-permute-start.33 = (bf16[4,64,1664]{2,1,0:T(8,128)(2,1)}, bf16[4,64,1664]{2,1,0:T(8,128)(2,1)S(1)}, u32[]{:S(2)}, u32[]{:S(2)}) collective-permute-start(bf16[4,64,1664]{2,1,0:T(8,128)(2,1)} %get-tuple-element.176), channel_id=1, source_target_pairs={{0,8},{1,33},{8,16},{9,41},{16,24},{17,49},{24,0},{25,57},{32,40},... | collective-permute-start | bytes 2555912 | tf_op jit(solution)/shard_map/ppermute | solution.py:1053
  332.9 46.9 %collective-permute-start.34 = (bf16[4,64,1664]{2,1,0:T(8,128)(2,1)}, bf16[4,64,1664]{2,1,0:T(8,128)(2,1)S(1)}, u32[]{:S(2)}, u32[]{:S(2)}) collective-permute-start(bf16[4,64,1664]{2,1,0:T(8,128)(2,1)} %get-tuple-element.177), channel_id=1, source_target_pairs={{0,24},{1,97},{8,0},{9,105},{16,8},{17,113},{24,16},{25,121},{32,5... | collective-permute-start | bytes 2555912 | tf_op jit(solution)/shard_map/ppermute | solution.py:1053
  335.8 44.0 %collective-permute-start.35 = (bf16[4,64,1664]{2,1,0:T(8,128)(2,1)}, bf16[4,64,1664]{2,1,0:T(8,128)(2,1)}, u32[]{:S(2)}, u32[]{:S(2)}) collective-permute-start(bf16[4,64,1664]{2,1,0:T(8,128)(2,1)} %get-tuple-element.178), channel_id=1, source_target_pairs={{0,16},{1,65},{8,24},{9,73},{16,0},{17,81},{24,8},{25,89},{32,48},... | collective-permute-start | bytes 2555912 | tf_op jit(solution)/shard_map/ppermute | solution.py:1053
  367.2 63.1 %collective-permute-start.46 = (f32[256,1024]{1,0:T(8,128)}, f32[256,1024]{1,0:T(8,128)}, u32[]{:S(2)}, u32[]{:S(2)}) collective-permute-start(f32[256,1024]{1,0:T(8,128)} %finish.1.refs_1_), channel_id=1, source_target_pairs={{0,1},{1,0},{2,3},{3,2},{4,5},{5,4},{6,7},{7,6},{8,9},{9,8},{10,11... | collective-permute-start | bytes 3145736 | tf_op jit(solution)/shard_map/ppermute | solution.py:1061
  406.9 26.3 %collective-permute-start.45 = (bf16[64,1664]{1,0:T(8,128)(2,1)}, bf16[64,1664]{1,0:T(8,128)(2,1)S(1)}, u32[]{:S(2)}, u32[]{:S(2)}) collective-permute-start(bf16[64,1664]{1,0:T(8,128)(2,1)} %add_blocks.7.refs_0_), channel_id=1, source_target_pairs={{0,4},{2,6},{4,0},{6,2},{1,5},{3,7},{5,1},{7,3},{8,12},{10,14},{12... | collective-permute-start | bytes 638984 | tf_op jit(solution)/shard_map/ppermute | solution.py:1057
  413.8 19.4 %collective-permute-start.44 = (bf16[64,1664]{1,0:T(8,128)(2,1)}, bf16[64,1664]{1,0:T(8,128)(2,1)S(1)}, u32[]{:S(2)}, u32[]{:S(2)}) collective-permute-start(bf16[64,1664]{1,0:T(8,128)(2,1)} %add_blocks.7.refs_0_), channel_id=1, source_target_pairs={{0,6},{2,0},{4,2},{6,4},{1,7},{3,1},{5,3},{7,5},{8,14},{10,8},{12,... | collective-permute-start | bytes 638984 | tf_op jit(solution)/shard_map/ppermute | solution.py:1057
  413.8 19.4 %collective-permute-start.43 = (bf16[64,1664]{1,0:T(8,128)(2,1)}, bf16[64,1664]{1,0:T(8,128)(2,1)S(1)}, u32[]{:S(2)}, u32[]{:S(2)}) collective-permute-start(bf16[64,1664]{1,0:T(8,128)(2,1)} %add_blocks.7.refs_0_), channel_id=1, source_target_pairs={{0,2},{2,4},{4,6},{6,0},{1,3},{3,5},{5,7},{7,1},{8,10},{10,12},{12... | collective-permute-start | bytes 638984 | tf_op jit(solution)/shard_map/ppermute | solution.py:1057
  (57 other events, 500.6 us)
Sparse Core Ops, SparseCore 0:
  10.3 35.7 all-gather.7
  47.8 13.2 all-gather.9
  62.7 14.6 all-gather.11
  78.9 15.1 all-gather.13
  253.6 69.0 reduce-scatter.4
  326.0 99.4 reduce-scatter.6

commit v3 on v2

--- a/solution.py
+++ b/solution.py
@@ -112,8 +112,10 @@
         here = lane == HD + 4 * where[0] + i
         for r, v in enumerate((q_gain, k_gain)):
             small = small + jnp.where(here & (row == r), v[0:1, i : i + 1].astype(F32), 0.0)
+    lanes = lax.broadcasted_iota(jnp.int32, (EXPERTS, 128), 1)
+    rows = lax.broadcasted_iota(jnp.int32, (EXPERTS, 128), 0)
+    small = small + dot_tn(router[...], jnp.where(lanes == rows, 1.0, 0.0).astype(BF))
     out[:, 1536:1664] = small.astype(BF)
-    out[:, 1536:1568] = router[...]
 
 
 def pack(where, *arrays):
@@ -136,14 +138,34 @@
 def stack_pairs(blocks, *others):
     rows, width = blocks[0].shape
 
-    def kernel(a, b, c, d, low, high):
-        low[0], low[1] = a[...], b[...]
-        high[0], high[1] = c[...], d[...]
-
-    return pl.pallas_call(
-        past(kernel, 4, len(others)),
-        in_specs=[pl.BlockSpec(memory_space=pltpu.VMEM)] * 4 + [HBM] * len(others),
+    def kernel(*refs):
+        low, high, held, load_sem, send_sem = refs[4 + len(others) :]
+        loads = [
+            pltpu.make_async_copy(refs[i], held.at[i], load_sem.at[i]) for i in range(4)
+        ]
+        sends = [
+            pltpu.make_async_copy(held.at[2 * i : 2 * i + 2], out, send_sem.at[i])
+            for i, out in enumerate((low, high))
+        ]
+        for load in loads:
+            load.start()
+        for i in range(2):
+            loads[2 * i].wait()
+            loads[2 * i + 1].wait()
+            sends[i].start()
+        for send in sends:
+            send.wait()
+
+    return pl.pallas_call(
+        kernel,
+        in_specs=[HBM] * (4 + len(others)),
+        out_specs=[HBM] * 2,
         out_shape=[jax.ShapeDtypeStruct((2, rows, width), BF)] * 2,
+        scratch_shapes=[
+            pltpu.VMEM((4, rows, width), BF),
+            pltpu.SemaphoreType.DMA((4,)),
+            pltpu.SemaphoreType.DMA((2,)),
+        ],
         compiler_params=pltpu.CompilerParams(vmem_limit_bytes=VMEM),
         cost_estimate=cost(10**6, 10**6),
         name="stack_pairs",
@@ -152,22 +174,42 @@
 
 def add_blocks(arrays, handed=(), *others):
     blocks, n, k = arrays[0].shape[0], len(arrays), len(handed)
+    shape = arrays[0].shape[1:]
 
     def kernel(*refs):
-        for i, out in enumerate(refs[n + k + len(others) :][:blocks]):
-            total = refs[0][i].astype(F32)
-            for ref in refs[1:n]:
-                total = total + ref[i].astype(F32)
-            out[...] = total.astype(BF)
-
-    vmem = pl.BlockSpec(memory_space=pltpu.VMEM)
+        outs = refs[n + k + len(others) :][:blocks]
+        held, total, load_sem, send_sem = refs[-4:]
+        load = lambda i, j: pltpu.make_async_copy(
+            refs[j].at[i], held.at[i * n + j], load_sem.at[i * n + j]
+        )
+        send = lambda i: pltpu.make_async_copy(total.at[i], outs[i], send_sem.at[i])
+        for i in range(blocks):
+            for j in range(n):
+                load(i, j).start()
+        for i in range(blocks):
+            for j in range(n):
+                load(i, j).wait()
+            summed = held[i * n].astype(F32)
+            for j in range(1, n):
+                summed = summed + held[i * n + j].astype(F32)
+            total[i] = summed.astype(BF)
+            send(i).start()
+        for i in range(blocks):
+            send(i).wait()
+
     out = pl.pallas_call(
         kernel,
-        in_specs=[vmem] * n + [HBM] * (k + len(others)),
-        out_specs=[vmem] * blocks + [HBM] * k,
-        out_shape=[jax.ShapeDtypeStruct(arrays[0].shape[1:], BF)] * blocks
+        in_specs=[HBM] * (n + k + len(others)),
+        out_specs=[HBM] * (blocks + k),
+        out_shape=[jax.ShapeDtypeStruct(shape, BF)] * blocks
         + [jax.ShapeDtypeStruct(v.shape, v.dtype) for v in handed],
         input_output_aliases={n + i: blocks + i for i in range(k)},
+        scratch_shapes=[
+            pltpu.VMEM((n * blocks, *shape), BF),
+            pltpu.VMEM((blocks, *shape), BF),
+            pltpu.SemaphoreType.DMA((n * blocks,)),
+            pltpu.SemaphoreType.DMA((blocks,)),
+        ],
         compiler_params=pltpu.CompilerParams(vmem_limit_bytes=VMEM),
         cost_estimate=cost(10**9, 10**7),
         name="add_blocks",
@@ -1107,7 +1149,7 @@
     near = near.reshape(8)
 
     shard = pack(
-        as_row(f), w_query, w_key, w_value, w_out, router, attention_gain[None, :],
+        as_row(f), w_query, w_key, w_value, w_out, router.T, attention_gain[None, :],
         feedforward_gain[None, :], query_gain[None, :], key_gain[None, :],
     )
     shards = jnp.stack(gather_row(shard))
@@ -1188,16 +1230,17 @@
     (grads_w,) = add_blocks(grads_w, (), *sent[1:])
     grads_w = [v[None] for v in scatter_parts(grads_w, along(0))]
     ((grads_w,),) = add_blocks(grads_w, (), *gin[1:])
+    summed_w = grads_w
+    block_output = both((hidden1 + mixed.astype(F32)).astype(BF), summed_w)
     g_query, g_key, g_value, g_out, sums = settle(
         *scatter_parts([grads_w] * 4, shift), w_query, w_key, w_value, attention_gain[None, :],
         grad_tokens,
     )
     sums = sums + swap_cores(sums)
 
-    block_half = (hidden1 + mixed.astype(F32)).astype(BF)
     grads_e = grads_e.astype(F32)
     return (
-        both(block_half, sums),
+        block_output,
         grad_tokens,
         sums[:, 35],
         g_query,

time: 445 us -> 442 us (level); the launches traced: 450 us -> 435 us
  starting transfers between devices: 98.7 us -> 77.2 us
  waiting for transfers between devices: 125 us -> 135 us
    ppermute x36, waiting for transfers between devices: 91.4 us -> 104 us  [ring(): return lax.ppermute(value, ('fsdp', 'tensor'), ring_pairs(stage, step))]
    ppermute x6, starting transfers between devices: 18.2 us -> 8.48 us  [shift(): lax.ppermute(value, 'context', [(i, (i + step) % 4) for i in range(4)])]
    ppermute x36, starting transfers between devices: 56.5 us -> 50 us  [ring(): return lax.ppermute(value, ('fsdp', 'tensor'), ring_pairs(stage, step))]
    ppermute x6, starting transfers between devices: 23.7 us -> 18.4 us  [swap_cores(): return lax.ppermute(value, 'tensor', [(0, 1), (1, 0)])]
    unnamed x72 -> x67, local copies, waits for them, and re-layouts: 9.77 us -> 7.85 us
  transfers between devices with their start and end apart: 54 -> 54, of which waited for: 20 -> 21; matrix products, arithmetic and copies ran while one was open for 4% -> 4% of each run, Pallas kernels for 39% -> 40%
where the time goes in v3:
time: 442 us; the launch traced here: 435 us
  Pallas kernels  183 us (41%)
  waiting for transfers between devices  135 us (31%)
  starting transfers between devices  77.2 us (17%)
  local copies, waits for them, and re-layouts  18.3 us (4%)
  between operations  15.1 us (3%)
  other arithmetic  5.79 us (1%)
    ppermute x36, waiting for transfers between devices, ring(): return lax.ppermute(value, ('fsdp', 'tensor'), ring_pairs(stage, step))  104 us
    pallas_call x4, Pallas kernels, expert_chunk(): pl.pallas_call(expert_kernel, grid_spec=pltpu.PrefetchScalarGridSpec(num_...  60 us
    ppermute x36, starting transfers between devices, ring(): return lax.ppermute(value, ('fsdp', 'tensor'), ring_pairs(stage, step))  50 us
    pallas_call x1, Pallas kernels, attend_back(): pl.pallas_call(attend_back_kernel, grid=(2, 2), in_specs=[queries, querie...  23 us
    pallas_call x1, Pallas kernels, expert_weights(): pl.pallas_call(expert_weight_kernel, grid_spec=pltpu.PrefetchScalarGridSp...  18.5 us
    ppermute x6, starting transfers between devices, swap_cores(): return lax.ppermute(value, 'tensor', [(0, 1), (1, 0)])  18.4 us
    ppermute x6, waiting for transfers between devices, shift(): lax.ppermute(value, 'context', [(i, (i + step) % 4) for i in range(4)])  16.2 us
    pallas_call x1, Pallas kernels, project(): pl.pallas_call(past(project_kernel, 16, len(others)), grid_spec=pltpu.Pre...  13.8 us
  transfers between devices with their start and end apart: 54, of which 21 were waited for; matrix products, arithmetic and copies ran while one was open for 4% of the time, Pallas kernels for 40%

profile of v3, /device:TPU:1, one launch (start us, length us, event | category | flops | bytes accessed | tf_op | source)
XLA Modules:
  0.0 435.4 jit_solution(61359665047740887)
XLA Ops:
  12.6 4.4 %collective-permute-start.2 = (bf16[64,1664]{1,0:T(8,128)(2,1)}, bf16[64,1664]{1,0:T(8,128)(2,1)S(1)}, u32[]{:S(2)}, u32[]{:S(2)}) collective-permute-start(bf16[64,1664]{1,0:T(8,128)(2,1)} %pack.1), channel_id=1, source_target_pairs={{0,64},{1,17},{8,72},{9,25},{16,80},{17,1},{24,88},{25,9},{32,96},... | collective-permute-start | bytes 638984 | tf_op jit(solution)/shard_map/ppermute | solution.py:1095
  31.0 6.4 %collective-permute-done.5.refs_13_.refs_5_ = bf16[4,64,1664]{2,1,0:T(8,128)(2,1)S(1)} collective-permute-done((bf16[4,64,1664]{2,1,0:T(8,128)(2,1)S(1)}, bf16[4,64,1664]{2,1,0:T(8,128)(2,1)S(1)}, u32[]{:S(2)}, u32[]{:S(2)}) %collective-permute-start.5) | collective-permute-done | bytes 852000 | tf_op jit(solution)/shard_map/ppermute | solution.py:1095
  37.4 9.1 %collective-permute-done.4.refs_12_.refs_4_ = bf16[4,64,1664]{2,1,0:T(8,128)(2,1)S(1)} collective-permute-done((bf16[4,64,1664]{2,1,0:T(8,128)(2,1)S(1)}, bf16[4,64,1664]{2,1,0:T(8,128)(2,1)S(1)}, u32[]{:S(2)}, u32[]{:S(2)}) %collective-permute-start.4) | collective-permute-done | bytes 852000 | tf_op jit(solution)/shard_map/ppermute | solution.py:1095
  53.6 13.8 %project.1 = (bf16[1024,1664]{1,0:T(8,128)(2,1)}, f32[128,1024]{1,0:T(8,128)}, f32[8,128]{1,0:T(8,128)}, f32[1024,128]{1,0:T(8,128)}, f32[1024,128]{1,0:T(8,128)...) custom-call(s32[16]{0:T(128)} %select_n.145.refs_0_, ...), custom_call_target="tpu_custom_call" | custom-call | flops 10000000000 | bytes 20000000 | tf_op jit(solution)/shard_map/project/pallas_call | solution.py:294
  76.5 10.3 %attend.1 = (bf16[2,256,512]{2,1,0:T(8,128)(2,1)}, f32[256,1024]{1,0:T(8,128)}, f32[256,1024]{1,0:T(8,128)}) custom-call(bf16[2,256,512]{2,1,0:T(8,128)(2,1)} %get-tuple-element.105.refs_0_.q, bf16[2,1024,256]{2,1,0:T(8,128)(2,1)} %get-tuple-element.106.refs_1_.k, bf16[2,1024,256]{2,1,0:T(8,128)(2,1)} %get-tuple-element.107.refs_2_.v, ...), custom_call_target="tpu_custom_call" | custom-call | flops 10000000000 | bytes 8000000 | tf_op jit(solution)/shard_map/attend/pallas_call | solution.py:366
  86.9 4.4 %collective-permute-start.9 = (f32[256,1024]{1,0:T(8,128)}, f32[256,1024]{1,0:T(8,128)}, u32[]{:S(2)}, u32[]{:S(2)}) collective-permute-start(f32[256,1024]{1,0:T(8,128)} %get-tuple-element.112), channel_id=1, source_target_pairs={{0,1},{1,0},{2,3},{3,2},{4,5},{5,4},{6,7},{7,6},{8,9},{9,8},{10,11... | collective-permute-start | bytes 3145736 | tf_op jit(solution)/shard_map/ppermute | solution.py:1103
  91.7 7.6 %collective-permute-done.12.refs_8_.c_low = bf16[2,272,1024]{2,1,0:T(8,128)(2,1)} collective-permute-done((bf16[2,272,1024]{2,1,0:T(8,128)(2,1)}, bf16[2,272,1024]{2,1,0:T(8,128)(2,1)}, u32[]{:S(2)}, u32[]{:S(2)}) %collective-permute-start.12) | collective-permute-done | bytes 1114144 | tf_op jit(solution)/shard_map/ppermute | solution.py:1095
  108.7 11.6 %collective-permute-done.16.refs_3_ = bf16[272,1024]{1,0:T(8,128)(2,1)S(1)} collective-permute-done((bf16[272,1024]{1,0:T(8,128)(2,1)}, bf16[272,1024]{1,0:T(8,128)(2,1)S(1)}, u32[]{:S(2)}, u32[]{:S(2)}) %collective-permute-start.16) | collective-permute-done | bytes 557088 | tf_op jit(solution)/shard_map/ppermute | solution.py:1095
  120.3 8.5 %collective-permute-done.15.refs_2_ = bf16[272,1024]{1,0:T(8,128)(2,1)S(1)} collective-permute-done((bf16[272,1024]{1,0:T(8,128)(2,1)}, bf16[272,1024]{1,0:T(8,128)(2,1)S(1)}, u32[]{:S(2)}, u32[]{:S(2)}) %collective-permute-start.15) | collective-permute-done | bytes 557088 | tf_op jit(solution)/shard_map/ppermute | solution.py:1095
  135.5 14.9 %experts.4 = (bf16[16,256,1024]{2,1,0:T(8,128)(2,1)}, bf16[4,272,1024]{2,1,0:T(8,128)(2,1)}, bf16[2,1536,1024]{2,1,0:T(8,128)(2,1)}, bf16[2,1536,1024]{2,1,0:T(8...) custom-call(s32[4]{0:T(128)} %get-tuple-element.265.order, ...), custom_call_target="tpu_custom_call" | custom-call | flops 14000000000 | bytes 30000000 | tf_op jit(solution)/shard_map/experts/pallas_call | solution.py:636
  150.5 8.7 %collective-permute-done.22.x_high = bf16[2,272,1024]{2,1,0:T(8,128)(2,1)} collective-permute-done((bf16[2,272,1024]{2,1,0:T(8,128)(2,1)}, bf16[2,272,1024]{2,1,0:T(8,128)(2,1)}, u32[]{:S(2)}, u32[]{:S(2)}) %collective-permute-start.22) | collective-permute-done | bytes 1114144 | tf_op jit(solution)/shard_map/ppermute | solution.py:1095
  160.9 15.3 %experts.5 = (bf16[16,256,1024]{2,1,0:T(8,128)(2,1)}, bf16[4,272,1024]{2,1,0:T(8,128)(2,1)}, bf16[2,1536,1024]{2,1,0:T(8,128)(2,1)}, bf16[2,1536,1024]{2,1,0:T(8...) custom-call(s32[4]{0:T(128)} %get-tuple-element.266.order, ...), custom_call_target="tpu_custom_call", output_to_operand_aliasing={{0}: (9, {}), {2}: (10, {}), {3}: (11, {}), {4}: (12, {})} | custom-call | flops 14000000000 | bytes 30000000 | tf_op jit(solution)/shard_map/experts/pallas_call | solution.py:636
  176.3 14.9 %experts.6 = (bf16[16,256,1024]{2,1,0:T(8,128)(2,1)}, bf16[4,272,1024]{2,1,0:T(8,128)(2,1)}, bf16[2,1536,1024]{2,1,0:T(8,128)(2,1)}, bf16[2,1536,1024]{2,1,0:T(8...) custom-call(s32[4]{0:T(128)} %get-tuple-element.267.order, ...), custom_call_target="tpu_custom_call", output_to_operand_aliasing={{0}: (9, {}), {2}: (10, {}), {3}: (11, {}), {4}: (12, {})} | custom-call | flops 14000000000 | bytes 30000000 | tf_op jit(solution)/shard_map/experts/pallas_call | solution.py:636
  192.5 14.9 %experts.7 = (bf16[16,256,1024]{2,1,0:T(8,128)(2,1)}, bf16[4,272,1024]{2,1,0:T(8,128)(2,1)}, bf16[2,1536,1024]{2,1,0:T(8,128)(2,1)}, bf16[2,1536,1024]{2,1,0:T(8...) custom-call(s32[4]{0:T(128)} %get-tuple-element.268.order, ...), custom_call_target="tpu_custom_call", output_to_operand_aliasing={{0}: (9, {}), {2}: (10, {}), {3}: (11, {}), {4}: (12, {})} | custom-call | flops 14000000000 | bytes 30000000 | tf_op jit(solution)/shard_map/experts/pallas_call | solution.py:636
  209.1 19.1 %collective-permute-done.25.refs_16_.refs_1_ = bf16[4,272,1024]{2,1,0:T(8,128)(2,1)} collective-permute-done((bf16[4,272,1024]{2,1,0:T(8,128)(2,1)}, bf16[4,272,1024]{2,1,0:T(8,128)(2,1)}, u32[]{:S(2)}, u32[]{:S(2)}) %collective-permute-start.25) | collective-permute-done | bytes 2228256 | tf_op jit(solution)/shard_map/ppermute | solution.py:1095
  228.3 18.5 %expert_weights.1.refs_4_ = bf16[4,2,2,256,768]{4,3,2,1,0:T(8,128)(2,1)} custom-call(s32[1]{0:T(128)} %bitcast.refs_0_.place, bf16[2,1536,1024]{2,1,0:T(8,128)(2,1)} %get-tuple-element.135.x, bf16[2,1536,1024]{2,1,0:T(8,128)(2,1)} %get-tuple-element.136.g, bf16[2,1536,1536]{2,1,0:T(8,128)(2,1)} %get-tuple-element.137.act.grad, ...), custom_call_target="tpu_custom_call" | custom-call | flops 20000000000 | bytes 30000000 | tf_op jit(solution)/shard_map/expert_weights/pallas_call | solution.py:710
  246.8 5.2 %add_blocks.4 = (bf16[272,1024]{1,0:T(8,128)(2,1)}, bf16[272,1024]{1,0:T(8,128)(2,1)}, bf16[272,1024]{1,0:T(8,128)(2,1)}, bf16[272,1024]{1,0:T(8,128)(2,1)}, bf16[4,2,2,256,768]{4,3,2,1,0:T(8,128)(2,1)}) custom-call(bf16[4,272,1024]{2,1,0:T(8,128)(2,1)} %get-tuple-element.131.refs_0_, ...), custom_call_target="tpu_custom_call", output_to_operand_aliasing={{4}: (4, {})} | custom-call | flops 1000000000 | bytes 10000000 | tf_op jit(solution)/shard_map/add_blocks/pallas_call | solution.py:200
  256.3 6.0 %collective-permute-done.28.refs_2_ = bf16[272,1024]{1,0:T(8,128)(2,1)S(1)} collective-permute-done((bf16[272,1024]{1,0:T(8,128)(2,1)}, bf16[272,1024]{1,0:T(8,128)(2,1)S(1)}, u32[]{:S(2)}, u32[]{:S(2)}) %collective-permute-start.28) | collective-permute-done | bytes 557088 | tf_op jit(solution)/shard_map/ppermute | solution.py:1095
  262.3 5.9 %collective-permute-done.29.refs_3_ = bf16[272,1024]{1,0:T(8,128)(2,1)S(1)} collective-permute-done((bf16[272,1024]{1,0:T(8,128)(2,1)S(1)}, bf16[272,1024]{1,0:T(8,128)(2,1)S(1)}, u32[]{:S(2)}, u32[]{:S(2)}) %collective-permute-start.29) | collective-permute-done | bytes 557088 | tf_op jit(solution)/shard_map/ppermute | solution.py:1095
  270.1 4.7 %route_back.1 = (bf16[16,256,1024]{2,1,0:T(8,128)(2,1)}, f32[256,1024]{1,0:T(8,128)}, bf16[256,1024]{1,0:T(8,128)(2,1)}, f32[32,1024]{1,0:T(8,128)}, f32[1,1024]{1,0:T(1,128)}) custom-call(bf16[16,256,1024]{2,1,0:T(8,128)(2,1)} %get-tuple-element.130.refs_0_, bf16[272,1024]{1,0:T(8,128)(2,1)} %get-tuple-element.154.refs_1_, ...), custom_call_target="tpu_custom_call", output_to_operand_aliasing={{0}: (0, {})} | custom-call | flops 4000000000 | bytes 6000000 | tf_op jit(solution)/shard_map/route_back/pallas_call | solution.py:774
  275.8 4.6 %collective-permute-start.32 = (bf16[256,1024]{1,0:T(8,128)(2,1)S(1)}, bf16[256,1024]{1,0:T(8,128)(2,1)S(1)}, u32[]{:S(2)}, u32[]{:S(2)}) collective-permute-start(bf16[256,1024]{1,0:T(8,128)(2,1)S(1)} %copy-done.28), channel_id=1, source_target_pairs={{0,1},{1,0},{2,3},{3,2},{4,5},{5,4},{6,7},{7,6},{8,9},{9,8},{10,11... | collective-permute-start | bytes 1572872 | tf_op jit(solution)/shard_map/ppermute | solution.py:1103
  282.7 23.0 %attend_back.1 = (bf16[2,256,512]{2,1,0:T(8,128)(2,1)}, bf16[2,1024,256]{2,1,0:T(8,128)(2,1)}, bf16[2,1024,256]{2,1,0:T(8,128)(2,1)}, f32[8,256]{1,0:T(8,128)}) custom-call(bf16[2,256,512]{2,1,0:T(8,128)(2,1)} %get-tuple-element.105.refs_0_.q, f32[2,256,512]{2,1,0:T(8,128)} %get-tuple-element.162.q_proj, bf16[2,1024,256]{2,1,0:T(8,128)(2,1)} %get-tuple-element.106.refs_1_.k, ...), custom_call_target="tpu_custom_call" | custom-call | flops 17999998976 | bytes 16000000 | tf_op jit(solution)/shard_map/attend_back/pallas_call | solution.py:860
  305.7 9.6 %weight_grads.1 = (bf16[4,64,1664]{2,1,0:T(8,128)(2,1)}, bf16[4,64,1664]{2,1,0:T(8,128)(2,1)}, bf16[4,64,1664]{2,1,0:T(8,128)(2,1)}, bf16[4,64,1664]{2,1,0:T(8,128)(2,1)}) custom-call(s32[16]{0:T(128)} %select_n.156.refs_0_, bf16[2,1024,1024]{2,1,0:T(8,128)(2,1)} %get-tuple-element.161.refs_1_, bf16[2,256,512]{2,1,0:T(8,128)(2,1)} %get-tuple-element.169.refs_2_.refs_0_, ...), custom_call_target="tpu_custom_call" | custom-call | flops 8999999488 | bytes 16000000 | tf_op jit(solution)/shard_map/weight_grads/pallas_call | solution.py:941
  315.3 6.7 %input_grads.1 = (bf16[4,256,1024]{2,1,0:T(8,128)(2,1)}, bf16[4,256,1024]{2,1,0:T(8,128)(2,1)}) custom-call(bf16[2,256,512]{2,1,0:T(8,128)(2,1)} %get-tuple-element.169.refs_2_.refs_0_, bf16[2,1024,256]{2,1,0:T(8,128)(2,1)} %get-tuple-element.170.refs_3_.refs_1_, bf16[2,1024,256]{2,1,0:T(8,128)(2,1)} %get-tuple-element.171.refs_4_.refs_2_, ...), custom_call_target="tpu_custom_call" | custom-call | flops 6000000000 | bytes 12000000 | tf_op jit(solution)/shard_map/input_grads/pallas_call | solution.py:982
  322.3 4.2 collective-permute-done.36.refs_1_
  336.8 7.8 %collective-permute-done.40.refs_4_.refs_1_ = bf16[256,1024]{1,0:T(8,128)(2,1)} collective-permute-done((bf16[256,1024]{1,0:T(8,128)(2,1)}, bf16[256,1024]{1,0:T(8,128)(2,1)}, u32[]{:S(2)}, u32[]{:S(2)}) %collective-permute-start.40) | collective-permute-done | bytes 524320 | tf_op jit(solution)/shard_map/ppermute | solution.py:1099
  346.3 8.3 %collective-permute-done.42.refs_6_.refs_3_ = bf16[256,1024]{1,0:T(8,128)(2,1)} collective-permute-done((bf16[256,1024]{1,0:T(8,128)(2,1)}, bf16[256,1024]{1,0:T(8,128)(2,1)}, u32[]{:S(2)}, u32[]{:S(2)}) %collective-permute-start.42) | collective-permute-done | bytes 524320 | tf_op jit(solution)/shard_map/ppermute | solution.py:1099
  354.7 3.8 finish.1.refs_1_
  358.5 7.4 %collective-permute-start.43 = (f32[256,1024]{1,0:T(8,128)}, f32[256,1024]{1,0:T(8,128)}, u32[]{:S(2)}, u32[]{:S(2)}) collective-permute-start(f32[256,1024]{1,0:T(8,128)} %finish.1.refs_1_), channel_id=1, source_target_pairs={{0,1},{1,0},{2,3},{3,2},{4,5},{5,4},{6,7},{7,6},{8,9},{9,8},{10,11... | collective-permute-start | bytes 3145736 | tf_op jit(solution)/shard_map/ppermute | solution.py:1103
  365.9 14.3 %collective-permute-done.35.refs_3_ = bf16[4,64,1664]{2,1,0:T(8,128)(2,1)} collective-permute-done((bf16[4,64,1664]{2,1,0:T(8,128)(2,1)}, bf16[4,64,1664]{2,1,0:T(8,128)(2,1)}, u32[]{:S(2)}, u32[]{:S(2)}) %collective-permute-start.35) | collective-permute-done | bytes 852000 | tf_op jit(solution)/shard_map/ppermute | solution.py:1095
  386.0 5.2 %collective-permute-start.39 = (bf16[64,1664]{1,0:T(8,128)(2,1)}, bf16[64,1664]{1,0:T(8,128)(2,1)S(1)}, u32[]{:S(2)}, u32[]{:S(2)}) collective-permute-start(bf16[64,1664]{1,0:T(8,128)(2,1)} %get-tuple-element.187), channel_id=1, source_target_pairs={{0,64},{1,17},{8,72},{9,25},{16,80},{17,1},{24,88},{25,9},{32,96},... | collective-permute-start | bytes 638984 | tf_op jit(solution)/shard_map/ppermute | solution.py:1095
  402.2 8.8 %reduce-scatter.7.cloned.1.call-done = bf16[1,256,1024]{2,1,0:T(8,128)(2,1)} async-done(((bf16[16,256,1024]{2,1,0:T(8,128)(2,1)}), bf16[1,256,1024]{2,1,0:T(8,128)(2,1)}) %reduce-scatter.7.cloned.1.call-update) | async-done | bytes 524304
  (223 shorter events, 112.3 us)
Async XLA Ops:
  7.2 46.4 %all-gather.8.cloned.1.call-start = ((), (), s32[]{:S(2)}) async-start(), calls=%async_computation.2 | async-start | bytes 4718592 | tf_op jit(solution)/shard_map/all_gather | solution.py:1162
  9.3 126.2 %all-gather.10.cloned.1.call-start = ((), (), s32[]{:S(2)}) async-start(), calls=%async_computation.4 | async-start | bytes 3145728 | tf_op jit(solution)/shard_map/all_gather | solution.py:1177
  10.0 125.4 %all-gather.12.cloned.1.call-start = ((), (), s32[]{:S(2)}) async-start(), calls=%async_computation.5 | async-start | bytes 3145728 | tf_op jit(solution)/shard_map/all_gather | solution.py:1177
  10.8 124.7 %all-gather.14.cloned.1.call-start = ((), (), s32[]{:S(2)}) async-start(), calls=%async_computation.6 | async-start | bytes 3145728 | tf_op jit(solution)/shard_map/all_gather | solution.py:1177
  19.7 335.0 %reduce-scatter.5.cloned.1.call-start = ((), (), s32[]{:S(2)}) async-start(), calls=%async_computation.3 | async-start | bytes 7077888 | tf_op jit(solution)/shard_map/reduce_scatter | solution.py:1208
  26.5 20.0 %collective-permute-start.4 = (bf16[4,64,1664]{2,1,0:T(8,128)(2,1)S(1)}, bf16[4,64,1664]{2,1,0:T(8,128)(2,1)S(1)}, u32[]{:S(2)}, u32[]{:S(2)}) collective-permute-start(bf16[4,64,1664]{2,1,0:T(8,128)(2,1)S(1)} %pad_maximum_fusion.refs_10_), channel_id=1, source_target_pairs={{0,8},{1,33},{8,16},{9,41},{16,24},{17,49},{24,0},{25,57},{32,40},... | collective-permute-start | bytes 2555912 | tf_op jit(solution)/shard_map/ppermute | solution.py:1095
  27.1 19.6 %collective-permute-start.3 = (bf16[4,64,1664]{2,1,0:T(8,128)(2,1)S(1)}, bf16[4,64,1664]{2,1,0:T(8,128)(2,1)}, u32[]{:S(2)}, u32[]{:S(2)}) collective-permute-start(bf16[4,64,1664]{2,1,0:T(8,128)(2,1)S(1)} %pad_maximum_fusion.refs_10_), channel_id=1, source_target_pairs={{0,24},{1,97},{8,0},{9,105},{16,8},{17,113},{24,16},{25,121},{32,5... | collective-permute-start | bytes 2555912 | tf_op jit(solution)/shard_map/ppermute | solution.py:1095
  49.3 18.1 %collective-permute-start.8 = (bf16[272,1024]{1,0:T(8,128)(2,1)}, bf16[272,1024]{1,0:T(8,128)(2,1)S(1)}, u32[]{:S(2)}, u32[]{:S(2)}) collective-permute-start(bf16[272,1024]{1,0:T(8,128)(2,1)} %pack_cotangent.1.refs_0_.refs_5_), channel_id=1, source_target_pairs={{0,64},{1,17},{8,72},{9,25},{16,80},{17,1},{24,88},{25,9},{32,96},... | collective-permute-start | bytes 1671176 | tf_op jit(solution)/shard_map/ppermute | solution.py:1095
  71.1 29.9 %collective-permute-start.13 = (bf16[2,272,1024]{2,1,0:T(8,128)(2,1)}, bf16[2,272,1024]{2,1,0:T(8,128)(2,1)}, u32[]{:S(2)}, u32[]{:S(2)}) collective-permute-start(bf16[2,272,1024]{2,1,0:T(8,128)(2,1)} %get-tuple-element.113.c_high), channel_id=1, source_target_pairs={{0,8},{1,33},{8,16},{9,41},{16,24},{17,49},{24,0},{25,57},{32,40},... | collective-permute-start | bytes 3342344 | tf_op jit(solution)/shard_map/ppermute | solution.py:1095
  73.0 18.3 %collective-permute-start.11 = (bf16[2,272,1024]{2,1,0:T(8,128)(2,1)}, bf16[2,272,1024]{2,1,0:T(8,128)(2,1)}, u32[]{:S(2)}, u32[]{:S(2)}) collective-permute-start(bf16[2,272,1024]{2,1,0:T(8,128)(2,1)} %get-tuple-element.113.c_high), channel_id=1, source_target_pairs={{0,24},{1,97},{8,0},{9,105},{16,8},{17,113},{24,16},{25,121},{32,5... | collective-permute-start | bytes 3342344 | tf_op jit(solution)/shard_map/ppermute | solution.py:1095
  73.9 25.4 %collective-permute-start.12 = (bf16[2,272,1024]{2,1,0:T(8,128)(2,1)}, bf16[2,272,1024]{2,1,0:T(8,128)(2,1)}, u32[]{:S(2)}, u32[]{:S(2)}) collective-permute-start(bf16[2,272,1024]{2,1,0:T(8,128)(2,1)} %get-tuple-element.110.refs_5_.c_low), channel_id=1, source_target_pairs={{0,8},{1,33},{8,16},{9,41},{16,24},{17,49},{24,0},{25,57},{32,40},... | collective-permute-start | bytes 3342344 | tf_op jit(solution)/shard_map/ppermute | solution.py:1095
  74.4 26.6 %collective-permute-start.10 = (bf16[2,272,1024]{2,1,0:T(8,128)(2,1)}, bf16[2,272,1024]{2,1,0:T(8,128)(2,1)}, u32[]{:S(2)}, u32[]{:S(2)}) collective-permute-start(bf16[2,272,1024]{2,1,0:T(8,128)(2,1)} %get-tuple-element.110.refs_5_.c_low), channel_id=1, source_target_pairs={{0,24},{1,97},{8,0},{9,105},{16,8},{17,113},{24,16},{25,121},{32,5... | collective-permute-start | bytes 3342344 | tf_op jit(solution)/shard_map/ppermute | solution.py:1095
  91.3 37.5 %collective-permute-start.18 = (bf16[2,272,1024]{2,1,0:T(8,128)(2,1)}, bf16[2,272,1024]{2,1,0:T(8,128)(2,1)}, u32[]{:S(2)}, u32[]{:S(2)}) collective-permute-start(bf16[2,272,1024]{2,1,0:T(8,128)(2,1)} %collective-permute-done.11.refs_7_.c_high), channel_id=1, source_target_pairs={{0,24},{1,97},{8,0},{9,105},{16,8},{17,113},{24,16},{25,121},{32,5... | collective-permute-start | bytes 3342344 | tf_op jit(solution)/shard_map/ppermute | solution.py:1095
  99.3 29.5 %collective-permute-start.17 = (bf16[2,272,1024]{2,1,0:T(8,128)(2,1)}, bf16[2,272,1024]{2,1,0:T(8,128)(2,1)}, u32[]{:S(2)}, u32[]{:S(2)}) collective-permute-start(bf16[2,272,1024]{2,1,0:T(8,128)(2,1)} %collective-permute-done.12.refs_8_.c_low), channel_id=1, source_target_pairs={{0,8},{1,33},{8,16},{9,41},{16,24},{17,49},{24,0},{25,57},{32,40},... | collective-permute-start | bytes 3342344 | tf_op jit(solution)/shard_map/ppermute | solution.py:1095
  104.2 24.5 %collective-permute-start.15 = (bf16[272,1024]{1,0:T(8,128)(2,1)}, bf16[272,1024]{1,0:T(8,128)(2,1)S(1)}, u32[]{:S(2)}, u32[]{:S(2)}) collective-permute-start(bf16[272,1024]{1,0:T(8,128)(2,1)} %get-tuple-element.115.refs_0_.refs_8_), channel_id=1, source_target_pairs={{0,32},{1,9},{8,40},{9,17},{16,48},{17,25},{24,56},{25,1},{32,64},... | collective-permute-start | bytes 1671176 | tf_op jit(solution)/shard_map/ppermute | solution.py:1095
  104.2 24.5 %collective-permute-start.14 = (bf16[272,1024]{1,0:T(8,128)(2,1)}, bf16[272,1024]{1,0:T(8,128)(2,1)}, u32[]{:S(2)}, u32[]{:S(2)}) collective-permute-start(bf16[272,1024]{1,0:T(8,128)(2,1)} %get-tuple-element.115.refs_0_.refs_8_), channel_id=1, source_target_pairs={{0,96},{1,25},{8,104},{9,1},{16,112},{17,9},{24,120},{25,17},{32,0... | collective-permute-start | bytes 1671176 | tf_op jit(solution)/shard_map/ppermute | solution.py:1095
  132.2 28.7 %collective-permute-start.24 = (bf16[2,272,1024]{2,1,0:T(8,128)(2,1)}, bf16[2,272,1024]{2,1,0:T(8,128)(2,1)}, u32[]{:S(2)}, u32[]{:S(2)}) collective-permute-start(bf16[2,272,1024]{2,1,0:T(8,128)(2,1)} %get-tuple-element.116.x_low), channel_id=1, source_target_pairs={{0,24},{1,97},{8,0},{9,105},{16,8},{17,113},{24,16},{25,121},{32,5... | collective-permute-start | bytes 3342344 | tf_op jit(solution)/shard_map/ppermute | solution.py:1095
  132.8 17.6 %collective-permute-start.19 = (bf16[2,272,1024]{2,1,0:T(8,128)(2,1)}, bf16[2,272,1024]{2,1,0:T(8,128)(2,1)}, u32[]{:S(2)}, u32[]{:S(2)}) collective-permute-start(bf16[2,272,1024]{2,1,0:T(8,128)(2,1)} %get-tuple-element.116.x_low), channel_id=1, source_target_pairs={{0,8},{1,33},{8,16},{9,41},{16,24},{17,49},{24,0},{25,57},{32,40},... | collective-permute-start | bytes 3342344 | tf_op jit(solution)/shard_map/ppermute | solution.py:1095
  133.8 25.4 %collective-permute-start.22 = (bf16[2,272,1024]{2,1,0:T(8,128)(2,1)}, bf16[2,272,1024]{2,1,0:T(8,128)(2,1)}, u32[]{:S(2)}, u32[]{:S(2)}) collective-permute-start(bf16[2,272,1024]{2,1,0:T(8,128)(2,1)} %get-tuple-element.117.x_high), channel_id=1, source_target_pairs={{0,24},{1,97},{8,0},{9,105},{16,8},{17,113},{24,16},{25,121},{32,5... | collective-permute-start | bytes 3342344 | tf_op jit(solution)/shard_map/ppermute | solution.py:1095
  135.5 57.0 %collective-permute-start.20 = (bf16[2,272,1024]{2,1,0:T(8,128)(2,1)}, bf16[2,272,1024]{2,1,0:T(8,128)(2,1)}, u32[]{:S(2)}, u32[]{:S(2)}) collective-permute-start(bf16[2,272,1024]{2,1,0:T(8,128)(2,1)} %get-tuple-element.117.x_high), channel_id=1, source_target_pairs={{0,8},{1,33},{8,16},{9,41},{16,24},{17,49},{24,0},{25,57},{32,40},... | collective-permute-start | bytes 3342344 | tf_op jit(solution)/shard_map/ppermute | solution.py:1095
  150.4 25.9 %collective-permute-start.21 = (bf16[2,272,1024]{2,1,0:T(8,128)(2,1)}, bf16[2,272,1024]{2,1,0:T(8,128)(2,1)}, u32[]{:S(2)}, u32[]{:S(2)}) collective-permute-start(bf16[2,272,1024]{2,1,0:T(8,128)(2,1)} %collective-permute-done.19.x_low), channel_id=1, source_target_pairs={{0,8},{1,33},{8,16},{9,41},{16,24},{17,49},{24,0},{25,57},{32,40},... | collective-permute-start | bytes 3342344 | tf_op jit(solution)/shard_map/ppermute | solution.py:1095
  159.2 17.1 %collective-permute-start.23 = (bf16[2,272,1024]{2,1,0:T(8,128)(2,1)}, bf16[2,272,1024]{2,1,0:T(8,128)(2,1)}, u32[]{:S(2)}, u32[]{:S(2)}) collective-permute-start(bf16[2,272,1024]{2,1,0:T(8,128)(2,1)} %collective-permute-done.22.x_high), channel_id=1, source_target_pairs={{0,24},{1,97},{8,0},{9,105},{16,8},{17,113},{24,16},{25,121},{32,5... | collective-permute-start | bytes 3342344 | tf_op jit(solution)/shard_map/ppermute | solution.py:1095
  176.2 52.1 %collective-permute-start.25 = (bf16[4,272,1024]{2,1,0:T(8,128)(2,1)}, bf16[4,272,1024]{2,1,0:T(8,128)(2,1)}, u32[]{:S(2)}, u32[]{:S(2)}) collective-permute-start(bf16[4,272,1024]{2,1,0:T(8,128)(2,1)} %get-tuple-element.132), channel_id=1, source_target_pairs={{0,8},{1,33},{8,16},{9,41},{16,24},{17,49},{24,0},{25,57},{32,40},... | collective-permute-start | bytes 6684680 | tf_op jit(solution)/shard_map/ppermute | solution.py:1095
  191.3 37.0 %collective-permute-start.27 = (bf16[4,272,1024]{2,1,0:T(8,128)(2,1)}, bf16[4,272,1024]{2,1,0:T(8,128)(2,1)}, u32[]{:S(2)}, u32[]{:S(2)}) collective-permute-start(bf16[4,272,1024]{2,1,0:T(8,128)(2,1)} %get-tuple-element.134), channel_id=1, source_target_pairs={{0,16},{1,65},{8,24},{9,73},{16,0},{17,81},{24,8},{25,89},{32,48},... | collective-permute-start | bytes 6684680 | tf_op jit(solution)/shard_map/ppermute | solution.py:1095
  207.4 39.4 %collective-permute-start.26 = (bf16[4,272,1024]{2,1,0:T(8,128)(2,1)}, bf16[4,272,1024]{2,1,0:T(8,128)(2,1)}, u32[]{:S(2)}, u32[]{:S(2)}) collective-permute-start(bf16[4,272,1024]{2,1,0:T(8,128)(2,1)} %get-tuple-element.133), channel_id=1, source_target_pairs={{0,24},{1,97},{8,0},{9,105},{16,8},{17,113},{24,16},{25,121},{32,5... | collective-permute-start | bytes 6684680 | tf_op jit(solution)/shard_map/ppermute | solution.py:1095
  252.1 158.9 %reduce-scatter.7.cloned.1.call-start = ((), (), s32[]{:S(2)}) async-start(), calls=%async_computation.7 | async-start | bytes 8912896
  331.0 34.9 %collective-permute-start.33 = (bf16[4,64,1664]{2,1,0:T(8,128)(2,1)}, bf16[4,64,1664]{2,1,0:T(8,128)(2,1)S(1)}, u32[]{:S(2)}, u32[]{:S(2)}) collective-permute-start(bf16[4,64,1664]{2,1,0:T(8,128)(2,1)} %get-tuple-element.176), channel_id=1, source_target_pairs={{0,8},{1,33},{8,16},{9,41},{16,24},{17,49},{24,0},{25,57},{32,40},... | collective-permute-start | bytes 2555912 | tf_op jit(solution)/shard_map/ppermute | solution.py:1095
  331.0 34.9 %collective-permute-start.34 = (bf16[4,64,1664]{2,1,0:T(8,128)(2,1)}, bf16[4,64,1664]{2,1,0:T(8,128)(2,1)S(1)}, u32[]{:S(2)}, u32[]{:S(2)}) collective-permute-start(bf16[4,64,1664]{2,1,0:T(8,128)(2,1)} %get-tuple-element.177), channel_id=1, source_target_pairs={{0,24},{1,97},{8,0},{9,105},{16,8},{17,113},{24,16},{25,121},{32,5... | collective-permute-start | bytes 2555912 | tf_op jit(solution)/shard_map/ppermute | solution.py:1095
  334.0 46.3 %collective-permute-start.35 = (bf16[4,64,1664]{2,1,0:T(8,128)(2,1)}, bf16[4,64,1664]{2,1,0:T(8,128)(2,1)}, u32[]{:S(2)}, u32[]{:S(2)}) collective-permute-start(bf16[4,64,1664]{2,1,0:T(8,128)(2,1)} %get-tuple-element.178), channel_id=1, source_target_pairs={{0,16},{1,65},{8,24},{9,73},{16,0},{17,81},{24,8},{25,89},{32,48},... | collective-permute-start | bytes 2555912 | tf_op jit(solution)/shard_map/ppermute | solution.py:1095
  358.5 56.8 %collective-permute-start.43 = (f32[256,1024]{1,0:T(8,128)}, f32[256,1024]{1,0:T(8,128)}, u32[]{:S(2)}, u32[]{:S(2)}) collective-permute-start(f32[256,1024]{1,0:T(8,128)} %finish.1.refs_1_), channel_id=1, source_target_pairs={{0,1},{1,0},{2,3},{3,2},{4,5},{5,4},{6,7},{7,6},{8,9},{9,8},{10,11... | collective-permute-start | bytes 3145736 | tf_op jit(solution)/shard_map/ppermute | solution.py:1103
  398.4 19.8 %collective-permute-start.46 = (bf16[64,1664]{1,0:T(8,128)(2,1)}, bf16[64,1664]{1,0:T(8,128)(2,1)S(1)}, u32[]{:S(2)}, u32[]{:S(2)}) collective-permute-start(bf16[64,1664]{1,0:T(8,128)(2,1)} %add_blocks.7.refs_3_.refs_0_), channel_id=1, source_target_pairs={{0,4},{2,6},{4,0},{6,2},{1,5},{3,7},{5,1},{7,3},{8,12},{10,14},{12... | collective-permute-start | bytes 638984 | tf_op jit(solution)/shard_map/ppermute | solution.py:1099
  398.5 19.7 %collective-permute-start.45 = (bf16[64,1664]{1,0:T(8,128)(2,1)}, bf16[64,1664]{1,0:T(8,128)(2,1)S(1)}, u32[]{:S(2)}, u32[]{:S(2)}) collective-permute-start(bf16[64,1664]{1,0:T(8,128)(2,1)} %add_blocks.7.refs_3_.refs_0_), channel_id=1, source_target_pairs={{0,6},{2,0},{4,2},{6,4},{1,7},{3,1},{5,3},{7,5},{8,14},{10,8},{12,... | collective-permute-start | bytes 638984 | tf_op jit(solution)/shard_map/ppermute | solution.py:1099
  (55 other events, 480.3 us)
Sparse Core Ops, SparseCore 0:
  10.3 35.7 all-gather.7
  47.8 13.2 all-gather.9
  62.7 14.6 all-gather.11
  78.9 16.0 all-gather.13
  252.2 58.3 reduce-scatter.4
  313.9 97.0 reduce-scatter.6
